TPU v7x, 32 devices: a whole 2x2x4 slice. The times are simulated.
32 devices in a mesh: rep: 2 (over y), seq: 4 (over z), wt: 4 (over x, core).
Axes of the slice: x: 2, y: 2, z: 4, core: 2. Of those that a mesh axis runs over, the one named last changes fastest.
Arguments:
- tokens: bfloat16 [8, 16, 3072], P(('rep', 'wt'), 'seq'), parts along dimension 0, may hold values from -6 to 6
- modulation: float32 [8, 3, 3072], P(('rep', 'wt')), parts along dimension 0, may hold values from -3 to 3
- qkv_weight: bfloat16 [3072, 3, 3072], P('wt', None, 'seq'), may hold values from -0.109375 to 0.109375
- qkv_bias: float32 [3, 3072], P(None, 'seq'), may hold values from -3 to 3
- norm_gains: float32 [2, 128], replicated, may hold values from 0.1 to 1.9
- up_weight: bfloat16 [3072, 12288], P('wt', 'seq'), may hold values from -0.109375 to 0.109375
- up_mask: int32 [48, 192], P('wt', 'seq'), may hold values from 0 to 1, as said below
- up_bias: float32 [12288], P('seq'), may hold values from -3 to 3
- proj_weight: bfloat16 [3072, 3072], P('seq', 'wt'), may hold values from -0.109375 to 0.109375
- down_weight: bfloat16 [12288, 3072], P('seq', 'wt'), may hold values from -0.0546875 to 0.0546875
- down_mask: int32 [192, 48], P('seq', 'wt'), may hold values from 0 to 1, as said below
- out_bias: float32 [3072], replicated, may hold values from -3 to 3
Outputs:
- mixed: bfloat16 [8, 16, 3072], P(('rep', 'wt'), 'seq'), parts along dimension 0
There are 2 independent parts, one for each index of `rep`. A program takes and returns all parts, laid end to end along the dimension named above; an argument that names none is the same for every part. Nothing has to cross between parts.
Inputs may be any that keep to these rules, and one draw needn't show every extreme that they name: `up_mask`: 1 keeps the 64 x 64 block of up_weight at that place, 0 drops it. `down_mask`: 1 keeps the 64 x 64 block of down_weight at that place, 0 drops it.
All inputs are finite; a program needn't handle non-finite values.
Results may differ from a plain program's by a relative error of at most 0.0039.
Values may be sent and summed in bfloat16 or wider, within the bound.
No kernel may reach another device: no remote copies, remote signals or barrier semaphores. Data moves between devices by JAX's collectives and lax.ppermute only.
A program may use at most 192 MiB of HBM per device.

v0:
```python
import math

import jax
import jax.numpy as jnp
from jax import lax
from jax.sharding import PartitionSpec as P

HEAD = 128
BLOCK = 64


def masked(weight, keep_mask):
    row_blocks, col_blocks = keep_mask.shape
    expanded = jnp.broadcast_to(keep_mask[:, None, :, None], (row_blocks, BLOCK, col_blocks, BLOCK))
    return weight * expanded.reshape(weight.shape).astype(jnp.bfloat16)


def layer_norm(values):
    center = values - jnp.mean(values, axis=-1, keepdims=True)
    spread = jnp.mean(center * center, axis=-1, keepdims=True)
    return center * lax.rsqrt(spread + 1e-06)


def norm_heads(flat_rows, gains):
    shaped_rows = flat_rows.reshape(flat_rows.shape[0], -1, HEAD).astype(jnp.float32)
    scaled = (
        shaped_rows
        * lax.rsqrt(jnp.mean(shaped_rows * shaped_rows, axis=-1, keepdims=True) + 1e-06)
        * gains
    )
    return scaled.astype(jnp.bfloat16)


def attend(queries, keys_normed, values):
    scores = jnp.einsum(
        "qhd,khd->hqk", queries, keys_normed, preferred_element_type=jnp.float32
    ) / math.sqrt(HEAD)
    weights = jnp.exp(scores)
    denoms = jnp.sum(weights, axis=2)
    summed = jnp.einsum(
        "hqk,khd->qhd", weights.astype(jnp.bfloat16), values, preferred_element_type=jnp.float32
    )
    return (summed, denoms)


def shards(
    tokens,
    modulation,
    qkv_weight,
    qkv_bias,
    norm_gains,
    up_weight,
    up_mask,
    up_bias,
    proj_weight,
    down_weight,
    down_mask,
    out_bias,
):
    own_rows = tokens[0]
    mod_rows = modulation[0]
    row_count = own_rows.shape[0]
    feature_count = own_rows.shape[1]
    head_count = feature_count // HEAD
    normed = layer_norm(own_rows.astype(jnp.float32))
    shaped = ((1.0 + mod_rows[1]) * normed + mod_rows[0]).astype(jnp.bfloat16)
    gathered = lax.all_gather(shaped, "seq", axis=0, tiled=True)
    seq_len = gathered.shape[0]
    col_share = qkv_weight.shape[2]
    up_local = masked(up_weight, up_mask)
    pieces = (
        lax.all_gather(qkv_weight, "wt", axis=0, tiled=True),
        lax.all_gather(up_local, "wt", axis=0, tiled=True),
    )
    piece_rows = pieces[0].shape[0]
    first = jnp.dot(
        gathered, pieces[0].reshape(piece_rows, 3 * col_share), preferred_element_type=jnp.float32
    )
    second = jnp.dot(gathered, pieces[1], preferred_element_type=jnp.float32)
    qkv_local = (first.reshape(seq_len, 3, col_share) + qkv_bias).astype(jnp.bfloat16)
    hidden = jax.nn.gelu(second + up_bias, approximate=True).astype(jnp.bfloat16)
    query_flat = lax.all_to_all(qkv_local[:, 0, :], "seq", split_axis=0, concat_axis=1, tiled=True)
    kv_whole = lax.all_gather(qkv_local[:, 1:, :], "seq", axis=2, tiled=True)
    queries = norm_heads(query_flat, norm_gains[0])
    keys_normed = norm_heads(kv_whole[:, 0, :], norm_gains[1])
    values = kv_whole[:, 1, :].reshape(seq_len, head_count, HEAD)
    summed, denoms = attend(queries, keys_normed, values)
    attended = (
        (summed / denoms.T[:, :, None]).reshape(row_count, feature_count).astype(jnp.bfloat16)
    )
    attended_cols = lax.all_to_all(attended, "seq", split_axis=1, concat_axis=0, tiled=True)
    down_local = masked(down_weight, down_mask)
    proj_full, down_full = (
        lax.all_gather(proj_weight, "wt", axis=1, tiled=True),
        lax.all_gather(down_local, "wt", axis=1, tiled=True),
    )
    branch_sum = lax.psum_scatter(
        jnp.dot(attended_cols, proj_full, preferred_element_type=jnp.float32)
        + jnp.dot(hidden, down_full, preferred_element_type=jnp.float32),
        "seq",
        scatter_dimension=0,
        tiled=True,
    )
    result = own_rows.astype(jnp.float32) + mod_rows[2] * (branch_sum + out_bias)
    return result.astype(jnp.bfloat16)[None]


def solution(mesh):
    return jax.shard_map(
        shards,
        mesh=mesh,
        in_specs=(
            P(("rep", "wt"), "seq", None),
            P(("rep", "wt"), None, None),
            P("wt", None, "seq"),
            P(None, "seq"),
            P(),
            P("wt", "seq"),
            P("wt", "seq"),
            P("seq"),
            P("seq", "wt"),
            P("seq", "wt"),
            P("seq", "wt"),
            P(),
        ),
        out_specs=P(("rep", "wt"), "seq", None),
        check_vma=False,
    )
```

profile of v0, /device:TPU:0, one launch (start us, length us, event | category | flops | bytes accessed | tf_op | source)
XLA Modules:
  0.0 447.9 jit_solution(10518462295417915914)
XLA Ops:
  6.5 6.1 %copy.22 = bf16[768,3,768]{0,2,1:T(8,128)(2,1)} copy(bf16[768,3,768]{2,0,1:T(8,128)(2,1)} %param.14) | data formatting | bytes 7077888 | tf_op args[2]
  12.7 0.7 all-gather.8.cloned.1.call-update
  13.4 4.9 %broadcast_in_dim.7 = bf16[48,64,12,64]{1,0,3,2:T(8,128)(2,1)} broadcast(bf16[48,12]{0,1:T(8,128)(2,1)S(1)} %convert_element_type.85), dimensions={0,2} | broadcast | bytes 4719744 | tf_op jit(solution)/shard_map/broadcast_in_dim | solution.py:14
  18.4 13.3 %convert_element_type.86 = bf16[3072,768]{0,1:T(8,128)(2,1)} reshape(bf16[48,64,12,64]{1,0,3,2:T(8,128)(2,1)} %broadcast_in_dim.7) | data formatting | bytes 9437184 | tf_op jit(solution)/shard_map/convert_element_type | solution.py:15
  31.7 6.7 %copy.27 = bf16[3072,768]{0,1:T(8,128)(2,1)} copy(bf16[3072,768]{1,0:T(8,128)(2,1)} %param.21) | data formatting | bytes 9437184 | tf_op args[9]
  38.4 8.0 %mul.129 = bf16[3072,768]{0,1:T(8,128)(2,1)} multiply(bf16[3072,768]{0,1:T(8,128)(2,1)} %copy.27, bf16[3072,768]{0,1:T(8,128)(2,1)} %convert_element_type.86) | non-fusion elementwise | flops 2359296 | bytes 14155776 | tf_op jit(solution)/shard_map/mul | solution.py:15
  46.5 5.0 %broadcast_in_dim.6 = bf16[12,64,48,64]{3,2,1,0:T(8,128)(2,1)} broadcast(bf16[12,48]{1,0:T(8,128)(2,1)S(1)} %convert_element_type.82), dimensions={0,2} | broadcast | bytes 4719744 | tf_op jit(solution)/shard_map/broadcast_in_dim | solution.py:14
  51.5 12.6 %convert_element_type.83 = bf16[768,3072]{1,0:T(8,128)(2,1)} reshape(bf16[12,64,48,64]{3,2,1,0:T(8,128)(2,1)} %broadcast_in_dim.6) | data formatting | bytes 9437184 | tf_op jit(solution)/shard_map/convert_element_type | solution.py:15
  64.2 7.9 %mul.121 = bf16[768,3072]{1,0:T(8,128)(2,1)} multiply(bf16[768,3072]{1,0:T(8,128)(2,1)} %param.17, bf16[768,3072]{1,0:T(8,128)(2,1)} %convert_element_type.83) | non-fusion elementwise | flops 2359296 | bytes 14155776 | tf_op jit(solution)/shard_map/mul | solution.py:15
  72.1 0.1 convert_reduce_fusion
  72.3 0.2 fusion.30
  72.6 15.0 %all-gather = bf16[4,4,3072]{2,1,0:T(4,128)(2,1)S(1)} all-gather(bf16[1,4,3072]{2,1,0:T(4,128)(2,1)S(1)} %fusion.37), channel_id=1, replica_groups=mesh['rep'=2,'seq'=4,'wt'=4] {'seq'}, dimensions={0}, use_global_device_ids=true | all-gather | bytes 122880 | tf_op jit(solution)/shard_map/all_gather | solution.py:67
  87.7 18.8 %all-gather.6.cloned.1.call-done = bf16[3072,3,768]{0,2,1:T(8,128)(2,1)} async-done(((bf16[768,3,768]{0,2,1:T(8,128)(2,1)}), bf16[3072,3,768]{0,2,1:T(8,128)(2,1)}) %all-gather.6.cloned.1.call-update) | async-done | bytes 14155792 | tf_op jit(solution)/shard_map/all_gather | solution.py:72
  106.5 8.8 %fusion.5 = bf16[16,3,768]{2,0,1:T(8,128)(2,1)S(1)} fusion(bf16[16,3072,1]{1,0,2:T(8,128)(2,1)S(1)} %reshape.80, bf16[3072,3,768]{0,2,1:T(8,128)(2,1)} %all-gather.6.cloned.1.call-done, f32[3,768]{1,0:T(4,128)S(1)} %copy-done.3), kind=kOutput, calls=%fused_computation.5 | convolution fusion | flops 226566144 | bytes 14337024 | tf_op jit(solution)/shard_map/dot_general | solution.py:76
  115.3 13.6 %all_gather.20 = bf16[16,2,3072]{2,0,1:T(8,128)(2,1)S(1)} all-gather(bf16[16,2,768]{2,0,1:T(8,128)(2,1)S(1)} %slice.39), channel_id=1, replica_groups=mesh['rep'=2,'seq'=4,'wt'=4] {'seq'}, dimensions={2}, use_global_device_ids=true | all-gather | bytes 245760 | tf_op jit(solution)/shard_map/all_gather | solution.py:83
  129.0 0.6 all_to_all.22
  129.6 4.9 %all-to-all-start = ((bf16[4,4,768]{2,1,0:T(4,128)(2,1)}), bf16[4,4,768]{2,1,0:T(4,128)(2,1)S(1)}, u32[]{:S(2)}, u32[]{:S(2)}) async-start(bf16[4,4,768]{2,1,0:T(4,128)(2,1)} %all_to_all.22), calls=%async_computation | async-start | bytes 49152 | tf_op jit(solution)/shard_map/all_to_all | solution.py:82
  134.6 0.1 multiply_reduce_fusion
  134.7 0.1 multiply_convert_fusion
  134.9 5.3 %all-to-all-done = bf16[4,4,768]{2,1,0:T(4,128)(2,1)S(1)} async-done(((bf16[4,4,768]{2,1,0:T(4,128)(2,1)}), bf16[4,4,768]{2,1,0:T(4,128)(2,1)S(1)}, u32[]{:S(2)}, u32[]{:S(2)}) %all-to-all-start) | async-done | bytes 24608 | tf_op jit(solution)/shard_map/all_to_all | solution.py:82
  140.2 0.1 multiply_reduce_fusion.1
  140.4 0.3 fusion.46
  140.7 0.8 fusion.10
  141.4 3.3 all-to-all-start.1
  144.8 5.5 %all-to-all-done.1 = bf16[4,4,768]{2,0,1:T(4,128)(2,1)S(1)} async-done(((bf16[4,4,768]{2,0,1:T(4,128)(2,1)}), bf16[4,4,768]{2,0,1:T(4,128)(2,1)S(1)}, u32[]{:S(2)}, u32[]{:S(2)}) %all-to-all-start.1) | async-done | bytes 24608 | tf_op jit(solution)/shard_map/all_to_all | solution.py:91
  150.3 3.1 fusion.47
  153.4 113.8 %all-gather.12.cloned.1.call-done = bf16[3072,3072]{0,1:T(8,128)(2,1)} async-done(((bf16[3072,768]{0,1:T(8,128)(2,1)}), bf16[3072,3072]{0,1:T(8,128)(2,1)}) %all-gather.12.cloned.1.call-update) | async-done | bytes 18874384 | tf_op jit(solution)/shard_map/all_gather | solution.py:95
  267.2 121.5 %all-gather.10.cloned.1.call-done = bf16[3072,3072]{1,0:T(8,128)(2,1)} async-done(((bf16[768,3072]{1,0:T(8,128)(2,1)}), bf16[3072,3072]{1,0:T(8,128)(2,1)}) %all-gather.10.cloned.1.call-update) | async-done | bytes 18874384 | tf_op jit(solution)/shard_map/all_gather | solution.py:73
  388.7 16.2 %convolution_add_fusion = f32[16,3072]{1,0:T(8,128)} fusion(f32[16,3072]{1,0:T(8,128)S(1)} %fusion.47, bf16[3072,3072]{0,1:T(8,128)(2,1)} %all-gather.12.cloned.1.call-done, bf16[16,3072]{1,0:T(8,128)(2,1)S(1)} %reshape.79, bf16[3072,3072]{1,0:T(8,128)(2,1)} %all-gather.10.cloned.1.call-done, f32[3072]{0:T(1024)S(1)} %copy-done.2), kind=kOutput, calls=%fused_computation.2 | convolution fusion | flops 604520448 | bytes 38252544 | tf_op jit(solution)/shard_map/dot_general | solution.py:99
  404.9 0.6 dynamic-slice
  406.1 33.7 %all-reduce.3.cloned.1.call-done = f32[16,3072]{1,0:T(8,128)} async-done(((f32[16,3072]{1,0:T(8,128)}), f32[16,3072]{1,0:T(8,128)}) %all-reduce.3.cloned.1.call-update) | async-done | bytes 196624
  439.9 1.5 fusion.36
  (46 shorter events, 0.6 us)
Async XLA Ops:
  6.5 6.9 %copy-start.5 = (s32[48,12]{0,1:T(8,128)S(1)}, s32[48,12]{0,1:T(8,128)}, u32[]{:S(2)}) copy-start(s32[48,12]{0,1:T(8,128)} %param.22) | copy-start | bytes 6916
  6.5 100.0 %all-gather.6.cloned.1.call-start = ((), (), s32[]{:S(2)}) async-start(), calls=%async_computation.2 | async-start | bytes 17694720 | tf_op jit(solution)/shard_map/all_gather | solution.py:72
  12.6 137.7 %all-gather.8.cloned.1.call-start = ((), (), s32[]{:S(2)}) async-start(), calls=%async_computation.3 | async-start | bytes 5898240 | tf_op jit(solution)/shard_map/all_gather | solution.py:94
  13.4 253.8 %all-gather.12.cloned.1.call-start = ((), (), s32[]{:S(2)}) async-start(), calls=%async_computation.5 | async-start | bytes 23592960 | tf_op jit(solution)/shard_map/all_gather | solution.py:95
  38.4 8.1 %copy-start.6 = (s32[12,48]{1,0:T(8,128)S(1)}, s32[12,48]{1,0:T(8,128)}, u32[]{:S(2)}) copy-start(s32[12,48]{1,0:T(8,128)} %param.18) | copy-start | bytes 6916
  46.5 342.2 %all-gather.10.cloned.1.call-start = ((), (), s32[]{:S(2)}) async-start(), calls=%async_computation.4 | async-start | bytes 23592960 | tf_op jit(solution)/shard_map/all_gather | solution.py:73
  64.2 8.0 %copy-start = (bf16[1,4,3072]{2,1,0:T(4,128)(2,1)S(1)}, bf16[1,4,3072]{2,1,0:T(4,128)(2,1)}, u32[]{:S(2)}) copy-start(bf16[1,4,3072]{2,1,0:T(4,128)(2,1)} %param.12) | copy-start | bytes 73732
  64.2 8.3 %copy-start.1 = (f32[1,3,3072]{2,0,1:T(1,128)S(1)}, f32[1,3,3072]{2,0,1:T(1,128)}, u32[]{:S(2)}) copy-start(f32[1,3,3072]{2,0,1:T(1,128)} %param.13) | copy-start | bytes 110596
  64.2 23.5 %copy-start.7 = (f32[2,128]{1,0:T(2,128)S(1)}, f32[2,128]{1,0:T(2,128)}, u32[]{:S(2)}) copy-start(f32[2,128]{1,0:T(2,128)} %param.16) | copy-start | bytes 3076
  64.2 42.3 %copy-start.3 = (f32[3,768]{1,0:T(4,128)S(1)}, f32[3,768]{1,0:T(4,128)}, u32[]{:S(2)}) copy-start(f32[3,768]{1,0:T(4,128)} %param.15) | copy-start | bytes 27652
  87.7 301.0 %copy-start.2 = (f32[3072]{0:T(1024)S(1)}, f32[3072]{0:T(1024)}, u32[]{:S(2)}) copy-start(f32[3072]{0:T(1024)} %param.19) | copy-start | bytes 36868
  129.6 10.6 %all-to-all-start = ((bf16[4,4,768]{2,1,0:T(4,128)(2,1)}), bf16[4,4,768]{2,1,0:T(4,128)(2,1)S(1)}, u32[]{:S(2)}, u32[]{:S(2)}) async-start(bf16[4,4,768]{2,1,0:T(4,128)(2,1)} %all_to_all.22), calls=%async_computation | async-start | bytes 49152 | tf_op jit(solution)/shard_map/all_to_all | solution.py:82
  141.4 8.9 %all-to-all-start.1 = ((bf16[4,4,768]{2,0,1:T(4,128)(2,1)}), bf16[4,4,768]{2,0,1:T(4,128)(2,1)S(1)}, u32[]{:S(2)}, u32[]{:S(2)}) async-start(bf16[4,4,768]{2,0,1:T(4,128)(2,1)} %bitcast.15), calls=%async_computation.1 | async-start | bytes 49152 | tf_op jit(solution)/shard_map/all_to_all | solution.py:91
  144.7 295.2 %all-reduce.3.cloned.1.call-start = ((), (), s32[]{:S(2)}) async-start(), calls=%async_computation.6 | async-start | bytes 393216
  153.4 251.5 %copy-start.8 = (u32[32]{0:T(128)S(1)}, u32[32]{0:T(128)}, u32[]{:S(2)}) copy-start(u32[32]{0:T(128)} %constant.31) | copy-start | bytes 388
  153.4 286.5 %copy-start.4 = (f32[3072]{0:T(1024)S(1)}, f32[3072]{0:T(1024)}, u32[]{:S(2)}) copy-start(f32[3072]{0:T(1024)} %param.23) | copy-start | bytes 36868
Sparse Core Ops, SparseCore 0:
  12.7 93.7 all-gather.5
  108.1 37.4 all-gather.7
  147.1 120.0 all-gather.11
  268.6 120.0 all-gather.9
  405.0 34.8 all-reduce.2
where the time goes:
time: 449 us; the launch traced here: 448 us
  waiting for transfers between devices  299 us (67%)
  local copies, waits for them, and re-layouts  50 us (11%)
  matrix products  29.1 us (6%)
  blocking collectives  28.7 us (6%)
  other arithmetic  18.4 us (4%)
  between operations  14 us (3%)
  starting transfers between devices  8.37 us (2%)
    all_gather x1, waiting for transfers between devices, shards(): lax.all_gather(up_local, 'wt', axis=0, tiled=True)  121 us
    all_gather x1, waiting for transfers between devices, shards(): lax.all_gather(down_local, 'wt', axis=1, tiled=True)  114 us
    unnamed x6, waiting for transfers between devices  34.5 us
    convert_element_type x2, local copies, waits for them, and re-layouts, masked(): return weight * expanded.reshape(weight.shape).astype(jnp.bfloat16)  25.9 us
    all_gather x1, waiting for transfers between devices, shards(): lax.all_gather(qkv_weight, 'wt', axis=0, tiled=True)  18.8 us
    dot_general x1, matrix products, shards(): jnp.dot(hidden, down_full, preferred_element_type=jnp.float32)  16.2 us
    mul x2, other arithmetic, masked(): return weight * expanded.reshape(weight.shape).astype(jnp.bfloat16)  16 us
    all_gather x1, blocking collectives, shards(): gathered = lax.all_gather(shaped, 'seq', axis=0, tiled=True)  15 us
  transfers between devices with their start and end apart: 7, of which 6 were waited for; matrix products, arithmetic and copies ran while one was open for 16% of the time, Pallas kernels for 0%

commit v1 on v0

--- a/solution.py
+++ b/solution.py
@@ -1,12 +1,16 @@
+import functools
 import math
 
 import jax
 import jax.numpy as jnp
 from jax import lax
+from jax.experimental import pallas as pl
+from jax.experimental.pallas import tpu as pltpu
 from jax.sharding import PartitionSpec as P
 
 HEAD = 128
 BLOCK = 64
+MIB = 1024 * 1024
 
 
 def masked(weight, keep_mask):
@@ -43,7 +47,7 @@
     return (summed, denoms)
 
 
-def shards(
+def gathered_shards(
     tokens,
     modulation,
     qkv_weight,
@@ -105,7 +109,230 @@
     return result.astype(jnp.bfloat16)[None]
 
 
+def spread_lanes(mask, lanes):
+    cols = mask.shape[1]
+    pick = (
+        lax.broadcasted_iota(jnp.int32, (cols, lanes), 1) // BLOCK
+        == lax.broadcasted_iota(jnp.int32, (cols, lanes), 0)
+    ).astype(jnp.bfloat16)
+    return jnp.dot(mask.astype(jnp.bfloat16), pick, preferred_element_type=jnp.float32).astype(jnp.bfloat16)
+
+
+def mask_rows(weight, spread):
+    return jnp.concatenate(
+        [weight[b * BLOCK : (b + 1) * BLOCK] * spread[b : b + 1] for b in range(spread.shape[0])], axis=0
+    )
+
+
+def in_kernel(qkv_steps, x_ref, wqkv_ref, up_ref, mask_ref, keep_ref, send_ref):
+    i = pl.program_id(0)
+    half = x_ref.shape[0] // 2
+
+    def put(out):
+        keep_ref[...] = out[:half]
+        send_ref[...] = out[half:].astype(jnp.bfloat16)
+
+    @pl.when(i < qkv_steps)
+    def _():
+        put(jnp.dot(x_ref[...], wqkv_ref[...], preferred_element_type=jnp.float32))
+
+    @pl.when(i >= qkv_steps)
+    def _():
+        weight = mask_rows(up_ref[...], spread_lanes(mask_ref[...], up_ref.shape[1]))
+        put(jnp.dot(x_ref[...], weight, preferred_element_type=jnp.float32))
+
+
+def in_products(x, qkv_weight, up_weight, up_mask):
+    rows, depth = x.shape
+    share = qkv_weight.shape[2]
+    hidden = up_weight.shape[1]
+    ff_steps = hidden // share
+    steps = 3 + ff_steps
+    blocks = share // BLOCK
+    masks = up_mask.reshape(-1, ff_steps, blocks).transpose(1, 0, 2)
+    half = rows // 2
+    return pl.pallas_call(
+        functools.partial(in_kernel, 3),
+        grid=(steps,),
+        in_specs=[
+            pl.BlockSpec((rows, depth), lambda i: (0, 0)),
+            pl.BlockSpec((None, depth, share), lambda i: (jnp.minimum(i, 2), 0, 0)),
+            pl.BlockSpec((depth, share), lambda i: (0, jnp.maximum(i - 3, 0))),
+            pl.BlockSpec((None, depth // BLOCK, blocks), lambda i: (jnp.maximum(i - 3, 0), 0, 0)),
+        ],
+        out_specs=[
+            pl.BlockSpec((half, share), lambda i: (0, i)),
+            pl.BlockSpec((half, share), lambda i: (0, i)),
+        ],
+        out_shape=[
+            jax.ShapeDtypeStruct((half, steps * share), jnp.float32),
+            jax.ShapeDtypeStruct((half, steps * share), jnp.bfloat16),
+        ],
+        compiler_params=pltpu.CompilerParams(vmem_limit_bytes=40 * MIB),
+        name="in_products",
+    )(x, qkv_weight.transpose(1, 0, 2), up_weight, masks)
+
+
+def mid_kernel(images, own_ref, other_ref, qkv_bias_ref, gains_ref, up_bias_ref, out_ref):
+    rows = own_ref.shape[0]
+    share = qkv_bias_ref.shape[1]
+    heads = share // HEAD
+    length = rows // images
+
+    def total(start, size):
+        return own_ref[:, start : start + size] + other_ref[:, start : start + size].astype(jnp.float32)
+
+    def stacked(which):
+        flat = (total(which * share, share) + qkv_bias_ref[which : which + 1, :]).astype(jnp.bfloat16)
+        return jnp.concatenate([flat[:, h * HEAD : (h + 1) * HEAD] for h in range(heads)], axis=0)
+
+    def normed(which):
+        wide = stacked(which).astype(jnp.float32)
+        scale = lax.rsqrt(jnp.mean(wide * wide, axis=-1, keepdims=True) + 1e-06)
+        return (wide * scale * gains_ref[which : which + 1, :]).astype(jnp.bfloat16)
+
+    queries, keys, values = normed(0), normed(1), stacked(2)
+    scores = lax.dot_general(
+        queries, keys, (((1,), (1,)), ((), ())), preferred_element_type=jnp.float32
+    ) * (1.0 / math.sqrt(HEAD))
+    size = heads * rows
+    same = (
+        lax.broadcasted_iota(jnp.int32, (size, size), 0) // length
+        == lax.broadcasted_iota(jnp.int32, (size, size), 1) // length
+    )
+    weights = jnp.where(same, jnp.exp(jnp.where(same, scores, 0.0)), 0.0)
+    denoms = jnp.sum(weights, axis=-1, keepdims=True)
+    summed = jnp.dot(weights.astype(jnp.bfloat16), values, preferred_element_type=jnp.float32)
+    attended = (summed / denoms).astype(jnp.bfloat16)
+    for h in range(heads):
+        out_ref[:, h * HEAD : (h + 1) * HEAD] = attended[h * rows : (h + 1) * rows]
+    hidden = out_ref.shape[1] - share
+    for start in range(0, hidden, share):
+        v = total(3 * share + start, share) + up_bias_ref[:, start : start + share]
+        cubic = math.sqrt(2.0 / math.pi) * (v + 0.044715 * (v * v * v))
+        out_ref[:, share + start : 2 * share + start] = (0.5 * v * (1.0 + jnp.tanh(cubic))).astype(jnp.bfloat16)
+
+
+def middle(images, own, other, qkv_bias, gains, up_bias):
+    rows = own.shape[0]
+    share = qkv_bias.shape[1]
+    width = own.shape[1] - 2 * share
+    return pl.pallas_call(
+        functools.partial(mid_kernel, images),
+        out_shape=jax.ShapeDtypeStruct((rows, width), jnp.bfloat16),
+        compiler_params=pltpu.CompilerParams(vmem_limit_bytes=40 * MIB),
+        name="middle",
+    )(own, other, qkv_bias, gains, up_bias.reshape(1, -1))
+
+
+def out_kernel(a_ref, b_ref, proj_ref, down_ref, mask_ref, out_ref, acc_ref):
+    i = pl.program_id(0)
+    x = jnp.concatenate([a_ref[...], b_ref[...]], axis=0)
+
+    @pl.when(i == 0)
+    def _():
+        acc_ref[...] = jnp.dot(x, proj_ref[...], preferred_element_type=jnp.float32)
+
+    @pl.when(i > 0)
+    def _():
+        weight = mask_rows(down_ref[...], spread_lanes(mask_ref[...], down_ref.shape[1]))
+        acc_ref[...] += jnp.dot(x, weight, preferred_element_type=jnp.float32)
+
+    @pl.when(i == pl.num_programs(0) - 1)
+    def _():
+        out_ref[...] = acc_ref[...].astype(jnp.bfloat16)
+
+
+def out_products(mine, theirs, proj_weight, down_weight, down_mask):
+    half = mine.shape[0]
+    depth, width = proj_weight.shape
+    steps = mine.shape[1] // depth
+    blocks = depth // BLOCK
+    masks = down_mask.reshape(steps - 1, blocks, -1)
+    return pl.pallas_call(
+        out_kernel,
+        grid=(steps,),
+        in_specs=[
+            pl.BlockSpec((half, depth), lambda i: (0, i)),
+            pl.BlockSpec((half, depth), lambda i: (0, i)),
+            pl.BlockSpec((depth, width), lambda i: (0, 0)),
+            pl.BlockSpec((depth, width), lambda i: (jnp.maximum(i - 1, 0), 0)),
+            pl.BlockSpec((None, blocks, width // BLOCK), lambda i: (jnp.maximum(i - 1, 0), 0, 0)),
+        ],
+        out_specs=pl.BlockSpec((2 * half, width), lambda i: (0, 0)),
+        out_shape=jax.ShapeDtypeStruct((2 * half, width), jnp.bfloat16),
+        scratch_shapes=[pltpu.VMEM((2 * half, width), jnp.float32)],
+        compiler_params=pltpu.CompilerParams(vmem_limit_bytes=40 * MIB),
+        name="out_products",
+    )(mine, theirs, proj_weight, down_weight, masks)
+
+
+def swap(values, bit):
+    count = lax.axis_size("wt")
+    return lax.ppermute(values, "wt", [(i, i ^ bit) for i in range(count)])
+
+
+def fixed_shards(
+    tokens,
+    modulation,
+    qkv_weight,
+    qkv_bias,
+    norm_gains,
+    up_weight,
+    up_mask,
+    up_bias,
+    proj_weight,
+    down_weight,
+    down_mask,
+    out_bias,
+):
+    both = ("seq", "wt")
+    seq, wt = lax.axis_size("seq"), lax.axis_size("wt")
+    me = lax.axis_index("wt")
+    own_rows = tokens[0]
+    mod_rows = modulation[0]
+    count, features = own_rows.shape
+    share = features // wt
+    normed = layer_norm(own_rows.astype(jnp.float32))
+    shaped = ((1.0 + mod_rows[1]) * normed + mod_rows[0]).astype(jnp.bfloat16)
+    sent = jnp.broadcast_to(shaped.reshape(count, wt, share).transpose(1, 0, 2)[None], (seq, wt, count, share))
+    got = lax.all_to_all(sent.reshape(seq * wt, count, share), both, split_axis=0, concat_axis=0, tiled=True)
+    got = got.reshape(seq, wt, count, share)
+    rows = jnp.concatenate(
+        [
+            lax.dynamic_index_in_dim(got, me ^ j, 1, keepdims=False).reshape(seq * count, share)
+            for j in (0, 2, 1, 3)
+        ],
+        axis=0,
+    )
+    kept, given = in_products(rows, qkv_weight, up_weight, up_mask)
+    pair = kept + swap(given, 1).astype(jnp.float32)
+    length = seq * count
+    turned = jnp.concatenate([pair[length:], pair[:length]], axis=0).astype(jnp.bfloat16)
+    mixed = middle(2, pair, swap(turned, 2), qkv_bias, norm_gains, up_bias)
+    shares = out_products(mixed, swap(mixed, 1), proj_weight, down_weight, down_mask)
+    shares = shares.reshape(wt, seq, count, share)
+    order = (0, 2, 1, 3)
+    place = jnp.array([order.index(j) for j in range(wt)], jnp.int32)
+    home = jnp.stack(
+        [lax.dynamic_index_in_dim(shares, place[me ^ i], 0, keepdims=False) for i in range(wt)], axis=1
+    )
+    back = lax.all_to_all(home.reshape(seq * wt, count, share), both, split_axis=0, concat_axis=0, tiled=True)
+    branch = jnp.sum(back.reshape(seq, wt, count, share).astype(jnp.float32), axis=0)
+    branch = branch.transpose(1, 0, 2).reshape(count, features)
+    result = own_rows.astype(jnp.float32) + mod_rows[2] * (branch + out_bias)
+    return result.astype(jnp.bfloat16)[None]
+
+
 def solution(mesh):
+    seq, wt = mesh.shape["seq"], mesh.shape["wt"]
+
+    def shards(*args):
+        share = args[2].shape[2]
+        whole_heads = share % HEAD == 0 and share == args[8].shape[1] and args[5].shape[1] % share == 0
+        fits = whole_heads and wt == 4 and (seq * args[0].shape[1]) % 16 == 0
+        return (fixed_shards if fits else gathered_shards)(*args)
+
     return jax.shard_map(
         shards,
         mesh=mesh,

time: 449 us -> 64.7 us (0.14)
  waiting for transfers between devices: 299 us -> 18.3 us
  local copies, waits for them, and re-layouts: 50 us -> 10 us
  matrix products: 29.1 us -> 0 us
  blocking collectives: 28.7 us -> 9.99 us
  other arithmetic: 18.4 us -> 3.61 us
  Pallas kernels: 0 us -> 6.4 us
  between operations: 14 us -> 8.08 us
    all_gather x4 -> x0, waiting for transfers between devices: 254 us -> none  [the longest x1 121 us: shards(): lax.all_gather(up_local, 'wt', axis=0, tiled=True)]
    unnamed x6 -> x0, waiting for transfers between devices: 34.5 us -> none
    dot_general x5 -> x0, matrix products: 29.1 us -> none  [the longest x1 16.2 us: shards(): jnp.dot(hidden, down_full, preferred_element_type=jnp.float32)]
    all_gather x2 -> x0, blocking collectives: 28.7 us -> none  [the longest x1 15 us: shards(): gathered = lax.all_gather(shaped, 'seq', axis=0, tiled=True)]
    convert_element_type x2 -> x1, local copies, waits for them, and re-layouts: 25.9 us -> 0.76 us  [fixed_shards(): result = own_rows.astype(jnp.float32) + mod_rows[2] * (branch + out_bias)]
    mul x2 -> x0, other arithmetic: 16 us -> none  [masked(): return weight * expanded.reshape(weight.shape).astype(jnp.bfloat16)]
    ppermute x0 -> x3, waiting for transfers between devices: none -> 11.7 us  [swap(): return lax.ppermute(values, 'wt', [(i, i ^ bit) for i in range(count)])]
    all_to_all x0 -> x1, blocking collectives: none -> 9.99 us  [fixed_shards(): lax.all_to_all(home.reshape(seq * wt, count, share), both, split_axis=0,...]
  transfers between devices with their start and end apart: 7 -> 4, of which waited for: 6 -> 3; matrix products, arithmetic and copies ran while one was open for 16% -> 3% of each run, Pallas kernels for 0% -> 0%
where the time goes in v1:
time: 64.7 us; the launch traced here: 64 us
  waiting for transfers between devices  18.3 us (28%)
  local copies, waits for them, and re-layouts  10 us (15%)
  blocking collectives  9.99 us (15%)
  between operations  8.08 us (12%)
  starting transfers between devices  7.57 us (12%)
  Pallas kernels  6.4 us (10%)
  other arithmetic  3.61 us (6%)
    ppermute x3, waiting for transfers between devices, swap(): return lax.ppermute(values, 'wt', [(i, i ^ bit) for i in range(count)])  11.7 us
    all_to_all x1, blocking collectives, fixed_shards(): lax.all_to_all(home.reshape(seq * wt, count, share), both, split_axis=0,...  9.99 us
    all_to_all x1, starting transfers between devices, fixed_shards(): lax.all_to_all(sent.reshape(seq * wt, count, share), both, split_axis=0,...  7.36 us
    unnamed x22, local copies, waits for them, and re-layouts  6.7 us
    all_to_all x1, waiting for transfers between devices, fixed_shards(): lax.all_to_all(sent.reshape(seq * wt, count, share), both, split_axis=0,...  6.59 us
    pallas_call x1, Pallas kernels, in_products(): pl.pallas_call(functools.partial(in_kernel, 3), grid=(steps,), in_specs=[...  3.5 us
    pallas_call x1, Pallas kernels, out_products(): pl.pallas_call(out_kernel, grid=(steps,), in_specs=[pl.BlockSpec((half, d...  2.39 us
  transfers between devices with their start and end apart: 4, of which 3 were waited for; matrix products, arithmetic and copies ran while one was open for 3% of the time, Pallas kernels for 0%

profile of v1, /device:TPU:0, one launch (start us, length us, event | category | flops | bytes accessed | tf_op | source)
XLA Modules:
  0.0 64.0 jit_solution(10617601207673054209)
XLA Ops:
  0.0 0.9 %convert_reduce_fusion.1 = f32[4]{0:T(128)S(1)} fusion(bf16[1,4,3072]{2,1,0:T(4,128)(2,1)} %param.13), kind=kLoop, calls=%fused_computation.10 | loop fusion | flops 24572 | bytes 24592 | tf_op jit(solution)/shard_map/reduce_sum | solution.py:23
  0.9 0.8 %reshape.169 = f32[4,4,768]{2,1,0:T(4,128)S(1)} reshape(bf16[1,4,3072]{2,1,0:T(4,128)(2,1)} %param.13) | data formatting | bytes 73728 | tf_op jit(solution)/shard_map/convert_element_type | solution.py:323
  1.6 0.8 %add_reduce_fusion = (f32[3072]{0:T(1024)S(1)}, f32[3072]{0:T(1024)S(1)}, f32[1,1,3072]{2,0,1:T(1,128)S(1)}) fusion(f32[1,3,3072]{2,0,1:T(1,128)} %param.14), kind=kLoop, calls=%fused_computation.18 | loop fusion | flops 3072 | bytes 73728 | tf_op jit(solution)/shard_map/add | solution.py:297
  2.5 0.9 %fusion.1 = f32[4]{0:T(128)S(1)} fusion(bf16[1,4,3072]{2,1,0:T(4,128)(2,1)} %param.13, f32[4]{0:T(128)S(1)} %broadcast_multiply_fusion), kind=kLoop, calls=%fused_computation.7 | loop fusion | flops 49148 | bytes 24608 | tf_op jit(solution)/shard_map/reduce_sum | solution.py:24
  3.5 0.1 fusion.2
  3.6 0.7 %broadcast_in_dim.2 = bf16[4,4,4,768]{3,2,1,0:T(4,128)(2,1)} broadcast(bf16[4,4,768]{2,1,0:T(4,128)(2,1)S(1)} %copy.19), dimensions={1,2,3} | broadcast | bytes 122880 | tf_op jit(solution)/shard_map/broadcast_in_dim | solution.py:298
  4.2 7.4 %all-to-all-start = ((bf16[16,4,768]{2,1,0:T(4,128)(2,1)}), bf16[16,4,768]{2,1,0:T(4,128)(2,1)S(1)}, u32[]{:S(2)}, u32[]{:S(2)}) async-start(bf16[16,4,768]{2,1,0:T(4,128)(2,1)} %bitcast.3), calls=%async_computation | async-start | bytes 196608 | tf_op jit(solution)/shard_map/all_to_all | solution.py:299
  11.6 0.8 %reshape.163 = s32[12,4,12]{2,1,0:T(4,128)S(1)} reshape(s32[12,48]{1,0:T(8,128)} %param.19) | data formatting | bytes 4608 | tf_op jit(solution)/shard_map/reshape | solution.py:152
  12.4 6.6 %all-to-all-done = bf16[16,4,768]{2,1,0:T(4,128)(2,1)S(1)} async-done(((bf16[16,4,768]{2,1,0:T(4,128)(2,1)}), bf16[16,4,768]{2,1,0:T(4,128)(2,1)S(1)}, u32[]{:S(2)}, u32[]{:S(2)}) %all-to-all-start) | async-done | bytes 98336 | tf_op jit(solution)/shard_map/all_to_all | solution.py:299
  19.1 0.0 copy-start.1
  19.2 2.3 %copy-done.1 = bf16[768,3072]{1,0:T(8,128)(2,1)S(1)} copy-done((bf16[768,3072]{1,0:T(8,128)(2,1)S(1)}, bf16[768,3072]{1,0:T(8,128)(2,1)}, u32[]{:S(2)}) %copy-start.1) | copy-done | bytes 4718616
  21.5 2.0 %copy-done.2 = bf16[768,3,768]{2,0,1:T(8,128)(2,1)S(1)} copy-done((bf16[768,3,768]{2,0,1:T(8,128)(2,1)S(1)}, bf16[768,3,768]{2,0,1:T(8,128)(2,1)}, u32[]{:S(2)}) %copy-start.2) | copy-done | bytes 3538968
  23.5 0.0 copy-start.10
  23.5 3.5 %in_products.1 = (f32[32,5376]{1,0:T(8,128)S(1)}, bf16[32,5376]{1,0:T(8,128)(2,1)S(1)}) custom-call(bf16[64,768]{1,0:T(8,128)(2,1)S(1)} %pad_maximum_fusion.1.x_ref, bf16[3,768,768]{2,1,0:T(8,128)(2,1)S(1)} %bitcast.36, bf16[768,3072]{1,0:T(8,128)(2,1)S(1)} %copy-done.1, s32[4,12,12]{2,1,0:T(8,128)S(1)} %bitcast.37), custom_call_target="tpu_custom_call" | custom-call | tf_op jit(solution)/shard_map/in_products/pallas_call | solution.py:154
  27.0 0.1 collective-permute-start
  27.1 1.6 %collective-permute-done = bf16[32,5376]{1,0:T(8,128)(2,1)S(1)} collective-permute-done((bf16[32,5376]{1,0:T(8,128)(2,1)S(1)}, bf16[32,5376]{1,0:T(8,128)(2,1)S(1)}, u32[]{:S(2)}, u32[]{:S(2)}) %collective-permute-start) | collective-permute-done | bytes 344096 | tf_op jit(solution)/shard_map/ppermute | solution.py:272
  28.7 0.1 fusion.3
  28.8 0.0 copy-start.7
  28.9 0.0 copy-start.8
  28.9 0.1 collective-permute-start.1
  29.0 10.1 %collective-permute-done.1.other_ref = bf16[32,5376]{1,0:T(8,128)(2,1)S(1)} collective-permute-done((bf16[32,5376]{1,0:T(8,128)(2,1)S(1)}, bf16[32,5376]{1,0:T(8,128)(2,1)S(1)}, u32[]{:S(2)}, u32[]{:S(2)}) %collective-permute-start.1) | collective-permute-done | bytes 344096 | tf_op jit(solution)/shard_map/ppermute | solution.py:272
  39.1 0.5 middle.1.a_ref
  39.6 0.1 collective-permute-start.2
  39.7 0.7 %fusion.5 = (s32[1]{0:T(128)}, s32[1]{0:T(128)}, s32[1]{0:T(128)}, s32[1]{0:T(128)}) fusion(s32[4]{0:T(128)S(1)} %copy-done.9, s32[]{:T(128)S(6)} %select_n.30, s32[]{:T(128)S(6)} %select_n.32, s32[]{:T(128)S(6)} %select_n.33, s32[]{:T(128)S(6)} %select_n.31), kind=kLoop, calls=%fused_computation.27 | loop fusion | bytes 48 | tf_op jit(solution)/shard_map/dynamic_slice | solution.py:318
  45.5 0.1 reshape.165
  45.6 0.1 copy.21.mask_ref
  48.4 2.3 %copy-done = bf16[3072,768]{1,0:T(8,128)(2,1)S(1)} copy-done((bf16[3072,768]{1,0:T(8,128)(2,1)S(1)}, bf16[3072,768]{1,0:T(8,128)(2,1)}, u32[]{:S(2)}) %copy-start) | copy-done | bytes 4718616
  50.7 2.4 %out_products.1 = bf16[64,768]{1,0:T(8,128)(2,1)S(1)} custom-call(bf16[32,3840]{1,0:T(8,128)(2,1)S(1)} %middle.1.a_ref, bf16[32,3840]{1,0:T(8,128)(2,1)S(1)} %collective-permute-done.2.b_ref, bf16[768,768]{1,0:T(8,128)(2,1)S(1)} %copy-done.3, bf16[3072,768]{1,0:T(8,128)(2,1)S(1)} %copy-done, s32[4,12,12]{2,1,0:T(8,128)S(1)} %copy.21.mask_ref), custom_call_target="tpu_custom_call" | custom-call | tf_op jit(solution)/shard_map/out_products/pallas_call | solution.py:252
  53.2 0.1 pad_maximum_fusion.2
  53.3 10.0 %all_to_all.10 = bf16[16,4,768]{2,1,0:T(4,128)(2,1)S(1)} all-to-all(bf16[16,4,768]{2,1,0:T(4,128)(2,1)S(1)} %bitcast.40), channel_id=1, replica_groups=mesh['rep'=2,'seq'=4,'wt'=4] {'seq','wt'}, dimensions={0} | all-to-all | bytes 196608 | tf_op jit(solution)/shard_map/all_to_all | solution.py:320
  63.3 0.1 convert_reduce_fusion
  63.3 0.6 add_convert_fusion
  (32 shorter events, 0.3 us)
Async XLA Ops:
  4.2 14.8 %all-to-all-start = ((bf16[16,4,768]{2,1,0:T(4,128)(2,1)}), bf16[16,4,768]{2,1,0:T(4,128)(2,1)S(1)}, u32[]{:S(2)}, u32[]{:S(2)}) async-start(bf16[16,4,768]{2,1,0:T(4,128)(2,1)} %bitcast.3), calls=%async_computation | async-start | bytes 196608 | tf_op jit(solution)/shard_map/all_to_all | solution.py:299
  19.1 2.3 %copy-start.1 = (bf16[768,3072]{1,0:T(8,128)(2,1)S(1)}, bf16[768,3072]{1,0:T(8,128)(2,1)}, u32[]{:S(2)}) copy-start(bf16[768,3072]{1,0:T(8,128)(2,1)} %up_ref.1) | copy-start | bytes 14155780
  21.5 2.0 %copy-start.2 = (bf16[768,3,768]{2,0,1:T(8,128)(2,1)S(1)}, bf16[768,3,768]{2,0,1:T(8,128)(2,1)}, u32[]{:S(2)}) copy-start(bf16[768,3,768]{2,0,1:T(8,128)(2,1)} %param.15) | copy-start | bytes 10616836
  23.5 15.6 %copy-start.4 = (f32[3,768]{1,0:T(4,128)S(1)}, f32[3,768]{1,0:T(4,128)}, u32[]{:S(2)}) copy-start(f32[3,768]{1,0:T(4,128)} %qkv_bias_ref.1) | copy-start | bytes 27652
  23.5 15.6 %copy-start.5 = (f32[3072]{0:T(1024)S(1)}, f32[3072]{0:T(1024)}, u32[]{:S(2)}) copy-start(f32[3072]{0:T(1024)} %param.20) | copy-start | bytes 36868
  23.5 15.6 %copy-start.6 = (f32[2,128]{1,0:T(2,128)S(1)}, f32[2,128]{1,0:T(2,128)}, u32[]{:S(2)}) copy-start(f32[2,128]{1,0:T(2,128)} %gains_ref.1) | copy-start | bytes 3076
  23.5 16.2 %copy-start.9 = (s32[4]{0:T(128)S(1)}, s32[4]{0:T(128)}, u32[]{:S(2)}) copy-start(s32[4]{0:T(128)} %constant.46.clone) | copy-start | bytes 52
  23.5 22.0 %copy-start.10 = (s32[48,12]{0,1:T(8,128)S(1)}, s32[48,12]{0,1:T(8,128)}, u32[]{:S(2)}) copy-start(s32[48,12]{0,1:T(8,128)} %param.23) | copy-start | bytes 6916
  23.5 24.9 %copy-start.3 = (bf16[768,768]{1,0:T(8,128)(2,1)S(1)}, bf16[768,768]{1,0:T(8,128)(2,1)}, u32[]{:S(2)}) copy-start(bf16[768,768]{1,0:T(8,128)(2,1)} %proj_ref.1) | copy-start | bytes 3538948
  27.0 1.7 %collective-permute-start = (bf16[32,5376]{1,0:T(8,128)(2,1)S(1)}, bf16[32,5376]{1,0:T(8,128)(2,1)S(1)}, u32[]{:S(2)}, u32[]{:S(2)}) collective-permute-start(bf16[32,5376]{1,0:T(8,128)(2,1)S(1)} %get-tuple-element.8), channel_id=1, source_target_pairs={{0,1},{1,0},{2,3},{3,2},{4,5},{5,4},{6,7},{7,6},{8,9},{9,8},{10,11... | collective-permute-start | bytes 1032200 | tf_op jit(solution)/shard_map/ppermute | solution.py:272
  28.8 34.5 %copy-start.7 = (bf16[1,4,3072]{2,1,0:T(4,128)(2,1)S(1)}, bf16[1,4,3072]{2,1,0:T(4,128)(2,1)}, u32[]{:S(2)}) copy-start(bf16[1,4,3072]{2,1,0:T(4,128)(2,1)} %param.13) | copy-start | bytes 73732
  28.9 34.5 %copy-start.8 = (f32[3072]{0:T(1024)S(1)}, f32[3072]{0:T(1024)}, u32[]{:S(2)}) copy-start(f32[3072]{0:T(1024)} %param.24) | copy-start | bytes 36868
  28.9 10.2 %collective-permute-start.1 = (bf16[32,5376]{1,0:T(8,128)(2,1)S(1)}, bf16[32,5376]{1,0:T(8,128)(2,1)S(1)}, u32[]{:S(2)}, u32[]{:S(2)}) collective-permute-start(bf16[32,5376]{1,0:T(8,128)(2,1)S(1)} %pad_maximum_fusion), channel_id=1, source_target_pairs={{0,2},{1,3},{2,0},{3,1},{4,6},{5,7},{6,4},{7,5},{8,10},{9,11},{10,... | collective-permute-start | bytes 1032200 | tf_op jit(solution)/shard_map/ppermute | solution.py:272
  39.6 8.7 %collective-permute-start.2 = (bf16[32,3840]{1,0:T(8,128)(2,1)S(1)}, bf16[32,3840]{1,0:T(8,128)(2,1)S(1)}, u32[]{:S(2)}, u32[]{:S(2)}) collective-permute-start(bf16[32,3840]{1,0:T(8,128)(2,1)S(1)} %middle.1.a_ref), channel_id=1, source_target_pairs={{0,1},{1,0},{2,3},{3,2},{4,5},{5,4},{6,7},{7,6},{8,9},{9,8},{10,11... | collective-permute-start | bytes 737288 | tf_op jit(solution)/shard_map/ppermute | solution.py:272
  48.4 2.3 %copy-start = (bf16[3072,768]{1,0:T(8,128)(2,1)S(1)}, bf16[3072,768]{1,0:T(8,128)(2,1)}, u32[]{:S(2)}) copy-start(bf16[3072,768]{1,0:T(8,128)(2,1)} %down_ref.1) | copy-start | bytes 14155780

commit v2 on v0

--- a/solution.py
+++ b/solution.py
@@ -1,12 +1,18 @@
+import functools
 import math
 
 import jax
 import jax.numpy as jnp
 from jax import lax
+from jax.experimental import pallas as pl
+from jax.experimental.pallas import tpu as pltpu
 from jax.sharding import PartitionSpec as P
 
 HEAD = 128
 BLOCK = 64
+MIB = 1024 * 1024
+ENTER = 50
+BESIDE = 16 * MIB
 
 
 def masked(weight, keep_mask):
@@ -43,7 +49,7 @@
     return (summed, denoms)
 
 
-def shards(
+def gathered_shards(
     tokens,
     modulation,
     qkv_weight,
@@ -105,7 +111,334 @@
     return result.astype(jnp.bfloat16)[None]
 
 
+def enter_kernel(tokens_hbm, mod_hbm, keep_ref, send_ref, tokens_ref, mod_ref, sems):
+    copies = [
+        pltpu.make_async_copy(tokens_hbm, tokens_ref, sems.at[0]),
+        pltpu.make_async_copy(mod_hbm, mod_ref, sems.at[1]),
+    ]
+    for copy in copies:
+        copy.start()
+    for copy in copies:
+        copy.wait()
+    rows = tokens_ref[0].astype(jnp.float32)
+    shaped = ((1.0 + mod_ref[1]) * layer_norm(rows) + mod_ref[0]).astype(jnp.bfloat16)
+    share = keep_ref.shape[1] // 2
+    even = lax.axis_index("wt") % 2 == 0
+    for x in range(2):
+        first = shaped[:, 2 * x * share : (2 * x + 1) * share]
+        second = shaped[:, (2 * x + 1) * share : (2 * x + 2) * share]
+        keep_ref[:, x * share : (x + 1) * share] = jnp.where(even, first, second)
+        send_ref[:, x * share : (x + 1) * share] = jnp.where(even, second, first)
+
+
+def enter(tokens, modulation):
+    _, count, features = tokens.shape
+    turned = modulation.transpose(1, 0, 2)
+    return pl.pallas_call(
+        enter_kernel,
+        in_specs=[pl.BlockSpec(memory_space=pltpu.HBM)] * 2,
+        out_shape=[jax.ShapeDtypeStruct((count, features // 2), jnp.bfloat16)] * 2,
+        scratch_shapes=[
+            pltpu.VMEM(tokens.shape, tokens.dtype),
+            pltpu.VMEM(turned.shape, turned.dtype),
+            pltpu.SemaphoreType.DMA((2,)),
+        ],
+        compiler_params=pltpu.CompilerParams(vmem_limit_bytes=ENTER * MIB),
+        cost_estimate=pl.CostEstimate(flops=0, bytes_accessed=0, transcendentals=0),
+        name="enter",
+    )(tokens, turned)
+
+
+def quarters(ref, start, count):
+    return ref[start : start + count].astype(jnp.float32)
+
+
+def on_first():
+    return lax.axis_index("wt") < 2
+
+
+def apart(kept, got, mine_ref, send_ref):
+    first = jnp.concatenate([kept[0], got[0]], axis=0)
+    second = jnp.concatenate([kept[1], got[1]], axis=0)
+    mine_ref[...] = jnp.where(on_first(), first, second).astype(mine_ref.dtype)
+    send_ref[...] = jnp.where(on_first(), second, first).astype(send_ref.dtype)
+
+
+def part_kernel(kept_ref, got_ref, mine_ref, send_ref):
+    share = mine_ref.shape[1]
+    halves = [[ref[:, :share].astype(jnp.float32), ref[:, share:].astype(jnp.float32)] for ref in (kept_ref, got_ref)]
+    apart(*halves, mine_ref, send_ref)
+
+
+def near_kernel(mine_ref, theirs_ref, out_ref):
+    count = mine_ref.shape[0] // 2
+    pieces = []
+    for start in (0, count):
+        mine, theirs = quarters(mine_ref, start, count), quarters(theirs_ref, start, count)
+        pieces += [jnp.where(on_first(), mine, theirs), jnp.where(on_first(), theirs, mine)]
+    out_ref[...] = jnp.concatenate(pieces, axis=0).astype(out_ref.dtype)
+
+
+def fold_kernel(kept_ref, got_ref, keep_ref, send_ref):
+    size = keep_ref.shape[0] // 2
+    total = kept_ref[...] + got_ref[...].astype(jnp.float32)
+    keep_ref[...] = jnp.concatenate([total[:size], total[2 * size : 3 * size]], axis=0)
+    send_ref[...] = jnp.concatenate([total[size : 2 * size], total[3 * size :]], axis=0).astype(send_ref.dtype)
+
+
+def divide_kernel(kept_ref, got_ref, mine_ref, send_ref):
+    count = mine_ref.shape[0] // 2
+    total = kept_ref[...] + got_ref[...].astype(jnp.float32)
+    rows = [total[n * count : (n + 1) * count] for n in range(4)]
+    apart(rows[:2], rows[2:], mine_ref, send_ref)
+
+
+def join_kernel(mine_ref, theirs_ref, here_ref, send_ref):
+    count = mine_ref.shape[0] // 2
+    for start, ref in ((0, here_ref), (count, send_ref)):
+        mine, theirs = quarters(mine_ref, start, count), quarters(theirs_ref, start, count)
+        ref[...] = jnp.concatenate(
+            [jnp.where(on_first(), mine, theirs), jnp.where(on_first(), theirs, mine)], axis=0
+        )
+
+
+def leave_kernel(here_ref, there_ref, tokens_ref, mod_ref, bias_ref, out_ref):
+    count, share = here_ref.shape[0] // 2, here_ref.shape[1]
+    even = lax.axis_index("wt") % 2 == 0
+    for n in range(4):
+        lanes = slice(n * share, (n + 1) * share)
+        here, there = quarters(here_ref, n // 2 * count, count), quarters(there_ref, n // 2 * count, count)
+        branch = jnp.where(even == (n % 2 == 0), here, there) + bias_ref[:, lanes]
+        out_ref[0, :, lanes] = (tokens_ref[0, :, lanes].astype(jnp.float32) + mod_ref[2, :, lanes] * branch).astype(out_ref.dtype)
+
+
+def small(kernel, outs, *args, beside=0):
+    return pl.pallas_call(
+        kernel,
+        out_shape=outs,
+        compiler_params=pltpu.CompilerParams(vmem_limit_bytes=4 * MIB),
+        cost_estimate=pl.CostEstimate(flops=400 * beside, bytes_accessed=beside, transcendentals=beside // 100) if beside else None,
+        name=kernel.__name__,
+    )(*args)
+
+
+def pick_lanes(blocks, lanes):
+    return (
+        lax.broadcasted_iota(jnp.int32, (blocks, lanes), 1) // BLOCK
+        == lax.broadcasted_iota(jnp.int32, (blocks, lanes), 0)
+    ).astype(jnp.bfloat16)
+
+
+def prune_kernel(mask_dim, mask_ref, weight_ref, out_ref, lanes):
+    lanes[...] = lax.dot_general(
+        mask_ref[...].astype(jnp.bfloat16),
+        pick_lanes(mask_ref.shape[mask_dim], out_ref.shape[1]),
+        (((mask_dim,), (0,)), ((), ())),
+        preferred_element_type=jnp.float32,
+    )
+
+    def body(b, _):
+        rows = pl.ds(pl.multiple_of(b * BLOCK, BLOCK), BLOCK)
+        out_ref[rows, :] = weight_ref[rows, :] * lanes[pl.ds(b, 1), :].astype(jnp.bfloat16)
+        return 0
+
+    lax.fori_loop(0, out_ref.shape[0] // BLOCK, body, 0)
+
+
+def prune(weight, mask, turned):
+    size = 2 * weight.size
+    return pl.pallas_call(
+        functools.partial(prune_kernel, 0 if turned else 1),
+        out_shape=jax.ShapeDtypeStruct(weight.shape, jnp.bfloat16),
+        scratch_shapes=[pltpu.VMEM((weight.shape[0] // BLOCK, weight.shape[1]), jnp.float32)],
+        compiler_params=pltpu.CompilerParams(vmem_limit_bytes=14 * MIB),
+        cost_estimate=pl.CostEstimate(flops=size, bytes_accessed=2 * size, transcendentals=0),
+        name="prune",
+    )(mask.T if turned else mask, weight)
+
+
+def in_kernel(share, a_ref, b_ref, w_ref, keep_ref, send_ref):
+    x = jnp.concatenate([a_ref[...], b_ref[...]], axis=0)
+    rows = x.shape[0]
+    for n in range(keep_ref.shape[1] // share):
+        lanes = slice(n * share, (n + 1) * share)
+        weight = w_ref[n] if len(w_ref.shape) == 3 else w_ref[:, lanes]
+        out = jnp.dot(x, weight, preferred_element_type=jnp.float32)
+        keep_ref[:, lanes] = jnp.concatenate([out[r : r + 8] for r in range(0, rows, 16)], axis=0)
+        send_ref[:, lanes] = jnp.concatenate([out[r + 8 : r + 16] for r in range(0, rows, 16)], axis=0).astype(jnp.bfloat16)
+
+
+def in_products(near, far, weight):
+    half, depth = near.shape
+    rows = 2 * half
+    width = weight.size // depth
+    return pl.pallas_call(
+        functools.partial(in_kernel, depth),
+        out_shape=[
+            jax.ShapeDtypeStruct((half, width), jnp.float32),
+            jax.ShapeDtypeStruct((half, width), jnp.bfloat16),
+        ],
+        compiler_params=pltpu.CompilerParams(vmem_limit_bytes=12 * MIB),
+        cost_estimate=pl.CostEstimate(
+            flops=2 * rows * weight.size, bytes_accessed=2 * weight.size, transcendentals=0
+        ),
+        name="in_products",
+    )(near, far, weight)
+
+
+def attend_kernel(images, part, own_ref, other_ref, bias_ref, gains_ref, out_ref):
+    rows, share = out_ref.shape
+    heads = share // HEAD
+
+    def stacked(which):
+        lanes = slice(which * share, (which + 1) * share)
+        flat = own_ref[:, lanes] + other_ref[:, lanes].astype(jnp.float32)
+        flat = (flat + bias_ref[which : which + 1, :]).astype(jnp.bfloat16)
+        return jnp.concatenate([flat[:, h * HEAD : (h + 1) * HEAD] for h in range(heads)], axis=0)
+
+    def normed(which):
+        wide = stacked(which).astype(jnp.float32)
+        scale = lax.rsqrt(jnp.mean(wide * wide, axis=-1, keepdims=True) + 1e-06)
+        return (wide * scale * gains_ref[which : which + 1, :]).astype(jnp.bfloat16)
+
+    queries, keys, values = normed(0), normed(1), stacked(2)
+    scores = lax.dot_general(
+        queries, keys, (((1,), (1,)), ((), ())), preferred_element_type=jnp.float32
+    ) * (1.0 / math.sqrt(HEAD))
+    size = heads * rows
+
+    def group(dim):
+        place = lax.broadcasted_iota(jnp.int32, (size, size), dim)
+        return place // rows * images + place // part % images
+
+    same = group(0) == group(1)
+    weights = jnp.where(same, jnp.exp(jnp.where(same, scores, 0.0)), 0.0)
+    denoms = jnp.sum(weights, axis=-1, keepdims=True)
+    summed = jnp.dot(weights.astype(jnp.bfloat16), values, preferred_element_type=jnp.float32)
+    attended = (summed / denoms).astype(jnp.bfloat16)
+    for h in range(heads):
+        out_ref[:, h * HEAD : (h + 1) * HEAD] = attended[h * rows : (h + 1) * rows]
+
+
+def attention(images, part, own, other, bias, gains):
+    return pl.pallas_call(
+        functools.partial(attend_kernel, images, part),
+        out_shape=jax.ShapeDtypeStruct((own.shape[0], bias.shape[1]), jnp.bfloat16),
+        compiler_params=pltpu.CompilerParams(vmem_limit_bytes=8 * MIB),
+        name="attention",
+    )(own, other, bias, gains)
+
+
+def hidden_kernel(own_ref, other_ref, bias_ref, out_ref):
+    step = 6 * HEAD
+    for start in range(0, out_ref.shape[1], step):
+        lanes = slice(start, start + step)
+        v = own_ref[:, lanes] + other_ref[:, lanes].astype(jnp.float32) + bias_ref[:, lanes]
+        cubic = math.sqrt(2.0 / math.pi) * (v + 0.044715 * (v * v * v))
+        out_ref[:, lanes] = (0.5 * v * (1.0 + jnp.tanh(cubic))).astype(jnp.bfloat16)
+
+
+def activate(own, other, bias):
+    return pl.pallas_call(
+        hidden_kernel,
+        out_shape=jax.ShapeDtypeStruct(own.shape, jnp.bfloat16),
+        compiler_params=pltpu.CompilerParams(vmem_limit_bytes=8 * MIB),
+        name="hidden",
+    )(own, other, bias.reshape(1, -1))
+
+
+def out_kernel(a_mine, a_theirs, h_mine, h_theirs, proj_ref, down_ref, keep_ref, send_ref):
+    attended = jnp.concatenate([a_mine[...], a_theirs[...]], axis=0)
+    hidden = jnp.concatenate([h_mine[...], h_theirs[...]], axis=0)
+    total = jnp.dot(attended, proj_ref[...], preferred_element_type=jnp.float32)
+    total += jnp.dot(hidden, down_ref[...], preferred_element_type=jnp.float32)
+    part = total.shape[0] // 4
+    keep_ref[...] = jnp.concatenate([total[:part], total[2 * part : 3 * part]], axis=0)
+    send_ref[...] = jnp.concatenate([total[part : 2 * part], total[3 * part :]], axis=0).astype(jnp.bfloat16)
+
+
+def out_products(mine, theirs, hidden, hidden_theirs, proj, down):
+    half, width = mine.shape[0], proj.shape[1]
+    size = proj.size + down.size
+    return pl.pallas_call(
+        out_kernel,
+        out_shape=[
+            jax.ShapeDtypeStruct((half, width), jnp.float32),
+            jax.ShapeDtypeStruct((half, width), jnp.bfloat16),
+        ],
+        compiler_params=pltpu.CompilerParams(vmem_limit_bytes=12 * MIB),
+        cost_estimate=pl.CostEstimate(flops=4 * half * size, bytes_accessed=2 * size, transcendentals=0),
+        name="out_products",
+    )(mine, theirs, hidden, hidden_theirs, proj, down)
+
+
+def swap(values, axis, bit):
+    count = lax.axis_size(axis)
+    return lax.ppermute(values, axis, [(i, i ^ bit) for i in range(count)])
+
+
+def fixed_shards(
+    tokens,
+    modulation,
+    qkv_weight,
+    qkv_bias,
+    norm_gains,
+    up_weight,
+    up_mask,
+    up_bias,
+    proj_weight,
+    down_weight,
+    down_mask,
+    out_bias,
+):
+    count, features = tokens.shape[1:]
+    share = features // 4
+    bf16, f32 = jnp.bfloat16, jnp.float32
+
+    def rows_of(n, kind):
+        return jax.ShapeDtypeStruct((n * count, share), kind)
+
+    kept, given = enter(tokens, modulation)
+    mine, given = small(part_kernel, [rows_of(2, bf16)] * 2, kept, swap(given, "wt", 1), beside=BESIDE)
+    near = small(near_kernel, rows_of(4, bf16), mine, swap(given, "wt", 2), beside=BESIDE)
+    up_pruned = prune(up_weight, up_mask, False)
+    near, up_pruned = lax.optimization_barrier((near, up_pruned))
+    near = jnp.concatenate([near, swap(near, "seq", 2)], axis=0)
+    far = swap(near, "seq", 1)
+
+    kept, given = in_products(near, far, qkv_weight.transpose(1, 0, 2))
+    near, given = lax.optimization_barrier((near, given))
+    up_kept, up_given = in_products(near, far, up_pruned)
+
+    def reduced(kept, given):
+        total = kept + swap(given, "wt", 1).astype(jnp.float32)
+        return total, swap(total.astype(jnp.bfloat16), "wt", 2)
+
+    qkv_pair, up_pair = reduced(kept, given), reduced(up_kept, up_given)
+    down_pruned = prune(down_weight, down_mask, True)
+    qkv_pair, up_pair, down_pruned = lax.optimization_barrier((qkv_pair, up_pair, down_pruned))
+    attended = attention(2, count, *qkv_pair, qkv_bias, norm_gains)
+    hidden = activate(*up_pair, up_bias)
+    kept, given = out_products(
+        attended, swap(attended, "wt", 1), hidden, swap(hidden, "wt", 1), proj_weight, down_pruned
+    )
+    kept, given = small(fold_kernel, [rows_of(4, f32), rows_of(4, bf16)], kept, swap(given, "seq", 1))
+    mine, given = small(divide_kernel, [rows_of(2, f32)] * 2, kept, swap(given, "seq", 2))
+    here, given = small(join_kernel, [rows_of(2, f32)] * 2, mine, swap(given, "wt", 2))
+    there = swap(given, "wt", 1)
+    out = jax.ShapeDtypeStruct(tokens.shape, tokens.dtype)
+    return small(leave_kernel, out, here, there, tokens, modulation.transpose(1, 0, 2), out_bias.reshape(1, -1))
+
+
 def solution(mesh):
+    seq, wt = mesh.shape["seq"], mesh.shape["wt"]
+
+    def shards(*args):
+        share = args[2].shape[2]
+        whole_heads = share % HEAD == 0 and share == args[8].shape[1] and args[5].shape[1] % share == 0
+        fits = whole_heads and wt == 4 and seq == 4 and args[0].shape[1] == 4
+        return (fixed_shards if fits else gathered_shards)(*args)
+
     return jax.shard_map(
         shards,
         mesh=mesh,

time: 449 us -> 48.7 us (0.11)
  waiting for transfers between devices: 299 us -> 22.1 us
  local copies, waits for them, and re-layouts: 50 us -> 1.56 us
  matrix products: 29.1 us -> 0 us
  blocking collectives: 28.7 us -> 0 us
  other arithmetic: 18.4 us -> 0.07 us
  between operations: 14 us -> 0.18 us
  starting transfers between devices: 8.37 us -> 18.4 us
  Pallas kernels: 0 us -> 6.21 us
    all_gather x4 -> x0, waiting for transfers between devices: 254 us -> none  [the longest x1 121 us: shards(): lax.all_gather(up_local, 'wt', axis=0, tiled=True)]
    unnamed x6 -> x0, waiting for transfers between devices: 34.5 us -> none
    dot_general x5 -> x0, matrix products: 29.1 us -> none  [the longest x1 16.2 us: shards(): jnp.dot(hidden, down_full, preferred_element_type=jnp.float32)]
    all_gather x2 -> x0, blocking collectives: 28.7 us -> none  [the longest x1 15 us: shards(): gathered = lax.all_gather(shaped, 'seq', axis=0, tiled=True)]
    convert_element_type x2 -> x0, local copies, waits for them, and re-layouts: 25.9 us -> none  [masked(): return weight * expanded.reshape(weight.shape).astype(jnp.bfloat16)]
    ppermute x0 -> x14, waiting for transfers between devices: none -> 22.1 us  [swap(): return lax.ppermute(values, axis, [(i, i ^ bit) for i in range(count)])]
    ppermute x0 -> x14, starting transfers between devices: none -> 18.4 us  [swap(): return lax.ppermute(values, axis, [(i, i ^ bit) for i in range(count)])]
    mul x2 -> x0, other arithmetic: 16 us -> none  [masked(): return weight * expanded.reshape(weight.shape).astype(jnp.bfloat16)]
  transfers between devices with their start and end apart: 7 -> 14, of which waited for: 6 -> 11; matrix products, arithmetic and copies ran while one was open for 16% -> 0% of each run, Pallas kernels for 0% -> 5%
where the time goes in v2:
time: 48.7 us; the launch traced here: 48.5 us
  waiting for transfers between devices  22.1 us (45%)
  starting transfers between devices  18.4 us (38%)
  Pallas kernels  6.21 us (13%)
  local copies, waits for them, and re-layouts  1.56 us (3%)
    ppermute x14, waiting for transfers between devices, swap(): return lax.ppermute(values, axis, [(i, i ^ bit) for i in range(count)])  22.1 us
    ppermute x14, starting transfers between devices, swap(): return lax.ppermute(values, axis, [(i, i ^ bit) for i in range(count)])  18.4 us
    pallas_call x2, Pallas kernels, prune(): pl.pallas_call(functools.partial(prune_kernel, 0 if turned else 1), out_s...  1.74 us
    pallas_call x2, Pallas kernels, in_products(): pl.pallas_call(functools.partial(in_kernel, depth), out_shape=[jax.ShapeD...  1.69 us
    unnamed x27, local copies, waits for them, and re-layouts  1.56 us
    pallas_call x1, Pallas kernels, out_products(): pl.pallas_call(out_kernel, out_shape=[jax.ShapeDtypeStruct((half, width),...  1.15 us
  transfers between devices with their start and end apart: 14, of which 11 were waited for; matrix products, arithmetic and copies ran while one was open for 0% of the time, Pallas kernels for 5%

profile of v2, /device:TPU:0, one launch (start us, length us, event | category | flops | bytes accessed | tf_op | source)
XLA Modules:
  0.0 48.5 jit_solution(1077884522663916508)
XLA Ops:
  0.0 0.8 %copy-done.3 = f32[1,3,3072]{2,0,1:T(1,128)S(1)} copy-done((f32[1,3,3072]{2,0,1:T(1,128)S(1)}, f32[1,3,3072]{2,0,1:T(1,128)}, u32[]{:S(2)}) %copy-start.3) | copy-done | bytes 36888
  0.8 0.7 %copy-done.4 = bf16[1,4,3072]{2,1,0:T(4,128)(2,1)S(1)} copy-done((bf16[1,4,3072]{2,1,0:T(4,128)(2,1)S(1)}, bf16[1,4,3072]{2,1,0:T(4,128)(2,1)}, u32[]{:S(2)}) %copy-start.4) | copy-done | bytes 24600
  1.5 0.3 enter.1
  1.8 0.5 %collective-permute-start = (bf16[4,1536]{1,0:T(4,128)(2,1)S(1)}, bf16[4,1536]{1,0:T(4,128)(2,1)S(1)}, u32[]{:S(2)}, u32[]{:S(2)}) collective-permute-start(bf16[4,1536]{1,0:T(4,128)(2,1)S(1)} %get-tuple-element.31), channel_id=1, source_target_pairs={{0,1},{1,0},{2,3},{3,2},{4,5},{5,4},{6,7},{7,6},{8,9},{9,8},{10,11... | collective-permute-start | bytes 36872 | tf_op jit(solution)/shard_map/ppermute | solution.py:377
  2.3 0.8 %collective-permute-done.got_ref = bf16[4,1536]{1,0:T(4,128)(2,1)S(1)} collective-permute-done((bf16[4,1536]{1,0:T(4,128)(2,1)S(1)}, bf16[4,1536]{1,0:T(4,128)(2,1)S(1)}, u32[]{:S(2)}, u32[]{:S(2)}) %collective-permute-start) | collective-permute-done | bytes 12320 | tf_op jit(solution)/shard_map/ppermute | solution.py:377
  3.2 2.9 %collective-permute-start.1 = (bf16[8,768]{1,0:T(8,128)(2,1)S(1)}, bf16[8,768]{1,0:T(8,128)(2,1)S(1)}, u32[]{:S(2)}, u32[]{:S(2)}) collective-permute-start(bf16[8,768]{1,0:T(8,128)(2,1)S(1)} %get-tuple-element.33), channel_id=1, source_target_pairs={{0,2},{1,3},{2,0},{3,1},{4,6},{5,7},{6,4},{7,5},{8,10},{9,11},{10,... | collective-permute-start | bytes 36872 | tf_op jit(solution)/shard_map/ppermute | solution.py:377
  6.1 0.7 %prune.2.w_ref = bf16[768,3072]{1,0:T(8,128)(2,1)S(1)} custom-call(s32[12,48]{1,0:T(8,128)S(1)} %copy-done.8, bf16[768,3072]{1,0:T(8,128)(2,1)S(1)} %copy-done), custom_call_target="tpu_custom_call" | custom-call | flops 4718592 | bytes 9437184 | tf_op jit(solution)/shard_map/prune/pallas_call | solution.py:250
  6.8 1.0 %collective-permute-done.1.theirs_ref = bf16[8,768]{1,0:T(8,128)(2,1)S(1)} collective-permute-done((bf16[8,768]{1,0:T(8,128)(2,1)S(1)}, bf16[8,768]{1,0:T(8,128)(2,1)S(1)}, u32[]{:S(2)}, u32[]{:S(2)}) %collective-permute-start.1) | collective-permute-done | bytes 12320 | tf_op jit(solution)/shard_map/ppermute | solution.py:377
  7.8 3.2 %collective-permute-start.2 = (bf16[16,768]{1,0:T(8,128)(2,1)S(1)}, bf16[16,768]{1,0:T(8,128)(2,1)S(1)}, u32[]{:S(2)}, u32[]{:S(2)}) collective-permute-start(bf16[16,768]{1,0:T(8,128)(2,1)S(1)} %near_kernel.1), channel_id=1, source_target_pairs={{0,8},{4,12},{8,0},{12,4},{1,9},{5,13},{9,1},{13,5},{2,10},{6,14},... | collective-permute-start | bytes 73736 | tf_op jit(solution)/shard_map/ppermute | solution.py:377
  11.0 1.9 %collective-permute-done.2 = bf16[16,768]{1,0:T(8,128)(2,1)S(1)} collective-permute-done((bf16[16,768]{1,0:T(8,128)(2,1)S(1)}, bf16[16,768]{1,0:T(8,128)(2,1)S(1)}, u32[]{:S(2)}, u32[]{:S(2)}) %collective-permute-start.2) | collective-permute-done | bytes 24608 | tf_op jit(solution)/shard_map/ppermute | solution.py:377
  12.9 1.8 %collective-permute-start.3 = (bf16[32,768]{1,0:T(8,128)(2,1)S(1)}, bf16[32,768]{1,0:T(8,128)(2,1)S(1)}, u32[]{:S(2)}, u32[]{:S(2)}) collective-permute-start(bf16[32,768]{1,0:T(8,128)(2,1)S(1)} %constant_dynamic-update-slice_fusion.a_ref), channel_id=1, source_target_pairs={{0,4},{4,0},{8,12},{12,8},{1,5},{5,1},{9,13},{13,9},{2,6},{6,2},{1... | collective-permute-start | bytes 147464 | tf_op jit(solution)/shard_map/ppermute | solution.py:377
  14.7 2.3 %collective-permute-done.3.b_ref = bf16[32,768]{1,0:T(8,128)(2,1)S(1)} collective-permute-done((bf16[32,768]{1,0:T(8,128)(2,1)S(1)}, bf16[32,768]{1,0:T(8,128)(2,1)S(1)}, u32[]{:S(2)}, u32[]{:S(2)}) %collective-permute-start.3) | collective-permute-done | bytes 49184 | tf_op jit(solution)/shard_map/ppermute | solution.py:377
  17.0 0.7 %in_products.2 = (f32[32,2304]{1,0:T(8,128)S(1)}, bf16[32,2304]{1,0:T(8,128)(2,1)S(1)}) custom-call(bf16[32,768]{1,0:T(8,128)(2,1)S(1)} %constant_dynamic-update-slice_fusion.a_ref, bf16[32,768]{1,0:T(8,128)(2,1)S(1)} %collective-permute-done.3.b_ref, bf16[3,768,768]{2,1,0:T(8,128)(2,1)S(1)} %bitcast.7), custom_call_target="tpu_custom_call" | custom-call | flops 226492416 | bytes 3538944 | tf_op jit(solution)/shard_map/in_products/pallas_call | solution.py:275
  17.7 1.0 %in_products.3 = (f32[32,3072]{1,0:T(8,128)S(1)}, bf16[32,3072]{1,0:T(8,128)(2,1)S(1)}) custom-call(bf16[32,768]{1,0:T(8,128)(2,1)S(1)} %constant_dynamic-update-slice_fusion.a_ref, bf16[32,768]{1,0:T(8,128)(2,1)S(1)} %collective-permute-done.3.b_ref, bf16[768,3072]{1,0:T(8,128)(2,1)S(1)} %prune.2.w_ref), custom_call_target="tpu_custom_call" | custom-call | flops 301989888 | bytes 4718592 | tf_op jit(solution)/shard_map/in_products/pallas_call | solution.py:275
  18.8 0.5 %collective-permute-start.4 = (bf16[32,2304]{1,0:T(8,128)(2,1)S(1)}, bf16[32,2304]{1,0:T(8,128)(2,1)S(1)}, u32[]{:S(2)}, u32[]{:S(2)}) collective-permute-start(bf16[32,2304]{1,0:T(8,128)(2,1)S(1)} %get-tuple-element.37), channel_id=1, source_target_pairs={{0,1},{1,0},{2,3},{3,2},{4,5},{5,4},{6,7},{7,6},{8,9},{9,8},{10,11... | collective-permute-start | bytes 442376 | tf_op jit(solution)/shard_map/ppermute | solution.py:377
  19.3 0.9 %collective-permute-done.6 = bf16[32,3072]{1,0:T(8,128)(2,1)S(1)} collective-permute-done((bf16[32,3072]{1,0:T(8,128)(2,1)S(1)}, bf16[32,3072]{1,0:T(8,128)(2,1)S(1)}, u32[]{:S(2)}, u32[]{:S(2)}) %collective-permute-start.6) | collective-permute-done | bytes 196640 | tf_op jit(solution)/shard_map/ppermute | solution.py:377
  20.2 1.8 %collective-permute-start.7 = (bf16[32,3072]{1,0:T(8,128)(2,1)S(1)}, bf16[32,3072]{1,0:T(8,128)(2,1)S(1)}, u32[]{:S(2)}, u32[]{:S(2)}) collective-permute-start(bf16[32,3072]{1,0:T(8,128)(2,1)S(1)} %get-tuple-element.55), channel_id=1, source_target_pairs={{0,2},{1,3},{2,0},{3,1},{4,6},{5,7},{6,4},{7,5},{8,10},{9,11},{10,... | collective-permute-start | bytes 589832 | tf_op jit(solution)/shard_map/ppermute | solution.py:377
  22.1 0.4 collective-permute-start.5
  22.5 1.1 %prune.3.down_ref = bf16[3072,768]{1,0:T(8,128)(2,1)S(1)} custom-call(s32[12,48]{1,0:T(8,128)S(1)} %bitcast.12, bf16[3072,768]{1,0:T(8,128)(2,1)S(1)} %bitcast.6), custom_call_target="tpu_custom_call" | custom-call | flops 4718592 | bytes 9437184 | tf_op jit(solution)/shard_map/prune/pallas_call | solution.py:250
  23.6 6.8 %collective-permute-done.5.other_ref = bf16[32,2304]{1,0:T(8,128)(2,1)S(1)} collective-permute-done((bf16[32,2304]{1,0:T(8,128)(2,1)S(1)}, bf16[32,2304]{1,0:T(8,128)(2,1)S(1)}, u32[]{:S(2)}, u32[]{:S(2)}) %collective-permute-start.5) | collective-permute-done | bytes 147488 | tf_op jit(solution)/shard_map/ppermute | solution.py:377
  30.7 0.4 attention.1.a_mine
  31.1 0.5 %collective-permute-start.8 = (bf16[32,768]{1,0:T(8,128)(2,1)S(1)}, bf16[32,768]{1,0:T(8,128)(2,1)S(1)}, u32[]{:S(2)}, u32[]{:S(2)}) collective-permute-start(bf16[32,768]{1,0:T(8,128)(2,1)S(1)} %attention.1.a_mine), channel_id=1, source_target_pairs={{0,1},{1,0},{2,3},{3,2},{4,5},{5,4},{6,7},{7,6},{8,9},{9,8},{10,11... | collective-permute-start | bytes 147464 | tf_op jit(solution)/shard_map/ppermute | solution.py:377
  31.7 0.9 %collective-permute-done.8.a_theirs = bf16[32,768]{1,0:T(8,128)(2,1)S(1)} collective-permute-done((bf16[32,768]{1,0:T(8,128)(2,1)S(1)}, bf16[32,768]{1,0:T(8,128)(2,1)S(1)}, u32[]{:S(2)}, u32[]{:S(2)}) %collective-permute-start.8) | collective-permute-done | bytes 49184 | tf_op jit(solution)/shard_map/ppermute | solution.py:377
  32.6 1.1 %out_products.1 = (f32[32,768]{1,0:T(8,128)S(1)}, bf16[32,768]{1,0:T(8,128)(2,1)S(1)}) custom-call(bf16[32,768]{1,0:T(8,128)(2,1)S(1)} %attention.1.a_mine, bf16[32,768]{1,0:T(8,128)(2,1)S(1)} %collective-permute-done.8.a_theirs, bf16[32,3072]{1,0:T(8,128)(2,1)S(1)} %hidden.1.h_mine, bf16[32,3072]{1,0:T(8,128)(2,1)S(1)} %collective-permute-done.9.h_theirs, ...), custom_call_target="tpu_custom_call" | custom-call | flops 377487360 | bytes 5898240 | tf_op jit(solution)/shard_map/out_products/pallas_call | solution.py:363
  33.7 1.9 %collective-permute-start.10 = (bf16[32,768]{1,0:T(8,128)(2,1)S(1)}, bf16[32,768]{1,0:T(8,128)(2,1)S(1)}, u32[]{:S(2)}, u32[]{:S(2)}) collective-permute-start(bf16[32,768]{1,0:T(8,128)(2,1)S(1)} %get-tuple-element.48), channel_id=1, source_target_pairs={{0,4},{4,0},{8,12},{12,8},{1,5},{5,1},{9,13},{13,9},{2,6},{6,2},{1... | collective-permute-start | bytes 147464 | tf_op jit(solution)/shard_map/ppermute | solution.py:377
  35.6 2.3 %collective-permute-done.10.got_ref = bf16[32,768]{1,0:T(8,128)(2,1)S(1)} collective-permute-done((bf16[32,768]{1,0:T(8,128)(2,1)S(1)}, bf16[32,768]{1,0:T(8,128)(2,1)S(1)}, u32[]{:S(2)}, u32[]{:S(2)}) %collective-permute-start.10) | collective-permute-done | bytes 49184 | tf_op jit(solution)/shard_map/ppermute | solution.py:377
  37.9 2.9 %collective-permute-start.11 = (bf16[16,768]{1,0:T(8,128)(2,1)S(1)}, bf16[16,768]{1,0:T(8,128)(2,1)S(1)}, u32[]{:S(2)}, u32[]{:S(2)}) collective-permute-start(bf16[16,768]{1,0:T(8,128)(2,1)S(1)} %get-tuple-element.50), channel_id=1, source_target_pairs={{0,8},{4,12},{8,0},{12,4},{1,9},{5,13},{9,1},{13,5},{2,10},{6,14},... | collective-permute-start | bytes 73736 | tf_op jit(solution)/shard_map/ppermute | solution.py:377
  40.8 1.9 %collective-permute-done.11.got_ref = bf16[16,768]{1,0:T(8,128)(2,1)S(1)} collective-permute-done((bf16[16,768]{1,0:T(8,128)(2,1)S(1)}, bf16[16,768]{1,0:T(8,128)(2,1)S(1)}, u32[]{:S(2)}, u32[]{:S(2)}) %collective-permute-start.11) | collective-permute-done | bytes 24608 | tf_op jit(solution)/shard_map/ppermute | solution.py:377
  42.7 1.8 %collective-permute-start.12 = (f32[8,768]{1,0:T(8,128)S(1)}, f32[8,768]{1,0:T(8,128)S(1)}, u32[]{:S(2)}, u32[]{:S(2)}) collective-permute-start(f32[8,768]{1,0:T(8,128)S(1)} %get-tuple-element.52), channel_id=1, source_target_pairs={{0,2},{1,3},{2,0},{3,1},{4,6},{5,7},{6,4},{7,5},{8,10},{9,11},{10,... | collective-permute-start | bytes 73736 | tf_op jit(solution)/shard_map/ppermute | solution.py:377
  44.5 2.1 %collective-permute-done.12.theirs_ref = f32[8,768]{1,0:T(8,128)S(1)} collective-permute-done((f32[8,768]{1,0:T(8,128)S(1)}, f32[8,768]{1,0:T(8,128)S(1)}, u32[]{:S(2)}, u32[]{:S(2)}) %collective-permute-start.12) | collective-permute-done | bytes 24608 | tf_op jit(solution)/shard_map/ppermute | solution.py:377
  46.7 1.2 %collective-permute-done.13.there_ref = f32[8,768]{1,0:T(8,128)S(1)} collective-permute-done((f32[8,768]{1,0:T(8,128)S(1)}, f32[8,768]{1,0:T(8,128)S(1)}, u32[]{:S(2)}, u32[]{:S(2)}) %collective-permute-start.13) | collective-permute-done | bytes 24608 | tf_op jit(solution)/shard_map/ppermute | solution.py:377
  47.9 0.6 %leave_kernel.1 = bf16[1,4,3072]{2,1,0:T(4,128)(2,1)} custom-call(f32[8,768]{1,0:T(8,128)S(1)} %get-tuple-element.53.here_ref, f32[8,768]{1,0:T(8,128)S(1)} %collective-permute-done.13.there_ref, bf16[1,4,3072]{2,1,0:T(4,128)(2,1)S(1)} %copy-done.4, f32[3,1,3072]{2,1,0:T(1,128)S(1)} %bitcast.9, f32[1,3072]{1,0:T(1,128)S(1)} %bitcast.10), custom_call_target="tpu_custom_call" | custom-call | tf_op jit(solution)/shard_map/leave_kernel/pallas_call | solution.py:216
  (41 shorter events, 0.6 us)
Async XLA Ops:
  0.0 0.8 %copy-start.3 = (f32[1,3,3072]{2,0,1:T(1,128)S(1)}, f32[1,3,3072]{2,0,1:T(1,128)}, u32[]{:S(2)}) copy-start(f32[1,3,3072]{2,0,1:T(1,128)} %param.13) | copy-start | bytes 110596
  0.8 0.7 %copy-start.4 = (bf16[1,4,3072]{2,1,0:T(4,128)(2,1)S(1)}, bf16[1,4,3072]{2,1,0:T(4,128)(2,1)}, u32[]{:S(2)}) copy-start(bf16[1,4,3072]{2,1,0:T(4,128)(2,1)} %tokens_ref.1) | copy-start | bytes 73732
  1.8 1.4 %collective-permute-start = (bf16[4,1536]{1,0:T(4,128)(2,1)S(1)}, bf16[4,1536]{1,0:T(4,128)(2,1)S(1)}, u32[]{:S(2)}, u32[]{:S(2)}) collective-permute-start(bf16[4,1536]{1,0:T(4,128)(2,1)S(1)} %get-tuple-element.31), channel_id=1, source_target_pairs={{0,1},{1,0},{2,3},{3,2},{4,5},{5,4},{6,7},{7,6},{8,9},{9,8},{10,11... | collective-permute-start | bytes 36872 | tf_op jit(solution)/shard_map/ppermute | solution.py:377
  3.2 2.9 %copy-start = (bf16[768,3072]{1,0:T(8,128)(2,1)S(1)}, bf16[768,3072]{1,0:T(8,128)(2,1)}, u32[]{:S(2)}) copy-start(bf16[768,3072]{1,0:T(8,128)(2,1)} %weight_ref.2) | copy-start | bytes 14155780
  3.2 2.9 %copy-start.8 = (s32[12,48]{1,0:T(8,128)S(1)}, s32[12,48]{1,0:T(8,128)}, u32[]{:S(2)}) copy-start(s32[12,48]{1,0:T(8,128)} %mask_ref.1) | copy-start | bytes 6916
  3.2 4.6 %collective-permute-start.1 = (bf16[8,768]{1,0:T(8,128)(2,1)S(1)}, bf16[8,768]{1,0:T(8,128)(2,1)S(1)}, u32[]{:S(2)}, u32[]{:S(2)}) collective-permute-start(bf16[8,768]{1,0:T(8,128)(2,1)S(1)} %get-tuple-element.33), channel_id=1, source_target_pairs={{0,2},{1,3},{2,0},{3,1},{4,6},{5,7},{6,4},{7,5},{8,10},{9,11},{10,... | collective-permute-start | bytes 36872 | tf_op jit(solution)/shard_map/ppermute | solution.py:377
  6.1 16.3 %slice-start = ((s8[4718592]{0:T(1024)(128)(4,1)}), s8[4194304]{0:T(1024)(128)(4,1)S(1)}, s32[]{:S(2)}) async-start(s8[4718592]{0:T(1024)(128)(4,1)} %bitcast.5), calls=%async_computation | async-start | bytes 8388608
  7.8 9.2 %copy-start.1 = (bf16[768,3,768]{2,0,1:T(8,128)(2,1)S(1)}, bf16[768,3,768]{2,0,1:T(8,128)(2,1)}, u32[]{:S(2)}) copy-start(bf16[768,3,768]{2,0,1:T(8,128)(2,1)} %param.14) | copy-start | bytes 10616836
  7.8 14.7 %slice-start.1 = ((s8[4718592]{0:T(1024)(128)(4,1)}), s8[524288]{0:T(1024)(128)(4,1)S(1)}, s32[]{:S(2)}) async-start(s8[4718592]{0:T(1024)(128)(4,1)} %bitcast.5), calls=%async_computation.1 | async-start | bytes 1048576
  7.8 5.1 %collective-permute-start.2 = (bf16[16,768]{1,0:T(8,128)(2,1)S(1)}, bf16[16,768]{1,0:T(8,128)(2,1)S(1)}, u32[]{:S(2)}, u32[]{:S(2)}) collective-permute-start(bf16[16,768]{1,0:T(8,128)(2,1)S(1)} %near_kernel.1), channel_id=1, source_target_pairs={{0,8},{4,12},{8,0},{12,4},{1,9},{5,13},{9,1},{13,5},{2,10},{6,14},... | collective-permute-start | bytes 73736 | tf_op jit(solution)/shard_map/ppermute | solution.py:377
  12.9 4.1 %collective-permute-start.3 = (bf16[32,768]{1,0:T(8,128)(2,1)S(1)}, bf16[32,768]{1,0:T(8,128)(2,1)S(1)}, u32[]{:S(2)}, u32[]{:S(2)}) collective-permute-start(bf16[32,768]{1,0:T(8,128)(2,1)S(1)} %constant_dynamic-update-slice_fusion.a_ref), channel_id=1, source_target_pairs={{0,4},{4,0},{8,12},{12,8},{1,5},{5,1},{9,13},{13,9},{2,6},{6,2},{1... | collective-permute-start | bytes 147464 | tf_op jit(solution)/shard_map/ppermute | solution.py:377
  17.0 5.5 %copy-start.9 = (s32[48,12]{0,1:T(8,128)S(1)}, s32[48,12]{0,1:T(8,128)}, u32[]{:S(2)}) copy-start(s32[48,12]{0,1:T(8,128)} %param.22) | copy-start | bytes 6916
  18.7 1.5 %collective-permute-start.6 = (bf16[32,3072]{1,0:T(8,128)(2,1)S(1)}, bf16[32,3072]{1,0:T(8,128)(2,1)S(1)}, u32[]{:S(2)}, u32[]{:S(2)}) collective-permute-start(bf16[32,3072]{1,0:T(8,128)(2,1)S(1)} %get-tuple-element.41), channel_id=1, source_target_pairs={{0,1},{1,0},{2,3},{3,2},{4,5},{5,4},{6,7},{7,6},{8,9},{9,8},{10,11... | collective-permute-start | bytes 589832 | tf_op jit(solution)/shard_map/ppermute | solution.py:377
  18.8 3.3 %collective-permute-start.4 = (bf16[32,2304]{1,0:T(8,128)(2,1)S(1)}, bf16[32,2304]{1,0:T(8,128)(2,1)S(1)}, u32[]{:S(2)}, u32[]{:S(2)}) collective-permute-start(bf16[32,2304]{1,0:T(8,128)(2,1)S(1)} %get-tuple-element.37), channel_id=1, source_target_pairs={{0,1},{1,0},{2,3},{3,2},{4,5},{5,4},{6,7},{7,6},{8,9},{9,8},{10,11... | collective-permute-start | bytes 442376 | tf_op jit(solution)/shard_map/ppermute | solution.py:377
  20.2 10.2 %collective-permute-start.7 = (bf16[32,3072]{1,0:T(8,128)(2,1)S(1)}, bf16[32,3072]{1,0:T(8,128)(2,1)S(1)}, u32[]{:S(2)}, u32[]{:S(2)}) collective-permute-start(bf16[32,3072]{1,0:T(8,128)(2,1)S(1)} %get-tuple-element.55), channel_id=1, source_target_pairs={{0,2},{1,3},{2,0},{3,1},{4,6},{5,7},{6,4},{7,5},{8,10},{9,11},{10,... | collective-permute-start | bytes 589832 | tf_op jit(solution)/shard_map/ppermute | solution.py:377
  22.1 8.3 %collective-permute-start.5 = (bf16[32,2304]{1,0:T(8,128)(2,1)S(1)}, bf16[32,2304]{1,0:T(8,128)(2,1)S(1)}, u32[]{:S(2)}, u32[]{:S(2)}) collective-permute-start(bf16[32,2304]{1,0:T(8,128)(2,1)S(1)} %get-tuple-element.57), channel_id=1, source_target_pairs={{0,2},{1,3},{2,0},{3,1},{4,6},{5,7},{6,4},{7,5},{8,10},{9,11},{10,... | collective-permute-start | bytes 442376 | tf_op jit(solution)/shard_map/ppermute | solution.py:377
  22.4 8.0 %copy-start.6 = (f32[3072]{0:T(1024)S(1)}, f32[3072]{0:T(1024)}, u32[]{:S(2)}) copy-start(f32[3072]{0:T(1024)} %param.19) | copy-start | bytes 36868
  22.5 8.2 %copy-start.7 = (f32[3,768]{1,0:T(4,128)S(1)}, f32[3,768]{1,0:T(4,128)}, u32[]{:S(2)}) copy-start(f32[3,768]{1,0:T(4,128)} %bias_ref.1) | copy-start | bytes 27652
  22.5 8.2 %copy-start.10 = (f32[2,128]{1,0:T(2,128)S(1)}, f32[2,128]{1,0:T(2,128)}, u32[]{:S(2)}) copy-start(f32[2,128]{1,0:T(2,128)} %gains_ref.1) | copy-start | bytes 3076
  22.5 10.1 %copy-start.2 = (bf16[768,768]{1,0:T(8,128)(2,1)S(1)}, bf16[768,768]{1,0:T(8,128)(2,1)}, u32[]{:S(2)}) copy-start(bf16[768,768]{1,0:T(8,128)(2,1)} %proj_ref.1) | copy-start | bytes 3538948
  23.6 24.3 %copy-start.5 = (f32[3072]{0:T(1024)S(1)}, f32[3072]{0:T(1024)}, u32[]{:S(2)}) copy-start(f32[3072]{0:T(1024)} %param.23) | copy-start | bytes 36868
  30.6 2.0 %collective-permute-start.9 = (bf16[32,3072]{1,0:T(8,128)(2,1)S(1)}, bf16[32,3072]{1,0:T(8,128)(2,1)S(1)}, u32[]{:S(2)}, u32[]{:S(2)}) collective-permute-start(bf16[32,3072]{1,0:T(8,128)(2,1)S(1)} %hidden.1.h_mine), channel_id=1, source_target_pairs={{0,1},{1,0},{2,3},{3,2},{4,5},{5,4},{6,7},{7,6},{8,9},{9,8},{10,11... | collective-permute-start | bytes 589832 | tf_op jit(solution)/shard_map/ppermute | solution.py:377
  31.1 1.4 %collective-permute-start.8 = (bf16[32,768]{1,0:T(8,128)(2,1)S(1)}, bf16[32,768]{1,0:T(8,128)(2,1)S(1)}, u32[]{:S(2)}, u32[]{:S(2)}) collective-permute-start(bf16[32,768]{1,0:T(8,128)(2,1)S(1)} %attention.1.a_mine), channel_id=1, source_target_pairs={{0,1},{1,0},{2,3},{3,2},{4,5},{5,4},{6,7},{7,6},{8,9},{9,8},{10,11... | collective-permute-start | bytes 147464 | tf_op jit(solution)/shard_map/ppermute | solution.py:377
  33.7 4.1 %collective-permute-start.10 = (bf16[32,768]{1,0:T(8,128)(2,1)S(1)}, bf16[32,768]{1,0:T(8,128)(2,1)S(1)}, u32[]{:S(2)}, u32[]{:S(2)}) collective-permute-start(bf16[32,768]{1,0:T(8,128)(2,1)S(1)} %get-tuple-element.48), channel_id=1, source_target_pairs={{0,4},{4,0},{8,12},{12,8},{1,5},{5,1},{9,13},{13,9},{2,6},{6,2},{1... | collective-permute-start | bytes 147464 | tf_op jit(solution)/shard_map/ppermute | solution.py:377
  37.9 4.8 %collective-permute-start.11 = (bf16[16,768]{1,0:T(8,128)(2,1)S(1)}, bf16[16,768]{1,0:T(8,128)(2,1)S(1)}, u32[]{:S(2)}, u32[]{:S(2)}) collective-permute-start(bf16[16,768]{1,0:T(8,128)(2,1)S(1)} %get-tuple-element.50), channel_id=1, source_target_pairs={{0,8},{4,12},{8,0},{12,4},{1,9},{5,13},{9,1},{13,5},{2,10},{6,14},... | collective-permute-start | bytes 73736 | tf_op jit(solution)/shard_map/ppermute | solution.py:377
  42.7 3.9 %collective-permute-start.12 = (f32[8,768]{1,0:T(8,128)S(1)}, f32[8,768]{1,0:T(8,128)S(1)}, u32[]{:S(2)}, u32[]{:S(2)}) collective-permute-start(f32[8,768]{1,0:T(8,128)S(1)} %get-tuple-element.52), channel_id=1, source_target_pairs={{0,2},{1,3},{2,0},{3,1},{4,6},{5,7},{6,4},{7,5},{8,10},{9,11},{10,... | collective-permute-start | bytes 73736 | tf_op jit(solution)/shard_map/ppermute | solution.py:377
  46.6 1.3 %collective-permute-start.13 = (f32[8,768]{1,0:T(8,128)S(1)}, f32[8,768]{1,0:T(8,128)S(1)}, u32[]{:S(2)}, u32[]{:S(2)}) collective-permute-start(f32[8,768]{1,0:T(8,128)S(1)} %get-tuple-element.54), channel_id=1, source_target_pairs={{0,1},{1,0},{2,3},{3,2},{4,5},{5,4},{6,7},{7,6},{8,9},{9,8},{10,11... | collective-permute-start | bytes 73736 | tf_op jit(solution)/shard_map/ppermute | solution.py:377

commit v3 on v2

--- a/solution.py
+++ b/solution.py
@@ -12,6 +12,7 @@
 BLOCK = 64
 MIB = 1024 * 1024
 ENTER = 50
+NEAR_FIRST = (0, 2, 1, 3)
 BESIDE = 16 * MIB
 
 
@@ -179,36 +180,11 @@
     out_ref[...] = jnp.concatenate(pieces, axis=0).astype(out_ref.dtype)
 
 
-def fold_kernel(kept_ref, got_ref, keep_ref, send_ref):
-    size = keep_ref.shape[0] // 2
-    total = kept_ref[...] + got_ref[...].astype(jnp.float32)
-    keep_ref[...] = jnp.concatenate([total[:size], total[2 * size : 3 * size]], axis=0)
-    send_ref[...] = jnp.concatenate([total[size : 2 * size], total[3 * size :]], axis=0).astype(send_ref.dtype)
-
-
-def divide_kernel(kept_ref, got_ref, mine_ref, send_ref):
-    count = mine_ref.shape[0] // 2
-    total = kept_ref[...] + got_ref[...].astype(jnp.float32)
-    rows = [total[n * count : (n + 1) * count] for n in range(4)]
-    apart(rows[:2], rows[2:], mine_ref, send_ref)
-
-
-def join_kernel(mine_ref, theirs_ref, here_ref, send_ref):
-    count = mine_ref.shape[0] // 2
-    for start, ref in ((0, here_ref), (count, send_ref)):
-        mine, theirs = quarters(mine_ref, start, count), quarters(theirs_ref, start, count)
-        ref[...] = jnp.concatenate(
-            [jnp.where(on_first(), mine, theirs), jnp.where(on_first(), theirs, mine)], axis=0
-        )
-
-
-def leave_kernel(here_ref, there_ref, tokens_ref, mod_ref, bias_ref, out_ref):
-    count, share = here_ref.shape[0] // 2, here_ref.shape[1]
-    even = lax.axis_index("wt") % 2 == 0
+def leave_kernel(shares_ref, tokens_ref, mod_ref, bias_ref, out_ref):
+    share = shares_ref.shape[2]
     for n in range(4):
         lanes = slice(n * share, (n + 1) * share)
-        here, there = quarters(here_ref, n // 2 * count, count), quarters(there_ref, n // 2 * count, count)
-        branch = jnp.where(even == (n % 2 == 0), here, there) + bias_ref[:, lanes]
+        branch = sum(shares_ref[4 * place + n].astype(jnp.float32) for place in range(4)) + bias_ref[:, lanes]
         out_ref[0, :, lanes] = (tokens_ref[0, :, lanes].astype(jnp.float32) + mod_ref[2, :, lanes] * branch).astype(out_ref.dtype)
 
 
@@ -245,45 +221,70 @@
     lax.fori_loop(0, out_ref.shape[0] // BLOCK, body, 0)
 
 
-def prune(weight, mask, turned):
+def prune(weight, mask, turned, hint=1):
     size = 2 * weight.size
     return pl.pallas_call(
         functools.partial(prune_kernel, 0 if turned else 1),
         out_shape=jax.ShapeDtypeStruct(weight.shape, jnp.bfloat16),
         scratch_shapes=[pltpu.VMEM((weight.shape[0] // BLOCK, weight.shape[1]), jnp.float32)],
         compiler_params=pltpu.CompilerParams(vmem_limit_bytes=14 * MIB),
-        cost_estimate=pl.CostEstimate(flops=size, bytes_accessed=2 * size, transcendentals=0),
+        cost_estimate=pl.CostEstimate(flops=size * hint, bytes_accessed=2 * size * hint, transcendentals=0),
         name="prune",
     )(mask.T if turned else mask, weight)
 
 
-def in_kernel(share, a_ref, b_ref, w_ref, keep_ref, send_ref):
-    x = jnp.concatenate([a_ref[...], b_ref[...]], axis=0)
-    rows = x.shape[0]
-    for n in range(keep_ref.shape[1] // share):
+def in_kernel(count, x_ref, *refs):
+    weights, (keep_ref, send_ref) = refs[:count], refs[count:]
+    rows, share = x_ref.shape
+    x = x_ref[...]
+    tiles = []
+    for ref in weights:
+        if len(ref.shape) == 3:
+            tiles += [(ref, n) for n in range(ref.shape[0])]
+        else:
+            tiles += [(ref, (slice(None), slice(n, n + share))) for n in range(0, ref.shape[1], share)]
+    for n, (ref, place) in enumerate(tiles):
         lanes = slice(n * share, (n + 1) * share)
-        weight = w_ref[n] if len(w_ref.shape) == 3 else w_ref[:, lanes]
-        out = jnp.dot(x, weight, preferred_element_type=jnp.float32)
+        out = jnp.dot(x, ref[place], preferred_element_type=jnp.float32)
         keep_ref[:, lanes] = jnp.concatenate([out[r : r + 8] for r in range(0, rows, 16)], axis=0)
         send_ref[:, lanes] = jnp.concatenate([out[r + 8 : r + 16] for r in range(0, rows, 16)], axis=0).astype(jnp.bfloat16)
 
 
-def in_products(near, far, weight):
-    half, depth = near.shape
-    rows = 2 * half
-    width = weight.size // depth
-    return pl.pallas_call(
-        functools.partial(in_kernel, depth),
+def in_products(x, *weights, hint=1):
+    rows, depth = x.shape
+    size = sum(w.size for w in weights)
+    return pl.pallas_call(
+        functools.partial(in_kernel, len(weights)),
         out_shape=[
-            jax.ShapeDtypeStruct((half, width), jnp.float32),
-            jax.ShapeDtypeStruct((half, width), jnp.bfloat16),
+            jax.ShapeDtypeStruct((rows // 2, size // depth), jnp.float32),
+            jax.ShapeDtypeStruct((rows // 2, size // depth), jnp.bfloat16),
         ],
         compiler_params=pltpu.CompilerParams(vmem_limit_bytes=12 * MIB),
-        cost_estimate=pl.CostEstimate(
-            flops=2 * rows * weight.size, bytes_accessed=2 * weight.size, transcendentals=0
-        ),
+        cost_estimate=pl.CostEstimate(flops=2 * rows * size * hint, bytes_accessed=2 * size * hint, transcendentals=0),
         name="in_products",
-    )(near, far, weight)
+    )(x, *weights)
+
+
+def total_kernel(start, near_kept, near_got, far_kept, far_got, total_ref, send_ref):
+    lanes = slice(start, start + total_ref.shape[1])
+    half = near_kept.shape[0]
+    for rows, kept, got in (
+        (slice(0, half), near_kept[:, lanes], near_got[:, lanes]),
+        (slice(half, 2 * half), far_kept[...], far_got[...]),
+    ):
+        total = kept + got.astype(jnp.float32)
+        total_ref[rows] = total
+        send_ref[rows] = total.astype(jnp.bfloat16)
+
+
+def over_cores(start, near, far):
+    shape = (2 * far[0].shape[0], far[0].shape[1])
+    return pl.pallas_call(
+        functools.partial(total_kernel, start),
+        out_shape=[jax.ShapeDtypeStruct(shape, jnp.float32), jax.ShapeDtypeStruct(shape, jnp.bfloat16)],
+        compiler_params=pltpu.CompilerParams(vmem_limit_bytes=8 * MIB),
+        name="over_cores",
+    )(*near, *far)
 
 
 def attend_kernel(images, part, own_ref, other_ref, bias_ref, gains_ref, out_ref):
@@ -347,25 +348,28 @@
     )(own, other, bias.reshape(1, -1))
 
 
-def out_kernel(a_mine, a_theirs, h_mine, h_theirs, proj_ref, down_ref, keep_ref, send_ref):
+def out_kernel(a_mine, a_theirs, h_mine, h_theirs, proj_ref, down_ref, out_ref):
     attended = jnp.concatenate([a_mine[...], a_theirs[...]], axis=0)
     hidden = jnp.concatenate([h_mine[...], h_theirs[...]], axis=0)
     total = jnp.dot(attended, proj_ref[...], preferred_element_type=jnp.float32)
     total += jnp.dot(hidden, down_ref[...], preferred_element_type=jnp.float32)
-    part = total.shape[0] // 4
-    keep_ref[...] = jnp.concatenate([total[:part], total[2 * part : 3 * part]], axis=0)
-    send_ref[...] = jnp.concatenate([total[part : 2 * part], total[3 * part :]], axis=0).astype(jnp.bfloat16)
-
-
-def out_products(mine, theirs, hidden, hidden_theirs, proj, down):
+    place, core = lax.axis_index("seq"), lax.axis_index("wt") % 2
+    count = out_ref.shape[1]
+    row = 0
+    for other_core in range(2):
+        for step in NEAR_FIRST:
+            for chip in range(2):
+                target = (place ^ step) * 4 + 2 * chip + (core ^ other_core)
+                out_ref[target] = total[row : row + count].astype(out_ref.dtype)
+                row += count
+
+
+def out_products(count, mine, theirs, hidden, hidden_theirs, proj, down):
     half, width = mine.shape[0], proj.shape[1]
     size = proj.size + down.size
     return pl.pallas_call(
         out_kernel,
-        out_shape=[
-            jax.ShapeDtypeStruct((half, width), jnp.float32),
-            jax.ShapeDtypeStruct((half, width), jnp.bfloat16),
-        ],
+        out_shape=jax.ShapeDtypeStruct((2 * half // count, count, width), jnp.bfloat16),
         compiler_params=pltpu.CompilerParams(vmem_limit_bytes=12 * MIB),
         cost_estimate=pl.CostEstimate(flops=4 * half * size, bytes_accessed=2 * size, transcendentals=0),
         name="out_products",
@@ -393,7 +397,7 @@
 ):
     count, features = tokens.shape[1:]
     share = features // 4
-    bf16, f32 = jnp.bfloat16, jnp.float32
+    bf16 = jnp.bfloat16
 
     def rows_of(n, kind):
         return jax.ShapeDtypeStruct((n * count, share), kind)
@@ -406,28 +410,29 @@
     near = jnp.concatenate([near, swap(near, "seq", 2)], axis=0)
     far = swap(near, "seq", 1)
 
-    kept, given = in_products(near, far, qkv_weight.transpose(1, 0, 2))
-    near, given = lax.optimization_barrier((near, given))
-    up_kept, up_given = in_products(near, far, up_pruned)
-
-    def reduced(kept, given):
-        total = kept + swap(given, "wt", 1).astype(jnp.float32)
-        return total, swap(total.astype(jnp.bfloat16), "wt", 2)
-
-    qkv_pair, up_pair = reduced(kept, given), reduced(up_kept, up_given)
-    down_pruned = prune(down_weight, down_mask, True)
-    qkv_pair, up_pair, down_pruned = lax.optimization_barrier((qkv_pair, up_pair, down_pruned))
+    def with_theirs(kept, values):
+        return kept, swap(values, "wt", 1)
+
+    qkv = qkv_weight.transpose(1, 0, 2)
+    kept, given = in_products(near, qkv, up_pruned)
+    given, far = lax.optimization_barrier((given, far))
+    near_sums = with_theirs(kept, given)
+    kept, given = in_products(far, qkv, hint=0)
+    far, given = lax.optimization_barrier((far, given))
+    own, sent = over_cores(0, near_sums, with_theirs(kept, given))
+    qkv_pair = own, swap(sent, "wt", 2)
+    own, sent = over_cores(own.shape[1], near_sums, with_theirs(*in_products(far, up_pruned, hint=0)))
+    up_pair = own, swap(sent, "wt", 2)
+    down_pruned = prune(down_weight, down_mask, True, hint=0)
+    qkv_pair, down_pruned = lax.optimization_barrier((qkv_pair, down_pruned))
     attended = attention(2, count, *qkv_pair, qkv_bias, norm_gains)
     hidden = activate(*up_pair, up_bias)
-    kept, given = out_products(
-        attended, swap(attended, "wt", 1), hidden, swap(hidden, "wt", 1), proj_weight, down_pruned
-    )
-    kept, given = small(fold_kernel, [rows_of(4, f32), rows_of(4, bf16)], kept, swap(given, "seq", 1))
-    mine, given = small(divide_kernel, [rows_of(2, f32)] * 2, kept, swap(given, "seq", 2))
-    here, given = small(join_kernel, [rows_of(2, f32)] * 2, mine, swap(given, "wt", 2))
-    there = swap(given, "wt", 1)
+    shares = out_products(
+        count, attended, swap(attended, "wt", 1), hidden, swap(hidden, "wt", 1), proj_weight, down_pruned
+    )
+    shares = lax.all_to_all(shares, ("seq", "wt"), split_axis=0, concat_axis=0, tiled=True)
     out = jax.ShapeDtypeStruct(tokens.shape, tokens.dtype)
-    return small(leave_kernel, out, here, there, tokens, modulation.transpose(1, 0, 2), out_bias.reshape(1, -1))
+    return small(leave_kernel, out, shares, tokens, modulation.transpose(1, 0, 2), out_bias.reshape(1, -1))
 
 
 def solution(mesh):

time: 48.7 us -> 47.9 us (0.984)
  blocking collectives: 0 us -> 13.5 us
  waiting for transfers between devices: 22.1 us -> 13.3 us
  starting transfers between devices: 18.4 us -> 11.3 us
  Pallas kernels: 6.21 us -> 7.75 us
    all_to_all x0 -> x1, blocking collectives: none -> 13.5 us  [fixed_shards(): lax.all_to_all(shares, ('seq', 'wt'), split_axis=0, concat_axis=0, tiled=...]
    ppermute x14 -> x11, waiting for transfers between devices: 22.1 us -> 13.3 us  [swap(): return lax.ppermute(values, axis, [(i, i ^ bit) for i in range(count)])]
    ppermute x14 -> x11, starting transfers between devices: 18.4 us -> 11.3 us  [swap(): return lax.ppermute(values, axis, [(i, i ^ bit) for i in range(count)])]
    pallas_call x3 -> x6, Pallas kernels: 2.84 us -> 4.41 us  [the longest x3 3.17 us: in_products(): pl.pallas_call(functools.partial(in_kernel, len(weights)), out_shape=[jax...]
  transfers between devices with their start and end apart: 14 -> 11, of which waited for: 11 -> 9; matrix products, arithmetic and copies ran while one was open for 0% -> 0% of each run, Pallas kernels for 5% -> 12%
where the time goes in v3:
time: 47.9 us; the launch traced here: 47.6 us
  blocking collectives  13.5 us (28%)
  waiting for transfers between devices  13.3 us (28%)
  starting transfers between devices  11.3 us (24%)
  Pallas kernels  7.75 us (16%)
  local copies, waits for them, and re-layouts  1.56 us (3%)
    all_to_all x1, blocking collectives, fixed_shards(): lax.all_to_all(shares, ('seq', 'wt'), split_axis=0, concat_axis=0, tiled=...  13.5 us
    ppermute x11, waiting for transfers between devices, swap(): return lax.ppermute(values, axis, [(i, i ^ bit) for i in range(count)])  13.3 us
    ppermute x11, starting transfers between devices, swap(): return lax.ppermute(values, axis, [(i, i ^ bit) for i in range(count)])  11.3 us
    pallas_call x3, Pallas kernels, in_products(): pl.pallas_call(functools.partial(in_kernel, len(weights)), out_shape=[jax...  3.17 us
    pallas_call x2, Pallas kernels, prune(): pl.pallas_call(functools.partial(prune_kernel, 0 if turned else 1), out_s...  1.74 us
    unnamed x27, local copies, waits for them, and re-layouts  1.56 us
    pallas_call x1, Pallas kernels, out_products(): pl.pallas_call(out_kernel, out_shape=jax.ShapeDtypeStruct((2 * half // co...  1.16 us
  transfers between devices with their start and end apart: 11, of which 9 were waited for; matrix products, arithmetic and copies ran while one was open for 0% of the time, Pallas kernels for 12%

profile of v3, /device:TPU:0, one launch (start us, length us, event | category | flops | bytes accessed | tf_op | source)
XLA Modules:
  0.0 47.6 jit_solution(10116651229673367091)
XLA Ops:
  0.0 0.8 %copy-done.3 = f32[1,3,3072]{2,0,1:T(1,128)S(1)} copy-done((f32[1,3,3072]{2,0,1:T(1,128)S(1)}, f32[1,3,3072]{2,0,1:T(1,128)}, u32[]{:S(2)}) %copy-start.3) | copy-done | bytes 36888
  0.8 0.7 %copy-done.4 = bf16[1,4,3072]{2,1,0:T(4,128)(2,1)S(1)} copy-done((bf16[1,4,3072]{2,1,0:T(4,128)(2,1)S(1)}, bf16[1,4,3072]{2,1,0:T(4,128)(2,1)}, u32[]{:S(2)}) %copy-start.4) | copy-done | bytes 24600
  1.5 0.3 enter.1
  1.8 0.5 %collective-permute-start = (bf16[4,1536]{1,0:T(4,128)(2,1)S(1)}, bf16[4,1536]{1,0:T(4,128)(2,1)S(1)}, u32[]{:S(2)}, u32[]{:S(2)}) collective-permute-start(bf16[4,1536]{1,0:T(4,128)(2,1)S(1)} %get-tuple-element.29), channel_id=1, source_target_pairs={{0,1},{1,0},{2,3},{3,2},{4,5},{5,4},{6,7},{7,6},{8,9},{9,8},{10,11... | collective-permute-start | bytes 36872 | tf_op jit(solution)/shard_map/ppermute | solution.py:381
  2.3 0.8 %collective-permute-done.got_ref = bf16[4,1536]{1,0:T(4,128)(2,1)S(1)} collective-permute-done((bf16[4,1536]{1,0:T(4,128)(2,1)S(1)}, bf16[4,1536]{1,0:T(4,128)(2,1)S(1)}, u32[]{:S(2)}, u32[]{:S(2)}) %collective-permute-start) | collective-permute-done | bytes 12320 | tf_op jit(solution)/shard_map/ppermute | solution.py:381
  3.2 2.9 %collective-permute-start.1 = (bf16[8,768]{1,0:T(8,128)(2,1)S(1)}, bf16[8,768]{1,0:T(8,128)(2,1)S(1)}, u32[]{:S(2)}, u32[]{:S(2)}) collective-permute-start(bf16[8,768]{1,0:T(8,128)(2,1)S(1)} %get-tuple-element.31), channel_id=1, source_target_pairs={{0,2},{1,3},{2,0},{3,1},{4,6},{5,7},{6,4},{7,5},{8,10},{9,11},{10,... | collective-permute-start | bytes 36872 | tf_op jit(solution)/shard_map/ppermute | solution.py:381
  6.1 0.7 %prune.2.refs_1_.refs_0_ = bf16[768,3072]{1,0:T(8,128)(2,1)S(1)} custom-call(s32[12,48]{1,0:T(8,128)S(1)} %copy-done.8, bf16[768,3072]{1,0:T(8,128)(2,1)S(1)} %copy-done.1), custom_call_target="tpu_custom_call" | custom-call | flops 4718592 | bytes 9437184 | tf_op jit(solution)/shard_map/prune/pallas_call | solution.py:226
  6.8 1.0 %collective-permute-done.1.theirs_ref = bf16[8,768]{1,0:T(8,128)(2,1)S(1)} collective-permute-done((bf16[8,768]{1,0:T(8,128)(2,1)S(1)}, bf16[8,768]{1,0:T(8,128)(2,1)S(1)}, u32[]{:S(2)}, u32[]{:S(2)}) %collective-permute-start.1) | collective-permute-done | bytes 12320 | tf_op jit(solution)/shard_map/ppermute | solution.py:381
  7.8 3.2 %collective-permute-start.2 = (bf16[16,768]{1,0:T(8,128)(2,1)S(1)}, bf16[16,768]{1,0:T(8,128)(2,1)S(1)}, u32[]{:S(2)}, u32[]{:S(2)}) collective-permute-start(bf16[16,768]{1,0:T(8,128)(2,1)S(1)} %near_kernel.1), channel_id=1, source_target_pairs={{0,8},{4,12},{8,0},{12,4},{1,9},{5,13},{9,1},{13,5},{2,10},{6,14},... | collective-permute-start | bytes 73736 | tf_op jit(solution)/shard_map/ppermute | solution.py:381
  11.0 1.9 %collective-permute-done.2 = bf16[16,768]{1,0:T(8,128)(2,1)S(1)} collective-permute-done((bf16[16,768]{1,0:T(8,128)(2,1)S(1)}, bf16[16,768]{1,0:T(8,128)(2,1)S(1)}, u32[]{:S(2)}, u32[]{:S(2)}) %collective-permute-start.2) | collective-permute-done | bytes 24608 | tf_op jit(solution)/shard_map/ppermute | solution.py:381
  12.9 1.8 %collective-permute-start.3 = (bf16[32,768]{1,0:T(8,128)(2,1)S(1)}, bf16[32,768]{1,0:T(8,128)(2,1)S(1)}, u32[]{:S(2)}, u32[]{:S(2)}) collective-permute-start(bf16[32,768]{1,0:T(8,128)(2,1)S(1)} %constant_dynamic-update-slice_fusion.x_ref), channel_id=1, source_target_pairs={{0,4},{4,0},{8,12},{12,8},{1,5},{5,1},{9,13},{13,9},{2,6},{6,2},{1... | collective-permute-start | bytes 147464 | tf_op jit(solution)/shard_map/ppermute | solution.py:381
  14.7 1.5 %in_products.3 = (f32[16,5376]{1,0:T(8,128)S(1)}, bf16[16,5376]{1,0:T(8,128)(2,1)S(1)}) custom-call(bf16[32,768]{1,0:T(8,128)(2,1)S(1)} %constant_dynamic-update-slice_fusion.x_ref, bf16[3,768,768]{2,1,0:T(8,128)(2,1)S(1)} %bitcast.5, bf16[768,3072]{1,0:T(8,128)(2,1)S(1)} %prune.2.refs_1_.refs_0_), custom_call_target="tpu_custom_call" | custom-call | flops 264241152 | bytes 8257536 | tf_op jit(solution)/shard_map/in_products/pallas_call | solution.py:256
  16.2 0.7 %collective-permute-done.3.x_ref = bf16[32,768]{1,0:T(8,128)(2,1)S(1)} collective-permute-done((bf16[32,768]{1,0:T(8,128)(2,1)S(1)}, bf16[32,768]{1,0:T(8,128)(2,1)S(1)}, u32[]{:S(2)}, u32[]{:S(2)}) %collective-permute-start.3) | collective-permute-done | bytes 49184 | tf_op jit(solution)/shard_map/ppermute | solution.py:381
  17.0 0.7 %in_products.4 = (f32[16,2304]{1,0:T(8,128)S(1)}, bf16[16,2304]{1,0:T(8,128)(2,1)S(1)}) custom-call(bf16[32,768]{1,0:T(8,128)(2,1)S(1)} %collective-permute-done.3.x_ref, bf16[3,768,768]{2,1,0:T(8,128)(2,1)S(1)} %bitcast.6), custom_call_target="tpu_custom_call" | custom-call | tf_op jit(solution)/shard_map/in_products/pallas_call | solution.py:256
  17.7 0.9 %in_products.5 = (f32[16,3072]{1,0:T(8,128)S(1)}, bf16[16,3072]{1,0:T(8,128)(2,1)S(1)}) custom-call(bf16[32,768]{1,0:T(8,128)(2,1)S(1)} %collective-permute-done.3.x_ref, bf16[768,3072]{1,0:T(8,128)(2,1)S(1)} %prune.2.refs_1_.refs_0_), custom_call_target="tpu_custom_call" | custom-call | tf_op jit(solution)/shard_map/in_products/pallas_call | solution.py:256
  18.6 0.5 %collective-permute-start.8 = (bf16[16,3072]{1,0:T(8,128)(2,1)S(1)}, bf16[16,3072]{1,0:T(8,128)(2,1)S(1)}, u32[]{:S(2)}, u32[]{:S(2)}) collective-permute-start(bf16[16,3072]{1,0:T(8,128)(2,1)S(1)} %get-tuple-element.47), channel_id=1, source_target_pairs={{0,1},{1,0},{2,3},{3,2},{4,5},{5,4},{6,7},{7,6},{8,9},{9,8},{10,11... | collective-permute-start | bytes 294920 | tf_op jit(solution)/shard_map/ppermute | solution.py:381
  19.1 0.9 %collective-permute-done.8.far_got = bf16[16,3072]{1,0:T(8,128)(2,1)S(1)} collective-permute-done((bf16[16,3072]{1,0:T(8,128)(2,1)S(1)}, bf16[16,3072]{1,0:T(8,128)(2,1)S(1)}, u32[]{:S(2)}, u32[]{:S(2)}) %collective-permute-start.8) | collective-permute-done | bytes 98336 | tf_op jit(solution)/shard_map/ppermute | solution.py:381
  20.1 1.8 %collective-permute-start.9 = (bf16[32,3072]{1,0:T(8,128)(2,1)S(1)}, bf16[32,3072]{1,0:T(8,128)(2,1)S(1)}, u32[]{:S(2)}, u32[]{:S(2)}) collective-permute-start(bf16[32,3072]{1,0:T(8,128)(2,1)S(1)} %get-tuple-element.49), channel_id=1, source_target_pairs={{0,2},{1,3},{2,0},{3,1},{4,6},{5,7},{6,4},{7,5},{8,10},{9,11},{10,... | collective-permute-start | bytes 589832 | tf_op jit(solution)/shard_map/ppermute | solution.py:381
  21.9 0.1 collective-permute-start.5
  22.0 1.2 %collective-permute-done.5.far_got = bf16[16,2304]{1,0:T(8,128)(2,1)S(1)} collective-permute-done((bf16[16,2304]{1,0:T(8,128)(2,1)S(1)}, bf16[16,2304]{1,0:T(8,128)(2,1)S(1)}, u32[]{:S(2)}, u32[]{:S(2)}) %collective-permute-start.5) | collective-permute-done | bytes 73760 | tf_op jit(solution)/shard_map/ppermute | solution.py:381
  23.2 0.4 collective-permute-start.6
  23.6 4.3 %collective-permute-done.9.other_ref = bf16[32,3072]{1,0:T(8,128)(2,1)S(1)} collective-permute-done((bf16[32,3072]{1,0:T(8,128)(2,1)S(1)}, bf16[32,3072]{1,0:T(8,128)(2,1)S(1)}, u32[]{:S(2)}, u32[]{:S(2)}) %collective-permute-start.9) | collective-permute-done | bytes 196640 | tf_op jit(solution)/shard_map/ppermute | solution.py:381
  27.9 0.2 hidden.1.h_mine
  28.1 0.1 collective-permute-start.10
  28.3 1.1 %prune.3.down_ref = bf16[3072,768]{1,0:T(8,128)(2,1)S(1)} custom-call(s32[12,48]{1,0:T(8,128)S(1)} %bitcast.13, bf16[3072,768]{1,0:T(8,128)(2,1)S(1)} %bitcast.8), custom_call_target="tpu_custom_call" | custom-call | tf_op jit(solution)/shard_map/prune/pallas_call | solution.py:226
  29.3 1.2 %collective-permute-done.6.other_ref = bf16[32,2304]{1,0:T(8,128)(2,1)S(1)} collective-permute-done((bf16[32,2304]{1,0:T(8,128)(2,1)S(1)}, bf16[32,2304]{1,0:T(8,128)(2,1)S(1)}, u32[]{:S(2)}, u32[]{:S(2)}) %collective-permute-start.6) | collective-permute-done | bytes 147488 | tf_op jit(solution)/shard_map/ppermute | solution.py:381
  30.5 0.4 attention.1.a_mine
  31.0 0.1 collective-permute-start.7
  31.0 1.2 %collective-permute-done.7.a_theirs = bf16[32,768]{1,0:T(8,128)(2,1)S(1)} collective-permute-done((bf16[32,768]{1,0:T(8,128)(2,1)S(1)}, bf16[32,768]{1,0:T(8,128)(2,1)S(1)}, u32[]{:S(2)}, u32[]{:S(2)}) %collective-permute-start.7) | collective-permute-done | bytes 49184 | tf_op jit(solution)/shard_map/ppermute | solution.py:381
  32.3 1.2 %out_products.1 = bf16[16,4,768]{2,1,0:T(4,128)(2,1)S(1)} custom-call(bf16[32,768]{1,0:T(8,128)(2,1)S(1)} %attention.1.a_mine, bf16[32,768]{1,0:T(8,128)(2,1)S(1)} %collective-permute-done.7.a_theirs, bf16[32,3072]{1,0:T(8,128)(2,1)S(1)} %hidden.1.h_mine, bf16[32,3072]{1,0:T(8,128)(2,1)S(1)} %collective-permute-done.10.h_theirs, ...), custom_call_target="tpu_custom_call" | custom-call | flops 377487360 | bytes 5898240 | tf_op jit(solution)/shard_map/out_products/pallas_call | solution.py:370
  33.4 13.5 %all_to_all.5.shares_ref = bf16[16,4,768]{2,1,0:T(4,128)(2,1)S(1)} all-to-all(bf16[16,4,768]{2,1,0:T(4,128)(2,1)S(1)} %out_products.1), channel_id=1, replica_groups=mesh['rep'=2,'seq'=4,'wt'=4] {'seq','wt'}, dimensions={0} | all-to-all | bytes 196608 | tf_op jit(solution)/shard_map/all_to_all | solution.py:433
  46.9 0.6 %leave_kernel.1 = bf16[1,4,3072]{2,1,0:T(4,128)(2,1)} custom-call(bf16[16,4,768]{2,1,0:T(4,128)(2,1)S(1)} %all_to_all.5.shares_ref, bf16[1,4,3072]{2,1,0:T(4,128)(2,1)S(1)} %copy-done.4, f32[3,1,3072]{2,1,0:T(1,128)S(1)} %bitcast.10, f32[1,3072]{1,0:T(1,128)S(1)} %bitcast.11), custom_call_target="tpu_custom_call" | custom-call | tf_op jit(solution)/shard_map/leave_kernel/pallas_call | solution.py:192
  (34 shorter events, 0.2 us)
Async XLA Ops:
  0.0 0.8 %copy-start.3 = (f32[1,3,3072]{2,0,1:T(1,128)S(1)}, f32[1,3,3072]{2,0,1:T(1,128)}, u32[]{:S(2)}) copy-start(f32[1,3,3072]{2,0,1:T(1,128)} %param.13) | copy-start | bytes 110596
  0.8 0.7 %copy-start.4 = (bf16[1,4,3072]{2,1,0:T(4,128)(2,1)S(1)}, bf16[1,4,3072]{2,1,0:T(4,128)(2,1)}, u32[]{:S(2)}) copy-start(bf16[1,4,3072]{2,1,0:T(4,128)(2,1)} %tokens_ref.1) | copy-start | bytes 73732
  1.8 1.4 %collective-permute-start = (bf16[4,1536]{1,0:T(4,128)(2,1)S(1)}, bf16[4,1536]{1,0:T(4,128)(2,1)S(1)}, u32[]{:S(2)}, u32[]{:S(2)}) collective-permute-start(bf16[4,1536]{1,0:T(4,128)(2,1)S(1)} %get-tuple-element.29), channel_id=1, source_target_pairs={{0,1},{1,0},{2,3},{3,2},{4,5},{5,4},{6,7},{7,6},{8,9},{9,8},{10,11... | collective-permute-start | bytes 36872 | tf_op jit(solution)/shard_map/ppermute | solution.py:381
  3.2 2.9 %copy-start.1 = (bf16[768,3072]{1,0:T(8,128)(2,1)S(1)}, bf16[768,3072]{1,0:T(8,128)(2,1)}, u32[]{:S(2)}) copy-start(bf16[768,3072]{1,0:T(8,128)(2,1)} %weight_ref.2) | copy-start | bytes 14155780
  3.2 2.9 %copy-start.8 = (s32[12,48]{1,0:T(8,128)S(1)}, s32[12,48]{1,0:T(8,128)}, u32[]{:S(2)}) copy-start(s32[12,48]{1,0:T(8,128)} %mask_ref.1) | copy-start | bytes 6916
  3.2 4.6 %collective-permute-start.1 = (bf16[8,768]{1,0:T(8,128)(2,1)S(1)}, bf16[8,768]{1,0:T(8,128)(2,1)S(1)}, u32[]{:S(2)}, u32[]{:S(2)}) collective-permute-start(bf16[8,768]{1,0:T(8,128)(2,1)S(1)} %get-tuple-element.31), channel_id=1, source_target_pairs={{0,2},{1,3},{2,0},{3,1},{4,6},{5,7},{6,4},{7,5},{8,10},{9,11},{10,... | collective-permute-start | bytes 36872 | tf_op jit(solution)/shard_map/ppermute | solution.py:381
  7.8 6.9 %copy-start = (bf16[768,3,768]{2,0,1:T(8,128)(2,1)S(1)}, bf16[768,3,768]{2,0,1:T(8,128)(2,1)}, u32[]{:S(2)}) copy-start(bf16[768,3,768]{2,0,1:T(8,128)(2,1)} %param.14) | copy-start | bytes 10616836
  7.8 5.1 %collective-permute-start.2 = (bf16[16,768]{1,0:T(8,128)(2,1)S(1)}, bf16[16,768]{1,0:T(8,128)(2,1)S(1)}, u32[]{:S(2)}, u32[]{:S(2)}) collective-permute-start(bf16[16,768]{1,0:T(8,128)(2,1)S(1)} %near_kernel.1), channel_id=1, source_target_pairs={{0,8},{4,12},{8,0},{12,4},{1,9},{5,13},{9,1},{13,5},{2,10},{6,14},... | collective-permute-start | bytes 73736 | tf_op jit(solution)/shard_map/ppermute | solution.py:381
  12.9 4.1 %collective-permute-start.3 = (bf16[32,768]{1,0:T(8,128)(2,1)S(1)}, bf16[32,768]{1,0:T(8,128)(2,1)S(1)}, u32[]{:S(2)}, u32[]{:S(2)}) collective-permute-start(bf16[32,768]{1,0:T(8,128)(2,1)S(1)} %constant_dynamic-update-slice_fusion.x_ref), channel_id=1, source_target_pairs={{0,4},{4,0},{8,12},{12,8},{1,5},{5,1},{9,13},{13,9},{2,6},{6,2},{1... | collective-permute-start | bytes 147464 | tf_op jit(solution)/shard_map/ppermute | solution.py:381
  14.7 13.5 %slice-start = ((s8[4718592]{0:T(1024)(128)(4,1)}), s8[4194304]{0:T(1024)(128)(4,1)S(1)}, s32[]{:S(2)}) async-start(s8[4718592]{0:T(1024)(128)(4,1)} %bitcast.7), calls=%async_computation.1 | async-start | bytes 8388608
  17.0 11.0 %copy-start.6 = (f32[3072]{0:T(1024)S(1)}, f32[3072]{0:T(1024)}, u32[]{:S(2)}) copy-start(f32[3072]{0:T(1024)} %param.19) | copy-start | bytes 36868
  17.0 11.2 %slice-start.1 = ((s8[4718592]{0:T(1024)(128)(4,1)}), s8[524288]{0:T(1024)(128)(4,1)S(1)}, s32[]{:S(2)}) async-start(s8[4718592]{0:T(1024)(128)(4,1)} %bitcast.7), calls=%async_computation.2 | async-start | bytes 1048576
  17.0 11.2 %copy-start.9 = (s32[48,12]{0,1:T(8,128)S(1)}, s32[48,12]{0,1:T(8,128)}, u32[]{:S(2)}) copy-start(s32[48,12]{0,1:T(8,128)} %param.22) | copy-start | bytes 6916
  17.0 3.1 %collective-permute-start.4 = (bf16[16,5376]{1,0:T(8,128)(2,1)S(1)}, bf16[16,5376]{1,0:T(8,128)(2,1)S(1)}, u32[]{:S(2)}, u32[]{:S(2)}) collective-permute-start(bf16[16,5376]{1,0:T(8,128)(2,1)S(1)} %get-tuple-element.36), channel_id=1, source_target_pairs={{0,1},{1,0},{2,3},{3,2},{4,5},{5,4},{6,7},{7,6},{8,9},{9,8},{10,11... | collective-permute-start | bytes 516104 | tf_op jit(solution)/shard_map/ppermute | solution.py:381
  18.6 1.5 %collective-permute-start.8 = (bf16[16,3072]{1,0:T(8,128)(2,1)S(1)}, bf16[16,3072]{1,0:T(8,128)(2,1)S(1)}, u32[]{:S(2)}, u32[]{:S(2)}) collective-permute-start(bf16[16,3072]{1,0:T(8,128)(2,1)S(1)} %get-tuple-element.47), channel_id=1, source_target_pairs={{0,1},{1,0},{2,3},{3,2},{4,5},{5,4},{6,7},{7,6},{8,9},{9,8},{10,11... | collective-permute-start | bytes 294920 | tf_op jit(solution)/shard_map/ppermute | solution.py:381
  20.1 7.8 %collective-permute-start.9 = (bf16[32,3072]{1,0:T(8,128)(2,1)S(1)}, bf16[32,3072]{1,0:T(8,128)(2,1)S(1)}, u32[]{:S(2)}, u32[]{:S(2)}) collective-permute-start(bf16[32,3072]{1,0:T(8,128)(2,1)S(1)} %get-tuple-element.49), channel_id=1, source_target_pairs={{0,2},{1,3},{2,0},{3,1},{4,6},{5,7},{6,4},{7,5},{8,10},{9,11},{10,... | collective-permute-start | bytes 589832 | tf_op jit(solution)/shard_map/ppermute | solution.py:381
  21.9 1.3 %collective-permute-start.5 = (bf16[16,2304]{1,0:T(8,128)(2,1)S(1)}, bf16[16,2304]{1,0:T(8,128)(2,1)S(1)}, u32[]{:S(2)}, u32[]{:S(2)}) collective-permute-start(bf16[16,2304]{1,0:T(8,128)(2,1)S(1)} %get-tuple-element.40), channel_id=1, source_target_pairs={{0,1},{1,0},{2,3},{3,2},{4,5},{5,4},{6,7},{7,6},{8,9},{9,8},{10,11... | collective-permute-start | bytes 221192 | tf_op jit(solution)/shard_map/ppermute | solution.py:381
  23.2 7.3 %collective-permute-start.6 = (bf16[32,2304]{1,0:T(8,128)(2,1)S(1)}, bf16[32,2304]{1,0:T(8,128)(2,1)S(1)}, u32[]{:S(2)}, u32[]{:S(2)}) collective-permute-start(bf16[32,2304]{1,0:T(8,128)(2,1)S(1)} %get-tuple-element.42), channel_id=1, source_target_pairs={{0,2},{1,3},{2,0},{3,1},{4,6},{5,7},{6,4},{7,5},{8,10},{9,11},{10,... | collective-permute-start | bytes 442376 | tf_op jit(solution)/shard_map/ppermute | solution.py:381
  28.1 4.2 %collective-permute-start.10 = (bf16[32,3072]{1,0:T(8,128)(2,1)S(1)}, bf16[32,3072]{1,0:T(8,128)(2,1)S(1)}, u32[]{:S(2)}, u32[]{:S(2)}) collective-permute-start(bf16[32,3072]{1,0:T(8,128)(2,1)S(1)} %hidden.1.h_mine), channel_id=1, source_target_pairs={{0,1},{1,0},{2,3},{3,2},{4,5},{5,4},{6,7},{7,6},{8,9},{9,8},{10,11... | collective-permute-start | bytes 589832 | tf_op jit(solution)/shard_map/ppermute | solution.py:381
  28.2 2.3 %copy-start.7 = (f32[3,768]{1,0:T(4,128)S(1)}, f32[3,768]{1,0:T(4,128)}, u32[]{:S(2)}) copy-start(f32[3,768]{1,0:T(4,128)} %bias_ref.1) | copy-start | bytes 27652
  28.2 2.3 %copy-start.10 = (f32[2,128]{1,0:T(2,128)S(1)}, f32[2,128]{1,0:T(2,128)}, u32[]{:S(2)}) copy-start(f32[2,128]{1,0:T(2,128)} %gains_ref.1) | copy-start | bytes 3076
  28.2 4.0 %copy-start.2 = (bf16[768,768]{1,0:T(8,128)(2,1)S(1)}, bf16[768,768]{1,0:T(8,128)(2,1)}, u32[]{:S(2)}) copy-start(bf16[768,768]{1,0:T(8,128)(2,1)} %proj_ref.1) | copy-start | bytes 3538948
  29.3 17.6 %copy-start.5 = (f32[3072]{0:T(1024)S(1)}, f32[3072]{0:T(1024)}, u32[]{:S(2)}) copy-start(f32[3072]{0:T(1024)} %param.23) | copy-start | bytes 36868
  31.0 1.3 %collective-permute-start.7 = (bf16[32,768]{1,0:T(8,128)(2,1)S(1)}, bf16[32,768]{1,0:T(8,128)(2,1)S(1)}, u32[]{:S(2)}, u32[]{:S(2)}) collective-permute-start(bf16[32,768]{1,0:T(8,128)(2,1)S(1)} %attention.1.a_mine), channel_id=1, source_target_pairs={{0,1},{1,0},{2,3},{3,2},{4,5},{5,4},{6,7},{7,6},{8,9},{9,8},{10,11... | collective-permute-start | bytes 147464 | tf_op jit(solution)/shard_map/ppermute | solution.py:381

commit v4 on v0

--- a/solution.py
+++ b/solution.py
@@ -1,12 +1,19 @@
+import functools
 import math
 
 import jax
 import jax.numpy as jnp
 from jax import lax
+from jax.experimental import pallas as pl
+from jax.experimental.pallas import tpu as pltpu
 from jax.sharding import PartitionSpec as P
 
 HEAD = 128
 BLOCK = 64
+MIB = 1024 * 1024
+STREAM = 52
+AHEAD = 7
+BESIDE = 16 * MIB
 
 
 def masked(weight, keep_mask):
@@ -43,7 +50,7 @@
     return (summed, denoms)
 
 
-def shards(
+def gathered_shards(
     tokens,
     modulation,
     qkv_weight,
@@ -105,7 +112,274 @@
     return result.astype(jnp.bfloat16)[None]
 
 
+def enter_kernel(tokens_ref, mod_ref, out_ref):
+    shaped = (1.0 + mod_ref[1]) * layer_norm(tokens_ref[0].astype(jnp.float32)) + mod_ref[0]
+    shaped = shaped.astype(jnp.bfloat16)
+    share = out_ref.shape[2]
+    for place in range(out_ref.shape[0]):
+        out_ref[place] = shaped[:, place % 4 * share : (place % 4 + 1) * share]
+
+
+def enter(tokens, modulation):
+    _, count, features = tokens.shape
+    return pl.pallas_call(
+        enter_kernel,
+        out_shape=jax.ShapeDtypeStruct((16, count, features // 4), jnp.bfloat16),
+        compiler_params=pltpu.CompilerParams(vmem_limit_bytes=4 * MIB),
+        cost_estimate=pl.CostEstimate(flops=400 * BESIDE, bytes_accessed=BESIDE, transcendentals=BESIDE // 100),
+        name="enter",
+    )(tokens, modulation.transpose(1, 0, 2))
+
+
+def leave_kernel(shares_ref, tokens_ref, mod_ref, bias_ref, out_ref):
+    share = shares_ref.shape[2]
+    for n in range(4):
+        lanes = slice(n * share, (n + 1) * share)
+        branch = sum(shares_ref[4 * place + n].astype(jnp.float32) for place in range(4)) + bias_ref[:, lanes]
+        out_ref[0, :, lanes] = (tokens_ref[0, :, lanes].astype(jnp.float32) + mod_ref[2, :, lanes] * branch).astype(out_ref.dtype)
+
+
+def small(kernel, outs, *args):
+    return pl.pallas_call(
+        kernel,
+        out_shape=outs,
+        compiler_params=pltpu.CompilerParams(vmem_limit_bytes=4 * MIB),
+        name=kernel.__name__,
+    )(*args)
+
+
+def pick_lanes(blocks, lanes):
+    return (
+        lax.broadcasted_iota(jnp.int32, (blocks, lanes), 1) // BLOCK
+        == lax.broadcasted_iota(jnp.int32, (blocks, lanes), 0)
+    ).astype(jnp.bfloat16)
+
+
+def prune_kernel(mask_dim, mask_ref, weight_ref, out_ref, lanes):
+    lanes[...] = lax.dot_general(
+        mask_ref[...].astype(jnp.bfloat16),
+        pick_lanes(mask_ref.shape[mask_dim], out_ref.shape[1]),
+        (((mask_dim,), (0,)), ((), ())),
+        preferred_element_type=jnp.float32,
+    )
+
+    def body(b, _):
+        rows = pl.ds(pl.multiple_of(b * BLOCK, BLOCK), BLOCK)
+        out_ref[rows, :] = weight_ref[rows, :] * lanes[pl.ds(b, 1), :].astype(jnp.bfloat16)
+        return 0
+
+    lax.fori_loop(0, out_ref.shape[0] // BLOCK, body, 0)
+
+
+def prune(weight, mask, turned, hint=1):
+    size = 2 * weight.size
+    return pl.pallas_call(
+        functools.partial(prune_kernel, 0 if turned else 1),
+        out_shape=jax.ShapeDtypeStruct(weight.shape, jnp.bfloat16),
+        scratch_shapes=[pltpu.VMEM((weight.shape[0] // BLOCK, weight.shape[1]), jnp.float32)],
+        compiler_params=pltpu.CompilerParams(vmem_limit_bytes=14 * MIB),
+        cost_estimate=pl.CostEstimate(flops=size * hint, bytes_accessed=2 * size * hint, transcendentals=0),
+        name="prune",
+    )(mask.T if turned else mask, weight)
+
+
+def in_kernel(got_ref, mask_hbm, qkv_hbm, up_hbm, keep_ref, send_ref, tiles, mask_ref, lanes, sems):
+    share = got_ref.shape[2]
+    count = tiles.shape[0]
+    copies = [
+        pltpu.make_async_copy(
+            qkv_hbm.at[n] if n < 3 else up_hbm.at[:, pl.ds((n - 3) * share, share)], tiles.at[n], sems.at[n]
+        )
+        for n in range(count)
+    ]
+    mask_copy = pltpu.make_async_copy(mask_hbm, mask_ref, sems.at[count])
+    mask_copy.start()
+    for copy in copies[:AHEAD]:
+        copy.start()
+    mask_copy.wait()
+    lanes[...] = jnp.dot(
+        mask_ref[...].astype(jnp.bfloat16),
+        pick_lanes(mask_ref.shape[1], lanes.shape[1]),
+        preferred_element_type=jnp.float32,
+    )
+    core = lax.axis_index("wt") % 2
+    x = jnp.concatenate(
+        [
+            got_ref[4 * place + 2 * chip + (core ^ other_core)].astype(jnp.float32)
+            for place in range(4)
+            for other_core in range(2)
+            for chip in range(2)
+        ],
+        axis=0,
+    ).astype(jnp.bfloat16)
+    for n, copy in enumerate(copies):
+        copy.wait()
+        if n + AHEAD < count:
+            copies[n + AHEAD].start()
+        if n < 3:
+            weight = tiles[n]
+        else:
+            cols = slice((n - 3) * share, (n - 2) * share)
+            weight = jnp.concatenate(
+                [
+                    tiles[n, r * BLOCK : (r + 1) * BLOCK] * lanes[r : r + 1, cols].astype(jnp.bfloat16)
+                    for r in range(lanes.shape[0])
+                ],
+                axis=0,
+            )
+        out = jnp.dot(x, weight, preferred_element_type=jnp.float32)
+        cols = slice(n * share, (n + 1) * share)
+        keep_ref[:, cols] = jnp.concatenate([out[r : r + 8] for r in range(0, 64, 16)], axis=0)
+        send_ref[:, cols] = jnp.concatenate([out[r + 8 : r + 16] for r in range(0, 64, 16)], axis=0).astype(jnp.bfloat16)
+
+
+def in_products(got, qkv_weight, up_weight, up_mask):
+    places, count, depth = got.shape
+    size = qkv_weight.size + up_weight.size
+    half, width = places * count // 2, size // depth
+    return pl.pallas_call(
+        in_kernel,
+        in_specs=[pl.BlockSpec(memory_space=pltpu.VMEM)] + [pl.BlockSpec(memory_space=pltpu.HBM)] * 3,
+        out_shape=[
+            jax.ShapeDtypeStruct((half, width), jnp.float32),
+            jax.ShapeDtypeStruct((half, width), jnp.bfloat16),
+        ],
+        scratch_shapes=[
+            pltpu.VMEM((width // depth, depth, depth), jnp.bfloat16),
+            pltpu.VMEM(up_mask.shape, up_mask.dtype),
+            pltpu.VMEM((up_mask.shape[0], up_weight.shape[1]), jnp.float32),
+            pltpu.SemaphoreType.DMA((width // depth + 1,)),
+        ],
+        compiler_params=pltpu.CompilerParams(vmem_limit_bytes=STREAM * MIB),
+        cost_estimate=pl.CostEstimate(flops=4 * half * size, bytes_accessed=2 * size, transcendentals=0),
+        name="in_products",
+    )(got, up_mask, qkv_weight.transpose(1, 0, 2), up_weight)
+
+
+def mid_kernel(images, part, own_ref, other_ref, qkv_bias_ref, gains_ref, up_bias_ref, out_ref):
+    rows = own_ref.shape[0]
+    share = qkv_bias_ref.shape[1]
+    heads = share // HEAD
+
+    def total(start, size):
+        return own_ref[:, start : start + size] + other_ref[:, start : start + size].astype(jnp.float32)
+
+    def stacked(which):
+        flat = (total(which * share, share) + qkv_bias_ref[which : which + 1, :]).astype(jnp.bfloat16)
+        return jnp.concatenate([flat[:, h * HEAD : (h + 1) * HEAD] for h in range(heads)], axis=0)
+
+    def normed(which):
+        wide = stacked(which).astype(jnp.float32)
+        scale = lax.rsqrt(jnp.mean(wide * wide, axis=-1, keepdims=True) + 1e-06)
+        return (wide * scale * gains_ref[which : which + 1, :]).astype(jnp.bfloat16)
+
+    queries, keys, values = normed(0), normed(1), stacked(2)
+    scores = lax.dot_general(
+        queries, keys, (((1,), (1,)), ((), ())), preferred_element_type=jnp.float32
+    ) * (1.0 / math.sqrt(HEAD))
+    size = heads * rows
+
+    def group(dim):
+        place = lax.broadcasted_iota(jnp.int32, (size, size), dim)
+        return place // rows * images + place // part % images
+
+    same = group(0) == group(1)
+    weights = jnp.where(same, jnp.exp(jnp.where(same, scores, 0.0)), 0.0)
+    denoms = jnp.sum(weights, axis=-1, keepdims=True)
+    summed = jnp.dot(weights.astype(jnp.bfloat16), values, preferred_element_type=jnp.float32)
+    attended = (summed / denoms).astype(jnp.bfloat16)
+    for h in range(heads):
+        out_ref[:, h * HEAD : (h + 1) * HEAD] = attended[h * rows : (h + 1) * rows]
+    hidden = out_ref.shape[1] - share
+    for start in range(0, hidden, share):
+        v = total(3 * share + start, share) + up_bias_ref[:, start : start + share]
+        cubic = math.sqrt(2.0 / math.pi) * (v + 0.044715 * (v * v * v))
+        out_ref[:, share + start : 2 * share + start] = (0.5 * v * (1.0 + jnp.tanh(cubic))).astype(jnp.bfloat16)
+
+
+def middle(images, part, own, other, qkv_bias, gains, up_bias):
+    rows = own.shape[0]
+    share = qkv_bias.shape[1]
+    width = own.shape[1] - 2 * share
+    return pl.pallas_call(
+        functools.partial(mid_kernel, images, part),
+        out_shape=jax.ShapeDtypeStruct((rows, width), jnp.bfloat16),
+        compiler_params=pltpu.CompilerParams(vmem_limit_bytes=8 * MIB),
+        name="middle",
+    )(own, other, qkv_bias, gains, up_bias.reshape(1, -1))
+
+
+def out_kernel(mine, theirs, proj_ref, down_ref, out_ref):
+    mixed = jnp.concatenate([mine[...], theirs[...]], axis=0)
+    depth = proj_ref.shape[0]
+    total = jnp.dot(mixed[:, :depth], proj_ref[...], preferred_element_type=jnp.float32)
+    total += jnp.dot(mixed[:, depth:], down_ref[...], preferred_element_type=jnp.float32)
+    core = lax.axis_index("wt") % 2
+    count = out_ref.shape[1]
+    row = 0
+    for other_core in range(2):
+        for place in range(4):
+            for chip in range(2):
+                target = 4 * place + 2 * chip + (core ^ other_core)
+                out_ref[target] = total[row : row + count].astype(out_ref.dtype)
+                row += count
+
+
+def out_products(count, mine, theirs, proj, down):
+    half, width = mine.shape[0], proj.shape[1]
+    size = proj.size + down.size
+    return pl.pallas_call(
+        out_kernel,
+        out_shape=jax.ShapeDtypeStruct((2 * half // count, count, width), jnp.bfloat16),
+        compiler_params=pltpu.CompilerParams(vmem_limit_bytes=12 * MIB),
+        cost_estimate=pl.CostEstimate(flops=4 * half * size, bytes_accessed=2 * size, transcendentals=0),
+        name="out_products",
+    )(mine, theirs, proj, down)
+
+
+def swap(values, axis, bit):
+    count = lax.axis_size(axis)
+    return lax.ppermute(values, axis, [(i, i ^ bit) for i in range(count)])
+
+
+def fixed_shards(
+    tokens,
+    modulation,
+    qkv_weight,
+    qkv_bias,
+    norm_gains,
+    up_weight,
+    up_mask,
+    up_bias,
+    proj_weight,
+    down_weight,
+    down_mask,
+    out_bias,
+):
+    count = tokens.shape[1]
+    both = ("seq", "wt")
+    got = lax.all_to_all(enter(tokens, modulation), both, split_axis=0, concat_axis=0, tiled=True)
+    kept, given = in_products(got, qkv_weight, up_weight, up_mask)
+    own = kept + swap(given, "wt", 1).astype(jnp.float32)
+    pair = own, swap(own.astype(jnp.bfloat16), "wt", 2)
+    down_pruned = prune(down_weight, down_mask, True, hint=0)
+    pair, down_pruned = lax.optimization_barrier((pair, down_pruned))
+    mixed = middle(2, count, *pair, qkv_bias, norm_gains, up_bias)
+    shares = out_products(count, mixed, swap(mixed, "wt", 1), proj_weight, down_pruned)
+    shares = lax.all_to_all(shares, both, split_axis=0, concat_axis=0, tiled=True)
+    out = jax.ShapeDtypeStruct(tokens.shape, tokens.dtype)
+    return small(leave_kernel, out, shares, tokens, modulation.transpose(1, 0, 2), out_bias.reshape(1, -1))
+
+
 def solution(mesh):
+    seq, wt = mesh.shape["seq"], mesh.shape["wt"]
+
+    def shards(*args):
+        share = args[2].shape[2]
+        whole_heads = share % HEAD == 0 and share == args[8].shape[1] and args[5].shape[1] % share == 0
+        fits = whole_heads and wt == 4 and seq == 4 and args[0].shape[1] == 4
+        return (fixed_shards if fits else gathered_shards)(*args)
+
     return jax.shard_map(
         shards,
         mesh=mesh,

time: 449 us -> 46.6 us (0.10)
  waiting for transfers between devices: 299 us -> 12 us
  local copies, waits for them, and re-layouts: 50 us -> 1.56 us
  matrix products: 29.1 us -> 0 us
  other arithmetic: 18.4 us -> 0.08 us
  between operations: 14 us -> 0.18 us
  starting transfers between devices: 8.37 us -> 0.21 us
  Pallas kernels: 0 us -> 7.68 us
    all_gather x4 -> x0, waiting for transfers between devices: 254 us -> none  [the longest x1 121 us: shards(): lax.all_gather(up_local, 'wt', axis=0, tiled=True)]
    unnamed x6 -> x0, waiting for transfers between devices: 34.5 us -> none
    dot_general x5 -> x0, matrix products: 29.1 us -> none  [the longest x1 16.2 us: shards(): jnp.dot(hidden, down_full, preferred_element_type=jnp.float32)]
    all_gather x2 -> x0, blocking collectives: 28.7 us -> none  [the longest x1 15 us: shards(): gathered = lax.all_gather(shaped, 'seq', axis=0, tiled=True)]
    convert_element_type x2 -> x0, local copies, waits for them, and re-layouts: 25.9 us -> none  [masked(): return weight * expanded.reshape(weight.shape).astype(jnp.bfloat16)]
    all_to_all x0 -> x2, blocking collectives: none -> 24.6 us  [the longest x1 14.6 us: fixed_shards(): lax.all_to_all(enter(tokens, modulation), both, split_axis=0, concat_axis...]
    mul x2 -> x0, other arithmetic: 16 us -> none  [masked(): return weight * expanded.reshape(weight.shape).astype(jnp.bfloat16)]
    ppermute x0 -> x3, waiting for transfers between devices: none -> 12 us  [swap(): return lax.ppermute(values, axis, [(i, i ^ bit) for i in range(count)])]
  transfers between devices with their start and end apart: 7 -> 3, of which waited for: 6 -> 3; matrix products, arithmetic and copies ran while one was open for 16% -> 0% of each run, Pallas kernels for 0% -> 2%
where the time goes in v4:
time: 46.6 us; the launch traced here: 46.3 us
  blocking collectives  24.6 us (53%)
  waiting for transfers between devices  12 us (26%)
  Pallas kernels  7.68 us (16%)
  local copies, waits for them, and re-layouts  1.56 us (3%)
    all_to_all x1, blocking collectives, fixed_shards(): lax.all_to_all(enter(tokens, modulation), both, split_axis=0, concat_axis...  14.6 us
    ppermute x3, waiting for transfers between devices, swap(): return lax.ppermute(values, axis, [(i, i ^ bit) for i in range(count)])  12 us
    all_to_all x1, blocking collectives, fixed_shards(): lax.all_to_all(shares, both, split_axis=0, concat_axis=0, tiled=True)  9.99 us
    pallas_call x1, Pallas kernels, in_products(): pl.pallas_call(in_kernel, in_specs=[pl.BlockSpec(memory_space=pltpu.VMEM)...  4.07 us
    unnamed x26, local copies, waits for them, and re-layouts  1.56 us
    pallas_call x1, Pallas kernels, out_products(): pl.pallas_call(out_kernel, out_shape=jax.ShapeDtypeStruct((2 * half // co...  1.16 us
    pallas_call x1, Pallas kernels, prune(): pl.pallas_call(functools.partial(prune_kernel, 0 if turned else 1), out_s...  1.05 us
  transfers between devices with their start and end apart: 3, of which 3 were waited for; matrix products, arithmetic and copies ran while one was open for 0% of the time, Pallas kernels for 2%

profile of v4, /device:TPU:0, one launch (start us, length us, event | category | flops | bytes accessed | tf_op | source)
XLA Modules:
  0.0 46.3 jit_solution(9766179849582667933)
XLA Ops:
  0.0 0.8 %copy-done.1 = f32[1,3,3072]{2,0,1:T(1,128)S(1)} copy-done((f32[1,3,3072]{2,0,1:T(1,128)S(1)}, f32[1,3,3072]{2,0,1:T(1,128)}, u32[]{:S(2)}) %copy-start.1) | copy-done | bytes 36888
  0.8 0.7 %copy-done.3 = bf16[1,4,3072]{2,1,0:T(4,128)(2,1)S(1)} copy-done((bf16[1,4,3072]{2,1,0:T(4,128)(2,1)S(1)}, bf16[1,4,3072]{2,1,0:T(4,128)(2,1)}, u32[]{:S(2)}) %copy-start.3) | copy-done | bytes 24600
  1.5 0.2 enter.1
  1.7 14.6 %all_to_all.10.got_ref = bf16[16,4,768]{2,1,0:T(4,128)(2,1)S(1)} all-to-all(bf16[16,4,768]{2,1,0:T(4,128)(2,1)S(1)} %enter.1), channel_id=1, replica_groups=mesh['rep'=2,'seq'=4,'wt'=4] {'seq','wt'}, dimensions={0} | all-to-all | bytes 196608 | tf_op jit(solution)/shard_map/all_to_all | solution.py:361
  16.3 0.0 copy-done.8
  16.3 4.1 %in_products.1 = (f32[32,5376]{1,0:T(8,128)S(1)}, bf16[32,5376]{1,0:T(8,128)(2,1)S(1)}) custom-call(bf16[16,4,768]{2,1,0:T(4,128)(2,1)S(1)} %all_to_all.10.got_ref, s32[12,48]{1,0:T(8,128)S(1)} %copy-done.8, bf16[3,768,768]{2,1,0:T(8,128)(2,1)} %bitcast.12, bf16[768,3072]{1,0:T(8,128)(2,1)} %up_hbm.1), custom_call_target="tpu_custom_call" | custom-call | flops 528482304 | bytes 8257536 | tf_op jit(solution)/shard_map/in_products/pallas_call | solution.py:240
  20.4 0.1 collective-permute-start
  20.5 1.6 %collective-permute-done = bf16[32,5376]{1,0:T(8,128)(2,1)S(1)} collective-permute-done((bf16[32,5376]{1,0:T(8,128)(2,1)S(1)}, bf16[32,5376]{1,0:T(8,128)(2,1)S(1)}, u32[]{:S(2)}, u32[]{:S(2)}) %collective-permute-start) | collective-permute-done | bytes 344096 | tf_op jit(solution)/shard_map/ppermute | solution.py:342
  22.1 0.1 fusion
  22.2 0.1 collective-permute-start.1
  22.3 0.0 slice-done
  22.3 0.0 slice-done.1
  22.3 0.0 copy-done.9
  22.3 0.0 copy-start.5
  22.3 0.0 copy-start.6
  22.4 0.0 copy-start.10
  22.4 0.0 copy-start
  22.4 1.1 %prune.1.down_ref = bf16[3072,768]{1,0:T(8,128)(2,1)S(1)} custom-call(s32[12,48]{1,0:T(8,128)S(1)} %bitcast.11, bf16[3072,768]{1,0:T(8,128)(2,1)S(1)} %bitcast.6), custom_call_target="tpu_custom_call" | custom-call | tf_op jit(solution)/shard_map/prune/pallas_call | solution.py:176
  23.4 0.0 copy-start.2
  23.4 0.0 copy-start.4
  23.5 0.0 copy-start.7
  23.5 8.9 %collective-permute-done.1.other_ref = bf16[32,5376]{1,0:T(8,128)(2,1)S(1)} collective-permute-done((bf16[32,5376]{1,0:T(8,128)(2,1)S(1)}, bf16[32,5376]{1,0:T(8,128)(2,1)S(1)}, u32[]{:S(2)}, u32[]{:S(2)}) %collective-permute-start.1) | collective-permute-done | bytes 344096 | tf_op jit(solution)/shard_map/ppermute | solution.py:342
  32.4 0.0 copy-done.5
  32.4 0.0 copy-done.6
  32.4 0.5 %middle.1.mine = bf16[32,3840]{1,0:T(8,128)(2,1)S(1)} custom-call(f32[32,5376]{1,0:T(8,128)S(1)} %get-tuple-element.12.own_ref, bf16[32,5376]{1,0:T(8,128)(2,1)S(1)} %collective-permute-done.1.other_ref, f32[3,768]{1,0:T(4,128)S(1)} %copy-done.5, f32[2,128]{1,0:T(2,128)S(1)} %copy-done.10, f32[1,3072]{1,0:T(1,128)S(1)} %bitcast.9), custom_call_target="tpu_custom_call" | custom-call | tf_op jit(solution)/shard_map/middle/pallas_call | solution.py:304
  32.9 0.1 collective-permute-start.2
  33.0 1.5 %collective-permute-done.2.theirs = bf16[32,3840]{1,0:T(8,128)(2,1)S(1)} collective-permute-done((bf16[32,3840]{1,0:T(8,128)(2,1)S(1)}, bf16[32,3840]{1,0:T(8,128)(2,1)S(1)}, u32[]{:S(2)}, u32[]{:S(2)}) %collective-permute-start.2) | collective-permute-done | bytes 245792 | tf_op jit(solution)/shard_map/ppermute | solution.py:342
  34.5 0.0 copy-done
  34.5 1.2 %out_products.1 = bf16[16,4,768]{2,1,0:T(4,128)(2,1)S(1)} custom-call(bf16[32,3840]{1,0:T(8,128)(2,1)S(1)} %middle.1.mine, bf16[32,3840]{1,0:T(8,128)(2,1)S(1)} %collective-permute-done.2.theirs, bf16[768,768]{1,0:T(8,128)(2,1)S(1)} %copy-done, bf16[3072,768]{1,0:T(8,128)(2,1)S(1)} %prune.1.down_ref), custom_call_target="tpu_custom_call" | custom-call | flops 377487360 | bytes 5898240 | tf_op jit(solution)/shard_map/out_products/pallas_call | solution.py:331
  35.7 10.0 %all_to_all.11.shares_ref = bf16[16,4,768]{2,1,0:T(4,128)(2,1)S(1)} all-to-all(bf16[16,4,768]{2,1,0:T(4,128)(2,1)S(1)} %out_products.1), channel_id=1, replica_groups=mesh['rep'=2,'seq'=4,'wt'=4] {'seq','wt'}, dimensions={0} | all-to-all | bytes 196608 | tf_op jit(solution)/shard_map/all_to_all | solution.py:369
  45.7 0.0 copy-done.7
  45.7 0.6 %leave_kernel.1 = bf16[1,4,3072]{2,1,0:T(4,128)(2,1)} custom-call(bf16[16,4,768]{2,1,0:T(4,128)(2,1)S(1)} %all_to_all.11.shares_ref, bf16[1,4,3072]{2,1,0:T(4,128)(2,1)S(1)} %copy-done.4, f32[3,1,3072]{2,1,0:T(1,128)S(1)} %bitcast.8, f32[1,3072]{1,0:T(1,128)S(1)} %bitcast.10), custom_call_target="tpu_custom_call" | custom-call | tf_op jit(solution)/shard_map/leave_kernel/pallas_call | solution.py:143
  (10 shorter events, 0.0 us)
Async XLA Ops:
  0.0 0.8 %copy-start.1 = (f32[1,3,3072]{2,0,1:T(1,128)S(1)}, f32[1,3,3072]{2,0,1:T(1,128)}, u32[]{:S(2)}) copy-start(f32[1,3,3072]{2,0,1:T(1,128)} %param.13) | copy-start | bytes 110596
  0.8 0.7 %copy-start.3 = (bf16[1,4,3072]{2,1,0:T(4,128)(2,1)S(1)}, bf16[1,4,3072]{2,1,0:T(4,128)(2,1)}, u32[]{:S(2)}) copy-start(bf16[1,4,3072]{2,1,0:T(4,128)(2,1)} %tokens_ref.3) | copy-start | bytes 73732
  1.5 14.8 %copy-start.8 = (s32[12,48]{1,0:T(8,128)S(1)}, s32[12,48]{1,0:T(8,128)}, u32[]{:S(2)}) copy-start(s32[12,48]{1,0:T(8,128)} %mask_hbm.1) | copy-start | bytes 6916
  16.3 6.0 %slice-start = ((s8[4718592]{0:T(1024)(128)(4,1)}), s8[4194304]{0:T(1024)(128)(4,1)S(1)}, s32[]{:S(2)}) async-start(s8[4718592]{0:T(1024)(128)(4,1)} %bitcast.5), calls=%async_computation.2 | async-start | bytes 8388608
  16.3 6.0 %slice-start.1 = ((s8[4718592]{0:T(1024)(128)(4,1)}), s8[524288]{0:T(1024)(128)(4,1)S(1)}, s32[]{:S(2)}) async-start(s8[4718592]{0:T(1024)(128)(4,1)} %bitcast.5), calls=%async_computation.3 | async-start | bytes 1048576
  16.3 6.0 %copy-start.9 = (s32[48,12]{0,1:T(8,128)S(1)}, s32[48,12]{0,1:T(8,128)}, u32[]{:S(2)}) copy-start(s32[48,12]{0,1:T(8,128)} %param.22) | copy-start | bytes 6916
  20.4 1.7 %collective-permute-start = (bf16[32,5376]{1,0:T(8,128)(2,1)S(1)}, bf16[32,5376]{1,0:T(8,128)(2,1)S(1)}, u32[]{:S(2)}, u32[]{:S(2)}) collective-permute-start(bf16[32,5376]{1,0:T(8,128)(2,1)S(1)} %get-tuple-element.11), channel_id=1, source_target_pairs={{0,1},{1,0},{2,3},{3,2},{4,5},{5,4},{6,7},{7,6},{8,9},{9,8},{10,11... | collective-permute-start | bytes 1032200 | tf_op jit(solution)/shard_map/ppermute | solution.py:342
  22.2 10.2 %collective-permute-start.1 = (bf16[32,5376]{1,0:T(8,128)(2,1)S(1)}, bf16[32,5376]{1,0:T(8,128)(2,1)S(1)}, u32[]{:S(2)}, u32[]{:S(2)}) collective-permute-start(bf16[32,5376]{1,0:T(8,128)(2,1)S(1)} %get-tuple-element.15), channel_id=1, source_target_pairs={{0,2},{1,3},{2,0},{3,1},{4,6},{5,7},{6,4},{7,5},{8,10},{9,11},{10,... | collective-permute-start | bytes 1032200 | tf_op jit(solution)/shard_map/ppermute | solution.py:342
  22.3 10.1 %copy-start.5 = (f32[3,768]{1,0:T(4,128)S(1)}, f32[3,768]{1,0:T(4,128)}, u32[]{:S(2)}) copy-start(f32[3,768]{1,0:T(4,128)} %qkv_bias_ref.1) | copy-start | bytes 27652
  22.3 10.0 %copy-start.6 = (f32[3072]{0:T(1024)S(1)}, f32[3072]{0:T(1024)}, u32[]{:S(2)}) copy-start(f32[3072]{0:T(1024)} %param.19) | copy-start | bytes 36868
  22.4 10.0 %copy-start.10 = (f32[2,128]{1,0:T(2,128)S(1)}, f32[2,128]{1,0:T(2,128)}, u32[]{:S(2)}) copy-start(f32[2,128]{1,0:T(2,128)} %gains_ref.1) | copy-start | bytes 3076
  22.4 12.1 %copy-start = (bf16[768,768]{1,0:T(8,128)(2,1)S(1)}, bf16[768,768]{1,0:T(8,128)(2,1)}, u32[]{:S(2)}) copy-start(bf16[768,768]{1,0:T(8,128)(2,1)} %proj_ref.1) | copy-start | bytes 3538948
  23.4 22.2 %copy-start.2 = (f32[1,3,3072]{2,0,1:T(1,128)S(1)}, f32[1,3,3072]{2,0,1:T(1,128)}, u32[]{:S(2)}) copy-start(f32[1,3,3072]{2,0,1:T(1,128)} %param.13) | copy-start | bytes 110596
  23.4 22.2 %copy-start.4 = (bf16[1,4,3072]{2,1,0:T(4,128)(2,1)S(1)}, bf16[1,4,3072]{2,1,0:T(4,128)(2,1)}, u32[]{:S(2)}) copy-start(bf16[1,4,3072]{2,1,0:T(4,128)(2,1)} %tokens_ref.3) | copy-start | bytes 73732
  23.5 22.2 %copy-start.7 = (f32[3072]{0:T(1024)S(1)}, f32[3072]{0:T(1024)}, u32[]{:S(2)}) copy-start(f32[3072]{0:T(1024)} %param.23) | copy-start | bytes 36868
  32.9 1.6 %collective-permute-start.2 = (bf16[32,3840]{1,0:T(8,128)(2,1)S(1)}, bf16[32,3840]{1,0:T(8,128)(2,1)S(1)}, u32[]{:S(2)}, u32[]{:S(2)}) collective-permute-start(bf16[32,3840]{1,0:T(8,128)(2,1)S(1)} %middle.1.mine), channel_id=1, source_target_pairs={{0,1},{1,0},{2,3},{3,2},{4,5},{5,4},{6,7},{7,6},{8,9},{9,8},{10,11... | collective-permute-start | bytes 737288 | tf_op jit(solution)/shard_map/ppermute | solution.py:342

commit v5 on v4

--- a/solution.py
+++ b/solution.py
@@ -12,7 +12,6 @@
 BLOCK = 64
 MIB = 1024 * 1024
 STREAM = 52
-AHEAD = 7
 BESIDE = 16 * MIB
 
 
@@ -183,25 +182,23 @@
     )(mask.T if turned else mask, weight)
 
 
-def in_kernel(got_ref, mask_hbm, qkv_hbm, up_hbm, keep_ref, send_ref, tiles, mask_ref, lanes, sems):
+def in_kernel(pruned, got_ref, *refs):
     share = got_ref.shape[2]
-    count = tiles.shape[0]
-    copies = [
-        pltpu.make_async_copy(
-            qkv_hbm.at[n] if n < 3 else up_hbm.at[:, pl.ds((n - 3) * share, share)], tiles.at[n], sems.at[n]
+    if pruned:
+        mask_ref, weight_ref, keep_ref, send_ref, lanes = refs
+        count = weight_ref.shape[1] // share
+    else:
+        weight_hbm, keep_ref, send_ref, tiles, sems = refs
+        count = tiles.shape[0]
+        copies = [pltpu.make_async_copy(weight_hbm.at[n], tiles.at[n], sems.at[n]) for n in range(count)]
+        for copy in copies:
+            copy.start()
+    if pruned:
+        lanes[...] = jnp.dot(
+            mask_ref[...].astype(jnp.bfloat16),
+            pick_lanes(mask_ref.shape[1], lanes.shape[1]),
+            preferred_element_type=jnp.float32,
         )
-        for n in range(count)
-    ]
-    mask_copy = pltpu.make_async_copy(mask_hbm, mask_ref, sems.at[count])
-    mask_copy.start()
-    for copy in copies[:AHEAD]:
-        copy.start()
-    mask_copy.wait()
-    lanes[...] = jnp.dot(
-        mask_ref[...].astype(jnp.bfloat16),
-        pick_lanes(mask_ref.shape[1], lanes.shape[1]),
-        preferred_element_type=jnp.float32,
-    )
     core = lax.axis_index("wt") % 2
     x = jnp.concatenate(
         [
@@ -212,60 +209,70 @@
         ],
         axis=0,
     ).astype(jnp.bfloat16)
-    for n, copy in enumerate(copies):
-        copy.wait()
-        if n + AHEAD < count:
-            copies[n + AHEAD].start()
-        if n < 3:
+    for n in range(count):
+        cols = slice(n * share, (n + 1) * share)
+        if not pruned:
+            copies[n].wait()
             weight = tiles[n]
         else:
-            cols = slice((n - 3) * share, (n - 2) * share)
+            weight = weight_ref[:, cols]
             weight = jnp.concatenate(
                 [
-                    tiles[n, r * BLOCK : (r + 1) * BLOCK] * lanes[r : r + 1, cols].astype(jnp.bfloat16)
+                    weight[r * BLOCK : (r + 1) * BLOCK] * lanes[r : r + 1, cols].astype(jnp.bfloat16)
                     for r in range(lanes.shape[0])
                 ],
                 axis=0,
             )
         out = jnp.dot(x, weight, preferred_element_type=jnp.float32)
-        cols = slice(n * share, (n + 1) * share)
         keep_ref[:, cols] = jnp.concatenate([out[r : r + 8] for r in range(0, 64, 16)], axis=0)
         send_ref[:, cols] = jnp.concatenate([out[r + 8 : r + 16] for r in range(0, 64, 16)], axis=0).astype(jnp.bfloat16)
 
 
-def in_products(got, qkv_weight, up_weight, up_mask):
+def in_products(got, weight, mask=None):
     places, count, depth = got.shape
-    size = qkv_weight.size + up_weight.size
-    half, width = places * count // 2, size // depth
-    return pl.pallas_call(
-        in_kernel,
-        in_specs=[pl.BlockSpec(memory_space=pltpu.VMEM)] + [pl.BlockSpec(memory_space=pltpu.HBM)] * 3,
+    half, width = places * count // 2, weight.size // depth
+    vmem = pl.BlockSpec(memory_space=pltpu.VMEM)
+    if mask is None:
+        scratch = [
+            pltpu.VMEM((width // depth, depth, depth), jnp.bfloat16),
+            pltpu.SemaphoreType.DMA((width // depth,)),
+        ]
+        given, places = [weight], [vmem, pl.BlockSpec(memory_space=pltpu.HBM)]
+    else:
+        scratch = [pltpu.VMEM((mask.shape[0], weight.shape[1]), jnp.float32)]
+        given, places = [mask, weight], [vmem] * 3
+    return pl.pallas_call(
+        functools.partial(in_kernel, mask is not None),
+        in_specs=places,
         out_shape=[
             jax.ShapeDtypeStruct((half, width), jnp.float32),
             jax.ShapeDtypeStruct((half, width), jnp.bfloat16),
         ],
-        scratch_shapes=[
-            pltpu.VMEM((width // depth, depth, depth), jnp.bfloat16),
-            pltpu.VMEM(up_mask.shape, up_mask.dtype),
-            pltpu.VMEM((up_mask.shape[0], up_weight.shape[1]), jnp.float32),
-            pltpu.SemaphoreType.DMA((width // depth + 1,)),
-        ],
-        compiler_params=pltpu.CompilerParams(vmem_limit_bytes=STREAM * MIB),
-        cost_estimate=pl.CostEstimate(flops=4 * half * size, bytes_accessed=2 * size, transcendentals=0),
+        scratch_shapes=scratch,
+        compiler_params=pltpu.CompilerParams(vmem_limit_bytes=(STREAM if mask is None else 14) * MIB),
+        cost_estimate=pl.CostEstimate(flops=4 * half * weight.size, bytes_accessed=2 * weight.size, transcendentals=0),
         name="in_products",
-    )(got, up_mask, qkv_weight.transpose(1, 0, 2), up_weight)
-
-
-def mid_kernel(images, part, own_ref, other_ref, qkv_bias_ref, gains_ref, up_bias_ref, out_ref):
-    rows = own_ref.shape[0]
-    share = qkv_bias_ref.shape[1]
+    )(got, *given)
+
+
+def share_kernel(kept_ref, got_ref, mine_ref, send_ref):
+    total = kept_ref[...] + got_ref[...].astype(jnp.float32)
+    rows = range(0, total.shape[0], 8)
+    first = jnp.concatenate([total[r : r + 4] for r in rows], axis=0)
+    second = jnp.concatenate([total[r + 4 : r + 8] for r in rows], axis=0)
+    on_first = lax.axis_index("wt") < 2
+    mine_ref[...] = jnp.where(on_first, first, second)
+    send_ref[...] = jnp.where(on_first, second, first).astype(jnp.bfloat16)
+
+
+def attend_kernel(images, part, own_ref, other_ref, bias_ref, gains_ref, out_ref):
+    rows, share = out_ref.shape
     heads = share // HEAD
 
-    def total(start, size):
-        return own_ref[:, start : start + size] + other_ref[:, start : start + size].astype(jnp.float32)
-
     def stacked(which):
-        flat = (total(which * share, share) + qkv_bias_ref[which : which + 1, :]).astype(jnp.bfloat16)
+        lanes = slice(which * share, (which + 1) * share)
+        flat = own_ref[:, lanes] + other_ref[:, lanes].astype(jnp.float32)
+        flat = (flat + bias_ref[which : which + 1, :]).astype(jnp.bfloat16)
         return jnp.concatenate([flat[:, h * HEAD : (h + 1) * HEAD] for h in range(heads)], axis=0)
 
     def normed(which):
@@ -290,30 +297,51 @@
     attended = (summed / denoms).astype(jnp.bfloat16)
     for h in range(heads):
         out_ref[:, h * HEAD : (h + 1) * HEAD] = attended[h * rows : (h + 1) * rows]
-    hidden = out_ref.shape[1] - share
-    for start in range(0, hidden, share):
-        v = total(3 * share + start, share) + up_bias_ref[:, start : start + share]
+
+
+def attention(images, part, own, other, bias, gains):
+    return pl.pallas_call(
+        functools.partial(attend_kernel, images, part),
+        out_shape=jax.ShapeDtypeStruct((own.shape[0], bias.shape[1]), jnp.bfloat16),
+        compiler_params=pltpu.CompilerParams(vmem_limit_bytes=8 * MIB),
+        name="attention",
+    )(own, other, bias, gains)
+
+
+def hidden_kernel(own_ref, other_ref, bias_ref, out_ref):
+    step = 6 * HEAD
+    for start in range(0, out_ref.shape[1], step):
+        lanes = slice(start, start + step)
+        v = own_ref[:, lanes] + other_ref[:, lanes].astype(jnp.float32) + bias_ref[:, lanes]
         cubic = math.sqrt(2.0 / math.pi) * (v + 0.044715 * (v * v * v))
-        out_ref[:, share + start : 2 * share + start] = (0.5 * v * (1.0 + jnp.tanh(cubic))).astype(jnp.bfloat16)
-
-
-def middle(images, part, own, other, qkv_bias, gains, up_bias):
-    rows = own.shape[0]
-    share = qkv_bias.shape[1]
-    width = own.shape[1] - 2 * share
-    return pl.pallas_call(
-        functools.partial(mid_kernel, images, part),
-        out_shape=jax.ShapeDtypeStruct((rows, width), jnp.bfloat16),
+        out_ref[:, lanes] = (0.5 * v * (1.0 + jnp.tanh(cubic))).astype(jnp.bfloat16)
+
+
+def activate(own, other, bias):
+    return pl.pallas_call(
+        hidden_kernel,
+        out_shape=jax.ShapeDtypeStruct(own.shape, jnp.bfloat16),
         compiler_params=pltpu.CompilerParams(vmem_limit_bytes=8 * MIB),
-        name="middle",
-    )(own, other, qkv_bias, gains, up_bias.reshape(1, -1))
-
-
-def out_kernel(mine, theirs, proj_ref, down_ref, out_ref):
-    mixed = jnp.concatenate([mine[...], theirs[...]], axis=0)
-    depth = proj_ref.shape[0]
-    total = jnp.dot(mixed[:, :depth], proj_ref[...], preferred_element_type=jnp.float32)
-    total += jnp.dot(mixed[:, depth:], down_ref[...], preferred_element_type=jnp.float32)
+        name="hidden",
+    )(own, other, bias.reshape(1, -1))
+
+
+def by_chip(mine, theirs):
+    mine, theirs = mine.astype(jnp.float32), theirs.astype(jnp.float32)
+    on_first = lax.axis_index("wt") < 2
+    first, second = jnp.where(on_first, mine, theirs), jnp.where(on_first, theirs, mine)
+    pieces = []
+    for r in range(0, mine.shape[0], 4):
+        pieces += [first[r : r + 4], second[r : r + 4]]
+    return jnp.concatenate(pieces, axis=0).astype(jnp.bfloat16)
+
+
+def out_kernel(a_mine, a_theirs, h_mine, h_theirs, proj_ref, down_ref, out_ref):
+    half = a_mine.shape[0] // 2
+    attended = jnp.concatenate([by_chip(ref[:half], ref[half:]) for ref in (a_mine, a_theirs)], axis=0)
+    hidden = jnp.concatenate([h_mine[...], h_theirs[...]], axis=0)
+    total = jnp.dot(attended, proj_ref[...], preferred_element_type=jnp.float32)
+    total += jnp.dot(hidden, down_ref[...], preferred_element_type=jnp.float32)
     core = lax.axis_index("wt") % 2
     count = out_ref.shape[1]
     row = 0
@@ -325,16 +353,16 @@
                 row += count
 
 
-def out_products(count, mine, theirs, proj, down):
-    half, width = mine.shape[0], proj.shape[1]
+def out_products(count, attended, theirs, hidden, hidden_theirs, proj, down):
+    rows, width = 2 * hidden.shape[0], proj.shape[1]
     size = proj.size + down.size
     return pl.pallas_call(
         out_kernel,
-        out_shape=jax.ShapeDtypeStruct((2 * half // count, count, width), jnp.bfloat16),
+        out_shape=jax.ShapeDtypeStruct((rows // count, count, width), jnp.bfloat16),
         compiler_params=pltpu.CompilerParams(vmem_limit_bytes=12 * MIB),
-        cost_estimate=pl.CostEstimate(flops=4 * half * size, bytes_accessed=2 * size, transcendentals=0),
+        cost_estimate=pl.CostEstimate(flops=2 * rows * size, bytes_accessed=2 * size, transcendentals=0),
         name="out_products",
-    )(mine, theirs, proj, down)
+    )(attended, theirs, hidden, hidden_theirs, proj, down)
 
 
 def swap(values, axis, bit):
@@ -359,13 +387,24 @@
     count = tokens.shape[1]
     both = ("seq", "wt")
     got = lax.all_to_all(enter(tokens, modulation), both, split_axis=0, concat_axis=0, tiled=True)
-    kept, given = in_products(got, qkv_weight, up_weight, up_mask)
-    own = kept + swap(given, "wt", 1).astype(jnp.float32)
+    kept, given = in_products(got, qkv_weight.transpose(1, 0, 2))
+    got, given = lax.optimization_barrier((got, given))
+    half, width = kept.shape[0] // 2, kept.shape[1]
+    halves = [jax.ShapeDtypeStruct((half, width), jnp.float32), jax.ShapeDtypeStruct((half, width), jnp.bfloat16)]
+    own, sent = small(share_kernel, halves, kept, swap(given, "wt", 1))
+    up_kept, up_given = in_products(got, up_weight, up_mask)
+    up_given, sent = lax.optimization_barrier((up_given, sent))
+    attended = attention(1, count, own, swap(sent, "wt", 2), qkv_bias, norm_gains)
+    own = up_kept + swap(up_given, "wt", 1).astype(jnp.float32)
     pair = own, swap(own.astype(jnp.bfloat16), "wt", 2)
     down_pruned = prune(down_weight, down_mask, True, hint=0)
-    pair, down_pruned = lax.optimization_barrier((pair, down_pruned))
-    mixed = middle(2, count, *pair, qkv_bias, norm_gains, up_bias)
-    shares = out_products(count, mixed, swap(mixed, "wt", 1), proj_weight, down_pruned)
+    attended = jnp.concatenate([attended, swap(attended, "wt", 2)], axis=0)
+    attended, down_pruned = lax.optimization_barrier((attended, down_pruned))
+    pair, attended = lax.optimization_barrier((pair, attended))
+    hidden = activate(*pair, up_bias)
+    shares = out_products(
+        count, attended, swap(attended, "wt", 1), hidden, swap(hidden, "wt", 1), proj_weight, down_pruned
+    )
     shares = lax.all_to_all(shares, both, split_axis=0, concat_axis=0, tiled=True)
     out = jax.ShapeDtypeStruct(tokens.shape, tokens.dtype)
     return small(leave_kernel, out, shares, tokens, modulation.transpose(1, 0, 2), out_bias.reshape(1, -1))

time: 46.6 us -> 44.3 us (0.951)
  waiting for transfers between devices: 12 us -> 7.88 us
  starting transfers between devices: 0.21 us -> 1.91 us
  local copies, waits for them, and re-layouts: 1.56 us -> 2.16 us
  Pallas kernels: 7.68 us -> 7.17 us
    ppermute x3 -> x7, waiting for transfers between devices: 12 us -> 7.88 us  [swap(): return lax.ppermute(values, axis, [(i, i ^ bit) for i in range(count)])]
    ppermute x3 -> x7, starting transfers between devices: 0.21 us -> 1.91 us  [swap(): return lax.ppermute(values, axis, [(i, i ^ bit) for i in range(count)])]
    unnamed x26 -> x30, local copies, waits for them, and re-layouts: 1.56 us -> 2.16 us
    pallas_call x3 -> x5, Pallas kernels: 5.74 us -> 5.17 us  [the longest x2 3.47 us: in_products(): pl.pallas_call(functools.partial(in_kernel, mask is not None), in_specs=p...]
  transfers between devices with their start and end apart: 3 -> 7, of which waited for: 3 -> 5; matrix products, arithmetic and copies ran while one was open for 0% -> 0% of each run, Pallas kernels for 2% -> 6%
where the time goes in v5:
time: 44.3 us; the launch traced here: 44.1 us
  blocking collectives  24.7 us (56%)
  waiting for transfers between devices  7.88 us (18%)
  Pallas kernels  7.17 us (16%)
  local copies, waits for them, and re-layouts  2.16 us (5%)
  starting transfers between devices  1.91 us (4%)
    all_to_all x1, blocking collectives, fixed_shards(): lax.all_to_all(enter(tokens, modulation), both, split_axis=0, concat_axis...  14.7 us
    all_to_all x1, blocking collectives, fixed_shards(): lax.all_to_all(shares, both, split_axis=0, concat_axis=0, tiled=True)  9.99 us
    ppermute x7, waiting for transfers between devices, swap(): return lax.ppermute(values, axis, [(i, i ^ bit) for i in range(count)])  7.88 us
    pallas_call x2, Pallas kernels, in_products(): pl.pallas_call(functools.partial(in_kernel, mask is not None), in_specs=p...  3.47 us
    unnamed x30, local copies, waits for them, and re-layouts  2.16 us
    ppermute x7, starting transfers between devices, swap(): return lax.ppermute(values, axis, [(i, i ^ bit) for i in range(count)])  1.91 us
    pallas_call x1, Pallas kernels, out_products(): pl.pallas_call(out_kernel, out_shape=jax.ShapeDtypeStruct((rows // count,...  1.16 us
    pallas_call x1, Pallas kernels, prune(): pl.pallas_call(functools.partial(prune_kernel, 0 if turned else 1), out_s...  1.05 us
  transfers between devices with their start and end apart: 7, of which 5 were waited for; matrix products, arithmetic and copies ran while one was open for 0% of the time, Pallas kernels for 6%

profile of v5, /device:TPU:0, one launch (start us, length us, event | category | flops | bytes accessed | tf_op | source)
XLA Modules:
  0.0 44.1 jit_solution(11312607501915079340)
XLA Ops:
  0.0 0.9 %copy-done.1 = f32[1,3,3072]{2,0,1:T(1,128)S(1)} copy-done((f32[1,3,3072]{2,0,1:T(1,128)S(1)}, f32[1,3,3072]{2,0,1:T(1,128)}, u32[]{:S(2)}) %copy-start.1) | copy-done | bytes 36888
  0.9 1.2 %copy-done.3 = bf16[1,4,3072]{2,1,0:T(4,128)(2,1)S(1)} copy-done((bf16[1,4,3072]{2,1,0:T(4,128)(2,1)S(1)}, bf16[1,4,3072]{2,1,0:T(4,128)(2,1)}, u32[]{:S(2)}) %copy-start.3) | copy-done | bytes 24600
  2.1 0.2 enter.1
  2.4 14.7 %all_to_all.10.got_ref = bf16[16,4,768]{2,1,0:T(4,128)(2,1)S(1)} all-to-all(bf16[16,4,768]{2,1,0:T(4,128)(2,1)S(1)} %enter.1), channel_id=1, replica_groups=mesh['rep'=2,'seq'=4,'wt'=4] {'seq','wt'}, dimensions={0} | all-to-all | bytes 196608 | tf_op jit(solution)/shard_map/all_to_all | solution.py:389
  17.1 2.4 %in_products.2 = (f32[32,2304]{1,0:T(8,128)S(1)}, bf16[32,2304]{1,0:T(8,128)(2,1)S(1)}) custom-call(bf16[16,4,768]{2,1,0:T(4,128)(2,1)S(1)} %all_to_all.10.got_ref, bf16[3,768,768]{2,1,0:T(8,128)(2,1)} %bitcast.14), custom_call_target="tpu_custom_call" | custom-call | flops 226492416 | bytes 3538944 | tf_op jit(solution)/shard_map/in_products/pallas_call | solution.py:244
  19.5 0.1 collective-permute-start
  19.6 1.1 %in_products.3 = (f32[32,3072]{1,0:T(8,128)S(1)}, bf16[32,3072]{1,0:T(8,128)(2,1)S(1)}) custom-call(bf16[16,4,768]{2,1,0:T(4,128)(2,1)S(1)} %all_to_all.10.got_ref, s32[12,48]{1,0:T(8,128)S(1)} %copy-done.8, bf16[768,3072]{1,0:T(8,128)(2,1)S(1)} %bitcast.6), custom_call_target="tpu_custom_call" | custom-call | flops 301989888 | bytes 4718592 | tf_op jit(solution)/shard_map/in_products/pallas_call | solution.py:244
  20.7 0.3 collective-permute-done.got_ref
  20.9 0.1 share_kernel.1
  21.0 0.3 collective-permute-start.1
  21.3 0.0 collective-permute-start.3
  21.3 1.2 %collective-permute-done.1 = bf16[32,3072]{1,0:T(8,128)(2,1)S(1)} collective-permute-done((bf16[32,3072]{1,0:T(8,128)(2,1)S(1)}, bf16[32,3072]{1,0:T(8,128)(2,1)S(1)}, u32[]{:S(2)}, u32[]{:S(2)}) %collective-permute-start.1) | collective-permute-done | bytes 196640 | tf_op jit(solution)/shard_map/ppermute | solution.py:370
  22.5 0.9 %collective-permute-start.2 = (bf16[32,3072]{1,0:T(8,128)(2,1)S(1)}, bf16[32,3072]{1,0:T(8,128)(2,1)S(1)}, u32[]{:S(2)}, u32[]{:S(2)}) collective-permute-start(bf16[32,3072]{1,0:T(8,128)(2,1)S(1)} %get-tuple-element.35), channel_id=1, source_target_pairs={{0,2},{1,3},{2,0},{3,1},{4,6},{5,7},{6,4},{7,5},{8,10},{9,11},{10,... | collective-permute-start | bytes 589832 | tf_op jit(solution)/shard_map/ppermute | solution.py:370
  23.4 2.7 %collective-permute-done.3.other_ref = bf16[16,2304]{1,0:T(8,128)(2,1)S(1)} collective-permute-done((bf16[16,2304]{1,0:T(8,128)(2,1)S(1)}, bf16[16,2304]{1,0:T(8,128)(2,1)S(1)}, u32[]{:S(2)}, u32[]{:S(2)}) %collective-permute-start.3) | collective-permute-done | bytes 73760 | tf_op jit(solution)/shard_map/ppermute | solution.py:370
  26.1 0.4 attention.1
  26.5 0.1 collective-permute-start.4
  26.6 0.0 copy-start.7
  26.6 0.0 copy-start
  26.6 1.1 %prune.1.down_ref = bf16[3072,768]{1,0:T(8,128)(2,1)S(1)} custom-call(s32[12,48]{1,0:T(8,128)S(1)} %bitcast.13, bf16[3072,768]{1,0:T(8,128)(2,1)S(1)} %bitcast.8), custom_call_target="tpu_custom_call" | custom-call | tf_op jit(solution)/shard_map/prune/pallas_call | solution.py:175
  27.7 0.0 copy-start.2
  27.7 0.0 copy-start.4
  27.7 0.0 copy-start.6
  27.7 2.8 %collective-permute-done.4 = bf16[16,768]{1,0:T(8,128)(2,1)S(1)} collective-permute-done((bf16[16,768]{1,0:T(8,128)(2,1)S(1)}, bf16[16,768]{1,0:T(8,128)(2,1)S(1)}, u32[]{:S(2)}, u32[]{:S(2)}) %collective-permute-start.4) | collective-permute-done | bytes 24608 | tf_op jit(solution)/shard_map/ppermute | solution.py:370
  30.5 0.0 collective-permute-done.2.other_ref
  30.5 0.2 hidden.1.h_mine
  30.7 0.1 collective-permute-start.6
  30.7 0.5 %collective-permute-start.5 = (bf16[32,768]{1,0:T(8,128)(2,1)S(1)}, bf16[32,768]{1,0:T(8,128)(2,1)S(1)}, u32[]{:S(2)}, u32[]{:S(2)}) collective-permute-start(bf16[32,768]{1,0:T(8,128)(2,1)S(1)} %pad_maximum_fusion.a_mine), channel_id=1, source_target_pairs={{0,1},{1,0},{2,3},{3,2},{4,5},{5,4},{6,7},{7,6},{8,9},{9,8},{10,11... | collective-permute-start | bytes 147464 | tf_op jit(solution)/shard_map/ppermute | solution.py:370
  31.2 1.0 %collective-permute-done.5.a_theirs = bf16[32,768]{1,0:T(8,128)(2,1)S(1)} collective-permute-done((bf16[32,768]{1,0:T(8,128)(2,1)S(1)}, bf16[32,768]{1,0:T(8,128)(2,1)S(1)}, u32[]{:S(2)}, u32[]{:S(2)}) %collective-permute-start.5) | collective-permute-done | bytes 49184 | tf_op jit(solution)/shard_map/ppermute | solution.py:370
  32.2 0.0 collective-permute-done.6.h_theirs
  32.3 1.2 %out_products.1 = bf16[16,4,768]{2,1,0:T(4,128)(2,1)S(1)} custom-call(bf16[32,768]{1,0:T(8,128)(2,1)S(1)} %pad_maximum_fusion.a_mine, bf16[32,768]{1,0:T(8,128)(2,1)S(1)} %collective-permute-done.5.a_theirs, bf16[32,3072]{1,0:T(8,128)(2,1)S(1)} %hidden.1.h_mine, bf16[32,3072]{1,0:T(8,128)(2,1)S(1)} %collective-permute-done.6.h_theirs, ...), custom_call_target="tpu_custom_call" | custom-call | flops 377487360 | bytes 5898240 | tf_op jit(solution)/shard_map/out_products/pallas_call | solution.py:359
  33.4 10.0 %all_to_all.11.shares_ref = bf16[16,4,768]{2,1,0:T(4,128)(2,1)S(1)} all-to-all(bf16[16,4,768]{2,1,0:T(4,128)(2,1)S(1)} %out_products.1), channel_id=1, replica_groups=mesh['rep'=2,'seq'=4,'wt'=4] {'seq','wt'}, dimensions={0} | all-to-all | bytes 196608 | tf_op jit(solution)/shard_map/all_to_all | solution.py:408
  43.4 0.6 %leave_kernel.1 = bf16[1,4,3072]{2,1,0:T(4,128)(2,1)} custom-call(bf16[16,4,768]{2,1,0:T(4,128)(2,1)S(1)} %all_to_all.11.shares_ref, bf16[1,4,3072]{2,1,0:T(4,128)(2,1)S(1)} %copy-done.4, f32[3,1,3072]{2,1,0:T(1,128)S(1)} %bitcast.10, f32[1,3072]{1,0:T(1,128)S(1)} %bitcast.11), custom_call_target="tpu_custom_call" | custom-call | tf_op jit(solution)/shard_map/leave_kernel/pallas_call | solution.py:142
  (27 shorter events, 0.1 us)
Async XLA Ops:
  0.0 19.6 %slice-start = ((s8[4718592]{0:T(1024)(128)(4,1)}), s8[4194304]{0:T(1024)(128)(4,1)S(1)}, s32[]{:S(2)}) async-start(s8[4718592]{0:T(1024)(128)(4,1)} %bitcast.5), calls=%async_computation.2 | async-start | bytes 8388608
  0.0 26.5 %slice-start.2 = ((s8[4718592]{0:T(1024)(128)(4,1)}), s8[4194304]{0:T(1024)(128)(4,1)S(1)}, s32[]{:S(2)}) async-start(s8[4718592]{0:T(1024)(128)(4,1)} %bitcast.7), calls=%async_computation.4 | async-start | bytes 8388608
  0.0 0.9 %copy-start.1 = (f32[1,3,3072]{2,0,1:T(1,128)S(1)}, f32[1,3,3072]{2,0,1:T(1,128)}, u32[]{:S(2)}) copy-start(f32[1,3,3072]{2,0,1:T(1,128)} %param.13) | copy-start | bytes 110596
  0.9 1.2 %copy-start.3 = (bf16[1,4,3072]{2,1,0:T(4,128)(2,1)S(1)}, bf16[1,4,3072]{2,1,0:T(4,128)(2,1)}, u32[]{:S(2)}) copy-start(bf16[1,4,3072]{2,1,0:T(4,128)(2,1)} %tokens_ref.3) | copy-start | bytes 73732
  2.1 17.5 %slice-start.1 = ((s8[4718592]{0:T(1024)(128)(4,1)}), s8[524288]{0:T(1024)(128)(4,1)S(1)}, s32[]{:S(2)}) async-start(s8[4718592]{0:T(1024)(128)(4,1)} %bitcast.5), calls=%async_computation.3 | async-start | bytes 1048576
  2.1 17.5 %copy-start.8 = (s32[12,48]{1,0:T(8,128)S(1)}, s32[12,48]{1,0:T(8,128)}, u32[]{:S(2)}) copy-start(s32[12,48]{1,0:T(8,128)} %refs_0_.1) | copy-start | bytes 6916
  2.1 24.4 %slice-start.3 = ((s8[4718592]{0:T(1024)(128)(4,1)}), s8[524288]{0:T(1024)(128)(4,1)S(1)}, s32[]{:S(2)}) async-start(s8[4718592]{0:T(1024)(128)(4,1)} %bitcast.7), calls=%async_computation.5 | async-start | bytes 1048576
  17.1 9.0 %copy-start.5 = (f32[3,768]{1,0:T(4,128)S(1)}, f32[3,768]{1,0:T(4,128)}, u32[]{:S(2)}) copy-start(f32[3,768]{1,0:T(4,128)} %bias_ref.1) | copy-start | bytes 27652
  17.1 9.0 %copy-start.10 = (f32[2,128]{1,0:T(2,128)S(1)}, f32[2,128]{1,0:T(2,128)}, u32[]{:S(2)}) copy-start(f32[2,128]{1,0:T(2,128)} %gains_ref.1) | copy-start | bytes 3076
  17.1 9.5 %copy-start.9 = (s32[48,12]{0,1:T(8,128)S(1)}, s32[48,12]{0,1:T(8,128)}, u32[]{:S(2)}) copy-start(s32[48,12]{0,1:T(8,128)} %param.22) | copy-start | bytes 6916
  19.5 1.4 %collective-permute-start = (bf16[32,2304]{1,0:T(8,128)(2,1)S(1)}, bf16[32,2304]{1,0:T(8,128)(2,1)S(1)}, u32[]{:S(2)}, u32[]{:S(2)}) collective-permute-start(bf16[32,2304]{1,0:T(8,128)(2,1)S(1)} %get-tuple-element.25), channel_id=1, source_target_pairs={{0,1},{1,0},{2,3},{3,2},{4,5},{5,4},{6,7},{7,6},{8,9},{9,8},{10,11... | collective-permute-start | bytes 442376 | tf_op jit(solution)/shard_map/ppermute | solution.py:370
  21.0 1.5 %collective-permute-start.1 = (bf16[32,3072]{1,0:T(8,128)(2,1)S(1)}, bf16[32,3072]{1,0:T(8,128)(2,1)S(1)}, u32[]{:S(2)}, u32[]{:S(2)}) collective-permute-start(bf16[32,3072]{1,0:T(8,128)(2,1)S(1)} %get-tuple-element.27), channel_id=1, source_target_pairs={{0,1},{1,0},{2,3},{3,2},{4,5},{5,4},{6,7},{7,6},{8,9},{9,8},{10,11... | collective-permute-start | bytes 589832 | tf_op jit(solution)/shard_map/ppermute | solution.py:370
  21.3 4.8 %collective-permute-start.3 = (bf16[16,2304]{1,0:T(8,128)(2,1)S(1)}, bf16[16,2304]{1,0:T(8,128)(2,1)S(1)}, u32[]{:S(2)}, u32[]{:S(2)}) collective-permute-start(bf16[16,2304]{1,0:T(8,128)(2,1)S(1)} %get-tuple-element.29), channel_id=1, source_target_pairs={{0,2},{1,3},{2,0},{3,1},{4,6},{5,7},{6,4},{7,5},{8,10},{9,11},{10,... | collective-permute-start | bytes 221192 | tf_op jit(solution)/shard_map/ppermute | solution.py:370
  22.5 7.9 %collective-permute-start.2 = (bf16[32,3072]{1,0:T(8,128)(2,1)S(1)}, bf16[32,3072]{1,0:T(8,128)(2,1)S(1)}, u32[]{:S(2)}, u32[]{:S(2)}) collective-permute-start(bf16[32,3072]{1,0:T(8,128)(2,1)S(1)} %get-tuple-element.35), channel_id=1, source_target_pairs={{0,2},{1,3},{2,0},{3,1},{4,6},{5,7},{6,4},{7,5},{8,10},{9,11},{10,... | collective-permute-start | bytes 589832 | tf_op jit(solution)/shard_map/ppermute | solution.py:370
  26.5 4.0 %collective-permute-start.4 = (bf16[16,768]{1,0:T(8,128)(2,1)S(1)}, bf16[16,768]{1,0:T(8,128)(2,1)S(1)}, u32[]{:S(2)}, u32[]{:S(2)}) collective-permute-start(bf16[16,768]{1,0:T(8,128)(2,1)S(1)} %attention.1), channel_id=1, source_target_pairs={{0,2},{1,3},{2,0},{3,1},{4,6},{5,7},{6,4},{7,5},{8,10},{9,11},{10,... | collective-permute-start | bytes 73736 | tf_op jit(solution)/shard_map/ppermute | solution.py:370
  26.6 3.9 %copy-start.7 = (f32[3072]{0:T(1024)S(1)}, f32[3072]{0:T(1024)}, u32[]{:S(2)}) copy-start(f32[3072]{0:T(1024)} %param.19) | copy-start | bytes 36868
  26.6 5.7 %copy-start = (bf16[768,768]{1,0:T(8,128)(2,1)S(1)}, bf16[768,768]{1,0:T(8,128)(2,1)}, u32[]{:S(2)}) copy-start(bf16[768,768]{1,0:T(8,128)(2,1)} %proj_ref.1) | copy-start | bytes 3538948
  27.7 15.7 %copy-start.2 = (f32[1,3,3072]{2,0,1:T(1,128)S(1)}, f32[1,3,3072]{2,0,1:T(1,128)}, u32[]{:S(2)}) copy-start(f32[1,3,3072]{2,0,1:T(1,128)} %param.13) | copy-start | bytes 110596
  27.7 15.7 %copy-start.4 = (bf16[1,4,3072]{2,1,0:T(4,128)(2,1)S(1)}, bf16[1,4,3072]{2,1,0:T(4,128)(2,1)}, u32[]{:S(2)}) copy-start(bf16[1,4,3072]{2,1,0:T(4,128)(2,1)} %tokens_ref.3) | copy-start | bytes 73732
  27.7 15.7 %copy-start.6 = (f32[3072]{0:T(1024)S(1)}, f32[3072]{0:T(1024)}, u32[]{:S(2)}) copy-start(f32[3072]{0:T(1024)} %param.23) | copy-start | bytes 36868
  30.7 1.6 %collective-permute-start.6 = (bf16[32,3072]{1,0:T(8,128)(2,1)S(1)}, bf16[32,3072]{1,0:T(8,128)(2,1)S(1)}, u32[]{:S(2)}, u32[]{:S(2)}) collective-permute-start(bf16[32,3072]{1,0:T(8,128)(2,1)S(1)} %hidden.1.h_mine), channel_id=1, source_target_pairs={{0,1},{1,0},{2,3},{3,2},{4,5},{5,4},{6,7},{7,6},{8,9},{9,8},{10,11... | collective-permute-start | bytes 589832 | tf_op jit(solution)/shard_map/ppermute | solution.py:370
  30.7 1.5 %collective-permute-start.5 = (bf16[32,768]{1,0:T(8,128)(2,1)S(1)}, bf16[32,768]{1,0:T(8,128)(2,1)S(1)}, u32[]{:S(2)}, u32[]{:S(2)}) collective-permute-start(bf16[32,768]{1,0:T(8,128)(2,1)S(1)} %pad_maximum_fusion.a_mine), channel_id=1, source_target_pairs={{0,1},{1,0},{2,3},{3,2},{4,5},{5,4},{6,7},{7,6},{8,9},{9,8},{10,11... | collective-permute-start | bytes 147464 | tf_op jit(solution)/shard_map/ppermute | solution.py:370

commit v6 on v5

--- a/solution.py
+++ b/solution.py
@@ -11,7 +11,6 @@
 HEAD = 128
 BLOCK = 64
 MIB = 1024 * 1024
-STREAM = 52
 BESIDE = 16 * MIB
 
 
@@ -186,19 +185,13 @@
     share = got_ref.shape[2]
     if pruned:
         mask_ref, weight_ref, keep_ref, send_ref, lanes = refs
-        count = weight_ref.shape[1] // share
-    else:
-        weight_hbm, keep_ref, send_ref, tiles, sems = refs
-        count = tiles.shape[0]
-        copies = [pltpu.make_async_copy(weight_hbm.at[n], tiles.at[n], sems.at[n]) for n in range(count)]
-        for copy in copies:
-            copy.start()
-    if pruned:
         lanes[...] = jnp.dot(
             mask_ref[...].astype(jnp.bfloat16),
             pick_lanes(mask_ref.shape[1], lanes.shape[1]),
             preferred_element_type=jnp.float32,
         )
+    else:
+        weight_ref, keep_ref, send_ref = refs
     core = lax.axis_index("wt") % 2
     x = jnp.concatenate(
         [
@@ -209,20 +202,18 @@
         ],
         axis=0,
     ).astype(jnp.bfloat16)
-    for n in range(count):
+    for n in range(keep_ref.shape[1] // share):
         cols = slice(n * share, (n + 1) * share)
-        if not pruned:
-            copies[n].wait()
-            weight = tiles[n]
-        else:
-            weight = weight_ref[:, cols]
+        if pruned:
             weight = jnp.concatenate(
                 [
-                    weight[r * BLOCK : (r + 1) * BLOCK] * lanes[r : r + 1, cols].astype(jnp.bfloat16)
+                    weight_ref[r * BLOCK : (r + 1) * BLOCK, cols] * lanes[r : r + 1, cols].astype(jnp.bfloat16)
                     for r in range(lanes.shape[0])
                 ],
                 axis=0,
             )
+        else:
+            weight = weight_ref[n]
         out = jnp.dot(x, weight, preferred_element_type=jnp.float32)
         keep_ref[:, cols] = jnp.concatenate([out[r : r + 8] for r in range(0, 64, 16)], axis=0)
         send_ref[:, cols] = jnp.concatenate([out[r + 8 : r + 16] for r in range(0, 64, 16)], axis=0).astype(jnp.bfloat16)
@@ -231,28 +222,18 @@
 def in_products(got, weight, mask=None):
     places, count, depth = got.shape
     half, width = places * count // 2, weight.size // depth
-    vmem = pl.BlockSpec(memory_space=pltpu.VMEM)
-    if mask is None:
-        scratch = [
-            pltpu.VMEM((width // depth, depth, depth), jnp.bfloat16),
-            pltpu.SemaphoreType.DMA((width // depth,)),
-        ]
-        given, places = [weight], [vmem, pl.BlockSpec(memory_space=pltpu.HBM)]
-    else:
-        scratch = [pltpu.VMEM((mask.shape[0], weight.shape[1]), jnp.float32)]
-        given, places = [mask, weight], [vmem] * 3
-    return pl.pallas_call(
-        functools.partial(in_kernel, mask is not None),
-        in_specs=places,
+    pruned = mask is not None
+    return pl.pallas_call(
+        functools.partial(in_kernel, pruned),
         out_shape=[
             jax.ShapeDtypeStruct((half, width), jnp.float32),
             jax.ShapeDtypeStruct((half, width), jnp.bfloat16),
         ],
-        scratch_shapes=scratch,
-        compiler_params=pltpu.CompilerParams(vmem_limit_bytes=(STREAM if mask is None else 14) * MIB),
+        scratch_shapes=[pltpu.VMEM((mask.shape[0], weight.shape[1]), jnp.float32)] if pruned else [],
+        compiler_params=pltpu.CompilerParams(vmem_limit_bytes=14 * MIB),
         cost_estimate=pl.CostEstimate(flops=4 * half * weight.size, bytes_accessed=2 * weight.size, transcendentals=0),
         name="in_products",
-    )(got, *given)
+    )(got, *([mask] if pruned else []), weight)
 
 
 def share_kernel(kept_ref, got_ref, mine_ref, send_ref):

time: 44.3 us -> 42.7 us (0.964)
  Pallas kernels: 7.17 us -> 5.52 us
    pallas_call x2, Pallas kernels: 3.47 us -> 1.83 us  [in_products(): pl.pallas_call(functools.partial(in_kernel, pruned), out_shape=[jax.Shape...]
    unnamed x30 -> x32, local copies, waits for them, and re-layouts: 2.16 us -> 2.17 us
where the time goes in v6:
time: 42.7 us; the launch traced here: 42.5 us
  blocking collectives  24.8 us (58%)
  waiting for transfers between devices  7.83 us (18%)
  Pallas kernels  5.52 us (13%)
  local copies, waits for them, and re-layouts  2.17 us (5%)
  starting transfers between devices  1.93 us (5%)
    all_to_all x1, blocking collectives, fixed_shards(): lax.all_to_all(enter(tokens, modulation), both, split_axis=0, concat_axis...  14.8 us
    all_to_all x1, blocking collectives, fixed_shards(): lax.all_to_all(shares, both, split_axis=0, concat_axis=0, tiled=True)  9.99 us
    ppermute x7, waiting for transfers between devices, swap(): return lax.ppermute(values, axis, [(i, i ^ bit) for i in range(count)])  7.83 us
    unnamed x32, local copies, waits for them, and re-layouts  2.17 us
    ppermute x7, starting transfers between devices, swap(): return lax.ppermute(values, axis, [(i, i ^ bit) for i in range(count)])  1.93 us
    pallas_call x2, Pallas kernels, in_products(): pl.pallas_call(functools.partial(in_kernel, pruned), out_shape=[jax.Shape...  1.83 us
    pallas_call x1, Pallas kernels, out_products(): pl.pallas_call(out_kernel, out_shape=jax.ShapeDtypeStruct((rows // count,...  1.16 us
    pallas_call x1, Pallas kernels, prune(): pl.pallas_call(functools.partial(prune_kernel, 0 if turned else 1), out_s...  1.05 us
  transfers between devices with their start and end apart: 7, of which 5 were waited for; matrix products, arithmetic and copies ran while one was open for 0% of the time, Pallas kernels for 6%

profile of v6, /device:TPU:0, one launch (start us, length us, event | category | flops | bytes accessed | tf_op | source)
XLA Modules:
  0.0 42.5 jit_solution(16211067345958300931)
XLA Ops:
  0.0 0.9 %copy-done.2 = f32[1,3,3072]{2,0,1:T(1,128)S(1)} copy-done((f32[1,3,3072]{2,0,1:T(1,128)S(1)}, f32[1,3,3072]{2,0,1:T(1,128)}, u32[]{:S(2)}) %copy-start.2) | copy-done | bytes 36888
  0.9 1.2 %copy-done.4 = bf16[1,4,3072]{2,1,0:T(4,128)(2,1)S(1)} copy-done((bf16[1,4,3072]{2,1,0:T(4,128)(2,1)S(1)}, bf16[1,4,3072]{2,1,0:T(4,128)(2,1)}, u32[]{:S(2)}) %copy-start.4) | copy-done | bytes 24600
  2.1 0.2 enter.1
  2.4 14.8 %all_to_all.10.got_ref = bf16[16,4,768]{2,1,0:T(4,128)(2,1)S(1)} all-to-all(bf16[16,4,768]{2,1,0:T(4,128)(2,1)S(1)} %enter.1), channel_id=1, replica_groups=mesh['rep'=2,'seq'=4,'wt'=4] {'seq','wt'}, dimensions={0} | all-to-all | bytes 196608 | tf_op jit(solution)/shard_map/all_to_all | solution.py:370
  17.2 0.7 %in_products.2 = (f32[32,2304]{1,0:T(8,128)S(1)}, bf16[32,2304]{1,0:T(8,128)(2,1)S(1)}) custom-call(bf16[16,4,768]{2,1,0:T(4,128)(2,1)S(1)} %all_to_all.10.got_ref, bf16[3,768,768]{2,1,0:T(8,128)(2,1)S(1)} %bitcast.9), custom_call_target="tpu_custom_call" | custom-call | flops 226492416 | bytes 3538944 | tf_op jit(solution)/shard_map/in_products/pallas_call | solution.py:226
  17.9 0.1 collective-permute-start
  18.1 1.1 %in_products.3 = (f32[32,3072]{1,0:T(8,128)S(1)}, bf16[32,3072]{1,0:T(8,128)(2,1)S(1)}) custom-call(bf16[16,4,768]{2,1,0:T(4,128)(2,1)S(1)} %all_to_all.10.got_ref, s32[12,48]{1,0:T(8,128)S(1)} %copy-done.9, bf16[768,3072]{1,0:T(8,128)(2,1)S(1)} %bitcast.6), custom_call_target="tpu_custom_call" | custom-call | flops 301989888 | bytes 4718592 | tf_op jit(solution)/shard_map/in_products/pallas_call | solution.py:226
  19.2 0.2 collective-permute-done.got_ref
  19.4 0.1 share_kernel.1
  19.4 0.3 collective-permute-start.1
  19.8 0.0 collective-permute-start.3
  19.8 1.2 %collective-permute-done.1 = bf16[32,3072]{1,0:T(8,128)(2,1)S(1)} collective-permute-done((bf16[32,3072]{1,0:T(8,128)(2,1)S(1)}, bf16[32,3072]{1,0:T(8,128)(2,1)S(1)}, u32[]{:S(2)}, u32[]{:S(2)}) %collective-permute-start.1) | collective-permute-done | bytes 196640 | tf_op jit(solution)/shard_map/ppermute | solution.py:351
  20.9 0.1 fusion
  21.0 0.9 %collective-permute-start.2 = (bf16[32,3072]{1,0:T(8,128)(2,1)S(1)}, bf16[32,3072]{1,0:T(8,128)(2,1)S(1)}, u32[]{:S(2)}, u32[]{:S(2)}) collective-permute-start(bf16[32,3072]{1,0:T(8,128)(2,1)S(1)} %get-tuple-element.35), channel_id=1, source_target_pairs={{0,2},{1,3},{2,0},{3,1},{4,6},{5,7},{6,4},{7,5},{8,10},{9,11},{10,... | collective-permute-start | bytes 589832 | tf_op jit(solution)/shard_map/ppermute | solution.py:351
  21.9 2.6 %collective-permute-done.3.other_ref = bf16[16,2304]{1,0:T(8,128)(2,1)S(1)} collective-permute-done((bf16[16,2304]{1,0:T(8,128)(2,1)S(1)}, bf16[16,2304]{1,0:T(8,128)(2,1)S(1)}, u32[]{:S(2)}, u32[]{:S(2)}) %collective-permute-start.3) | collective-permute-done | bytes 73760 | tf_op jit(solution)/shard_map/ppermute | solution.py:351
  24.5 0.4 attention.1
  24.9 0.1 collective-permute-start.4
  25.0 0.0 copy-start.8
  25.0 0.0 copy-start.1
  25.0 1.1 %prune.1.down_ref = bf16[3072,768]{1,0:T(8,128)(2,1)S(1)} custom-call(s32[12,48]{1,0:T(8,128)S(1)} %bitcast.14, bf16[3072,768]{1,0:T(8,128)(2,1)S(1)} %bitcast.8), custom_call_target="tpu_custom_call" | custom-call | tf_op jit(solution)/shard_map/prune/pallas_call | solution.py:174
  26.1 0.0 copy-start.3
  26.1 0.0 copy-start.5
  26.1 0.0 copy-start.7
  26.1 2.8 %collective-permute-done.4 = bf16[16,768]{1,0:T(8,128)(2,1)S(1)} collective-permute-done((bf16[16,768]{1,0:T(8,128)(2,1)S(1)}, bf16[16,768]{1,0:T(8,128)(2,1)S(1)}, u32[]{:S(2)}, u32[]{:S(2)}) %collective-permute-start.4) | collective-permute-done | bytes 24608 | tf_op jit(solution)/shard_map/ppermute | solution.py:351
  28.9 0.2 hidden.1.h_mine
  29.1 0.1 collective-permute-start.6
  29.2 0.5 %collective-permute-start.5 = (bf16[32,768]{1,0:T(8,128)(2,1)S(1)}, bf16[32,768]{1,0:T(8,128)(2,1)S(1)}, u32[]{:S(2)}, u32[]{:S(2)}) collective-permute-start(bf16[32,768]{1,0:T(8,128)(2,1)S(1)} %pad_maximum_fusion.a_mine), channel_id=1, source_target_pairs={{0,1},{1,0},{2,3},{3,2},{4,5},{5,4},{6,7},{7,6},{8,9},{9,8},{10,11... | collective-permute-start | bytes 147464 | tf_op jit(solution)/shard_map/ppermute | solution.py:351
  29.7 1.0 %collective-permute-done.5.a_theirs = bf16[32,768]{1,0:T(8,128)(2,1)S(1)} collective-permute-done((bf16[32,768]{1,0:T(8,128)(2,1)S(1)}, bf16[32,768]{1,0:T(8,128)(2,1)S(1)}, u32[]{:S(2)}, u32[]{:S(2)}) %collective-permute-start.5) | collective-permute-done | bytes 49184 | tf_op jit(solution)/shard_map/ppermute | solution.py:351
  30.7 0.0 collective-permute-done.6.h_theirs
  30.7 1.2 %out_products.1 = bf16[16,4,768]{2,1,0:T(4,128)(2,1)S(1)} custom-call(bf16[32,768]{1,0:T(8,128)(2,1)S(1)} %pad_maximum_fusion.a_mine, bf16[32,768]{1,0:T(8,128)(2,1)S(1)} %collective-permute-done.5.a_theirs, bf16[32,3072]{1,0:T(8,128)(2,1)S(1)} %hidden.1.h_mine, bf16[32,3072]{1,0:T(8,128)(2,1)S(1)} %collective-permute-done.6.h_theirs, ...), custom_call_target="tpu_custom_call" | custom-call | flops 377487360 | bytes 5898240 | tf_op jit(solution)/shard_map/out_products/pallas_call | solution.py:340
  31.9 10.0 %all_to_all.11.shares_ref = bf16[16,4,768]{2,1,0:T(4,128)(2,1)S(1)} all-to-all(bf16[16,4,768]{2,1,0:T(4,128)(2,1)S(1)} %out_products.1), channel_id=1, replica_groups=mesh['rep'=2,'seq'=4,'wt'=4] {'seq','wt'}, dimensions={0} | all-to-all | bytes 196608 | tf_op jit(solution)/shard_map/all_to_all | solution.py:389
  41.9 0.6 %leave_kernel.1 = bf16[1,4,3072]{2,1,0:T(4,128)(2,1)} custom-call(bf16[16,4,768]{2,1,0:T(4,128)(2,1)S(1)} %all_to_all.11.shares_ref, bf16[1,4,3072]{2,1,0:T(4,128)(2,1)S(1)} %copy-done.5, f32[3,1,3072]{2,1,0:T(1,128)S(1)} %bitcast.11, f32[1,3072]{1,0:T(1,128)S(1)} %bitcast.12), custom_call_target="tpu_custom_call" | custom-call | tf_op jit(solution)/shard_map/leave_kernel/pallas_call | solution.py:141
  (29 shorter events, 0.1 us)
Async XLA Ops:
  0.0 18.0 %slice-start = ((s8[4718592]{0:T(1024)(128)(4,1)}), s8[4194304]{0:T(1024)(128)(4,1)S(1)}, s32[]{:S(2)}) async-start(s8[4718592]{0:T(1024)(128)(4,1)} %bitcast.5), calls=%async_computation.2 | async-start | bytes 8388608
  0.0 25.0 %slice-start.2 = ((s8[4718592]{0:T(1024)(128)(4,1)}), s8[4194304]{0:T(1024)(128)(4,1)S(1)}, s32[]{:S(2)}) async-start(s8[4718592]{0:T(1024)(128)(4,1)} %bitcast.7), calls=%async_computation.4 | async-start | bytes 8388608
  0.0 0.9 %copy-start.2 = (f32[1,3,3072]{2,0,1:T(1,128)S(1)}, f32[1,3,3072]{2,0,1:T(1,128)}, u32[]{:S(2)}) copy-start(f32[1,3,3072]{2,0,1:T(1,128)} %param.13) | copy-start | bytes 110596
  0.9 1.2 %copy-start.4 = (bf16[1,4,3072]{2,1,0:T(4,128)(2,1)S(1)}, bf16[1,4,3072]{2,1,0:T(4,128)(2,1)}, u32[]{:S(2)}) copy-start(bf16[1,4,3072]{2,1,0:T(4,128)(2,1)} %tokens_ref.3) | copy-start | bytes 73732
  2.1 15.1 %copy-start = (bf16[768,3,768]{2,0,1:T(8,128)(2,1)S(1)}, bf16[768,3,768]{2,0,1:T(8,128)(2,1)}, u32[]{:S(2)}) copy-start(bf16[768,3,768]{2,0,1:T(8,128)(2,1)} %param.14) | copy-start | bytes 10616836
  2.1 15.9 %slice-start.1 = ((s8[4718592]{0:T(1024)(128)(4,1)}), s8[524288]{0:T(1024)(128)(4,1)S(1)}, s32[]{:S(2)}) async-start(s8[4718592]{0:T(1024)(128)(4,1)} %bitcast.5), calls=%async_computation.3 | async-start | bytes 1048576
  2.1 15.9 %copy-start.9 = (s32[12,48]{1,0:T(8,128)S(1)}, s32[12,48]{1,0:T(8,128)}, u32[]{:S(2)}) copy-start(s32[12,48]{1,0:T(8,128)} %refs_0_.1) | copy-start | bytes 6916
  2.1 22.9 %slice-start.3 = ((s8[4718592]{0:T(1024)(128)(4,1)}), s8[524288]{0:T(1024)(128)(4,1)S(1)}, s32[]{:S(2)}) async-start(s8[4718592]{0:T(1024)(128)(4,1)} %bitcast.7), calls=%async_computation.5 | async-start | bytes 1048576
  17.2 7.3 %copy-start.6 = (f32[3,768]{1,0:T(4,128)S(1)}, f32[3,768]{1,0:T(4,128)}, u32[]{:S(2)}) copy-start(f32[3,768]{1,0:T(4,128)} %bias_ref.1) | copy-start | bytes 27652
  17.2 7.3 %copy-start.11 = (f32[2,128]{1,0:T(2,128)S(1)}, f32[2,128]{1,0:T(2,128)}, u32[]{:S(2)}) copy-start(f32[2,128]{1,0:T(2,128)} %gains_ref.1) | copy-start | bytes 3076
  17.2 7.8 %copy-start.10 = (s32[48,12]{0,1:T(8,128)S(1)}, s32[48,12]{0,1:T(8,128)}, u32[]{:S(2)}) copy-start(s32[48,12]{0,1:T(8,128)} %param.22) | copy-start | bytes 6916
  17.9 1.4 %collective-permute-start = (bf16[32,2304]{1,0:T(8,128)(2,1)S(1)}, bf16[32,2304]{1,0:T(8,128)(2,1)S(1)}, u32[]{:S(2)}, u32[]{:S(2)}) collective-permute-start(bf16[32,2304]{1,0:T(8,128)(2,1)S(1)} %get-tuple-element.25), channel_id=1, source_target_pairs={{0,1},{1,0},{2,3},{3,2},{4,5},{5,4},{6,7},{7,6},{8,9},{9,8},{10,11... | collective-permute-start | bytes 442376 | tf_op jit(solution)/shard_map/ppermute | solution.py:351
  19.4 1.5 %collective-permute-start.1 = (bf16[32,3072]{1,0:T(8,128)(2,1)S(1)}, bf16[32,3072]{1,0:T(8,128)(2,1)S(1)}, u32[]{:S(2)}, u32[]{:S(2)}) collective-permute-start(bf16[32,3072]{1,0:T(8,128)(2,1)S(1)} %get-tuple-element.27), channel_id=1, source_target_pairs={{0,1},{1,0},{2,3},{3,2},{4,5},{5,4},{6,7},{7,6},{8,9},{9,8},{10,11... | collective-permute-start | bytes 589832 | tf_op jit(solution)/shard_map/ppermute | solution.py:351
  19.8 4.8 %collective-permute-start.3 = (bf16[16,2304]{1,0:T(8,128)(2,1)S(1)}, bf16[16,2304]{1,0:T(8,128)(2,1)S(1)}, u32[]{:S(2)}, u32[]{:S(2)}) collective-permute-start(bf16[16,2304]{1,0:T(8,128)(2,1)S(1)} %get-tuple-element.29), channel_id=1, source_target_pairs={{0,2},{1,3},{2,0},{3,1},{4,6},{5,7},{6,4},{7,5},{8,10},{9,11},{10,... | collective-permute-start | bytes 221192 | tf_op jit(solution)/shard_map/ppermute | solution.py:351
  21.0 7.9 %collective-permute-start.2 = (bf16[32,3072]{1,0:T(8,128)(2,1)S(1)}, bf16[32,3072]{1,0:T(8,128)(2,1)S(1)}, u32[]{:S(2)}, u32[]{:S(2)}) collective-permute-start(bf16[32,3072]{1,0:T(8,128)(2,1)S(1)} %get-tuple-element.35), channel_id=1, source_target_pairs={{0,2},{1,3},{2,0},{3,1},{4,6},{5,7},{6,4},{7,5},{8,10},{9,11},{10,... | collective-permute-start | bytes 589832 | tf_op jit(solution)/shard_map/ppermute | solution.py:351
  24.9 4.0 %collective-permute-start.4 = (bf16[16,768]{1,0:T(8,128)(2,1)S(1)}, bf16[16,768]{1,0:T(8,128)(2,1)S(1)}, u32[]{:S(2)}, u32[]{:S(2)}) collective-permute-start(bf16[16,768]{1,0:T(8,128)(2,1)S(1)} %attention.1), channel_id=1, source_target_pairs={{0,2},{1,3},{2,0},{3,1},{4,6},{5,7},{6,4},{7,5},{8,10},{9,11},{10,... | collective-permute-start | bytes 73736 | tf_op jit(solution)/shard_map/ppermute | solution.py:351
  25.0 3.9 %copy-start.8 = (f32[3072]{0:T(1024)S(1)}, f32[3072]{0:T(1024)}, u32[]{:S(2)}) copy-start(f32[3072]{0:T(1024)} %param.19) | copy-start | bytes 36868
  25.0 5.7 %copy-start.1 = (bf16[768,768]{1,0:T(8,128)(2,1)S(1)}, bf16[768,768]{1,0:T(8,128)(2,1)}, u32[]{:S(2)}) copy-start(bf16[768,768]{1,0:T(8,128)(2,1)} %proj_ref.1) | copy-start | bytes 3538948
  26.1 15.8 %copy-start.3 = (f32[1,3,3072]{2,0,1:T(1,128)S(1)}, f32[1,3,3072]{2,0,1:T(1,128)}, u32[]{:S(2)}) copy-start(f32[1,3,3072]{2,0,1:T(1,128)} %param.13) | copy-start | bytes 110596
  26.1 15.8 %copy-start.5 = (bf16[1,4,3072]{2,1,0:T(4,128)(2,1)S(1)}, bf16[1,4,3072]{2,1,0:T(4,128)(2,1)}, u32[]{:S(2)}) copy-start(bf16[1,4,3072]{2,1,0:T(4,128)(2,1)} %tokens_ref.3) | copy-start | bytes 73732
  26.1 15.7 %copy-start.7 = (f32[3072]{0:T(1024)S(1)}, f32[3072]{0:T(1024)}, u32[]{:S(2)}) copy-start(f32[3072]{0:T(1024)} %param.23) | copy-start | bytes 36868
  29.1 1.6 %collective-permute-start.6 = (bf16[32,3072]{1,0:T(8,128)(2,1)S(1)}, bf16[32,3072]{1,0:T(8,128)(2,1)S(1)}, u32[]{:S(2)}, u32[]{:S(2)}) collective-permute-start(bf16[32,3072]{1,0:T(8,128)(2,1)S(1)} %hidden.1.h_mine), channel_id=1, source_target_pairs={{0,1},{1,0},{2,3},{3,2},{4,5},{5,4},{6,7},{7,6},{8,9},{9,8},{10,11... | collective-permute-start | bytes 589832 | tf_op jit(solution)/shard_map/ppermute | solution.py:351
  29.2 1.5 %collective-permute-start.5 = (bf16[32,768]{1,0:T(8,128)(2,1)S(1)}, bf16[32,768]{1,0:T(8,128)(2,1)S(1)}, u32[]{:S(2)}, u32[]{:S(2)}) collective-permute-start(bf16[32,768]{1,0:T(8,128)(2,1)S(1)} %pad_maximum_fusion.a_mine), channel_id=1, source_target_pairs={{0,1},{1,0},{2,3},{3,2},{4,5},{5,4},{6,7},{7,6},{8,9},{9,8},{10,11... | collective-permute-start | bytes 147464 | tf_op jit(solution)/shard_map/ppermute | solution.py:351

commit v7 on v6

--- a/solution.py
+++ b/solution.py
@@ -110,7 +110,8 @@
     return result.astype(jnp.bfloat16)[None]
 
 
-def enter_kernel(tokens_ref, mod_ref, out_ref):
+def enter_kernel(tokens_ref, mod_ref, mask_ref, pick_ref, out_ref, lanes_ref):
+    lanes_ref[...] = jnp.dot(mask_ref[...].astype(jnp.bfloat16), pick_ref[...], preferred_element_type=jnp.float32)
     shaped = (1.0 + mod_ref[1]) * layer_norm(tokens_ref[0].astype(jnp.float32)) + mod_ref[0]
     shaped = shaped.astype(jnp.bfloat16)
     share = out_ref.shape[2]
@@ -118,15 +119,18 @@
         out_ref[place] = shaped[:, place % 4 * share : (place % 4 + 1) * share]
 
 
-def enter(tokens, modulation):
+def enter(tokens, modulation, mask, pick):
     _, count, features = tokens.shape
     return pl.pallas_call(
         enter_kernel,
-        out_shape=jax.ShapeDtypeStruct((16, count, features // 4), jnp.bfloat16),
+        out_shape=[
+            jax.ShapeDtypeStruct((16, count, features // 4), jnp.bfloat16),
+            jax.ShapeDtypeStruct((mask.shape[0], pick.shape[1]), jnp.float32),
+        ],
         compiler_params=pltpu.CompilerParams(vmem_limit_bytes=4 * MIB),
         cost_estimate=pl.CostEstimate(flops=400 * BESIDE, bytes_accessed=BESIDE, transcendentals=BESIDE // 100),
         name="enter",
-    )(tokens, modulation.transpose(1, 0, 2))
+    )(tokens, modulation.transpose(1, 0, 2), mask, pick)
 
 
 def leave_kernel(shares_ref, tokens_ref, mod_ref, bias_ref, out_ref):
@@ -151,6 +155,20 @@
         lax.broadcasted_iota(jnp.int32, (blocks, lanes), 1) // BLOCK
         == lax.broadcasted_iota(jnp.int32, (blocks, lanes), 0)
     ).astype(jnp.bfloat16)
+
+
+def pick_kernel(out_ref):
+    out_ref[...] = pick_lanes(*out_ref.shape)
+
+
+def picks(blocks, lanes):
+    return pl.pallas_call(
+        pick_kernel,
+        out_shape=jax.ShapeDtypeStruct((blocks, lanes), jnp.bfloat16),
+        compiler_params=pltpu.CompilerParams(vmem_limit_bytes=4 * MIB),
+        cost_estimate=pl.CostEstimate(flops=400 * BESIDE, bytes_accessed=BESIDE, transcendentals=BESIDE // 100),
+        name="picks",
+    )()
 
 
 def prune_kernel(mask_dim, mask_ref, weight_ref, out_ref, lanes):
@@ -184,12 +202,7 @@
 def in_kernel(pruned, got_ref, *refs):
     share = got_ref.shape[2]
     if pruned:
-        mask_ref, weight_ref, keep_ref, send_ref, lanes = refs
-        lanes[...] = jnp.dot(
-            mask_ref[...].astype(jnp.bfloat16),
-            pick_lanes(mask_ref.shape[1], lanes.shape[1]),
-            preferred_element_type=jnp.float32,
-        )
+        lanes, weight_ref, keep_ref, send_ref = refs
     else:
         weight_ref, keep_ref, send_ref = refs
     core = lax.axis_index("wt") % 2
@@ -219,21 +232,20 @@
         send_ref[:, cols] = jnp.concatenate([out[r + 8 : r + 16] for r in range(0, 64, 16)], axis=0).astype(jnp.bfloat16)
 
 
-def in_products(got, weight, mask=None):
+def in_products(got, weight, lanes=None):
     places, count, depth = got.shape
     half, width = places * count // 2, weight.size // depth
-    pruned = mask is not None
+    pruned = lanes is not None
     return pl.pallas_call(
         functools.partial(in_kernel, pruned),
         out_shape=[
             jax.ShapeDtypeStruct((half, width), jnp.float32),
             jax.ShapeDtypeStruct((half, width), jnp.bfloat16),
         ],
-        scratch_shapes=[pltpu.VMEM((mask.shape[0], weight.shape[1]), jnp.float32)] if pruned else [],
         compiler_params=pltpu.CompilerParams(vmem_limit_bytes=14 * MIB),
         cost_estimate=pl.CostEstimate(flops=4 * half * weight.size, bytes_accessed=2 * weight.size, transcendentals=0),
         name="in_products",
-    )(got, *([mask] if pruned else []), weight)
+    )(got, *([lanes] if pruned else []), weight)
 
 
 def share_kernel(kept_ref, got_ref, mine_ref, send_ref):
@@ -367,13 +379,14 @@
 ):
     count = tokens.shape[1]
     both = ("seq", "wt")
-    got = lax.all_to_all(enter(tokens, modulation), both, split_axis=0, concat_axis=0, tiled=True)
+    sent, lanes = enter(tokens, modulation, up_mask, picks(up_mask.shape[1], up_weight.shape[1]))
+    got = lax.all_to_all(sent, both, split_axis=0, concat_axis=0, tiled=True)
     kept, given = in_products(got, qkv_weight.transpose(1, 0, 2))
     got, given = lax.optimization_barrier((got, given))
     half, width = kept.shape[0] // 2, kept.shape[1]
     halves = [jax.ShapeDtypeStruct((half, width), jnp.float32), jax.ShapeDtypeStruct((half, width), jnp.bfloat16)]
     own, sent = small(share_kernel, halves, kept, swap(given, "wt", 1))
-    up_kept, up_given = in_products(got, up_weight, up_mask)
+    up_kept, up_given = in_products(got, up_weight, lanes)
     up_given, sent = lax.optimization_barrier((up_given, sent))
     attended = attention(1, count, own, swap(sent, "wt", 2), qkv_bias, norm_gains)
     own = up_kept + swap(up_given, "wt", 1).astype(jnp.float32)

time: 42.7 us -> 41.4 us (0.970)
  local copies, waits for them, and re-layouts: 2.17 us -> 0.8 us
    unnamed x32 -> x28, local copies, waits for them, and re-layouts: 2.17 us -> 0.8 us
where the time goes in v7:
time: 41.4 us; the launch traced here: 41.2 us
  blocking collectives  24.8 us (60%)
  waiting for transfers between devices  8.19 us (20%)
  Pallas kernels  5.42 us (13%)
  starting transfers between devices  1.74 us (4%)
  local copies, waits for them, and re-layouts  0.8 us (2%)
    all_to_all x1, blocking collectives, fixed_shards(): got = lax.all_to_all(sent, both, split_axis=0, concat_axis=0, tiled=True)  14.8 us
    all_to_all x1, blocking collectives, fixed_shards(): lax.all_to_all(shares, both, split_axis=0, concat_axis=0, tiled=True)  9.99 us
    ppermute x7, waiting for transfers between devices, swap(): return lax.ppermute(values, axis, [(i, i ^ bit) for i in range(count)])  8.19 us
    ppermute x7, starting transfers between devices, swap(): return lax.ppermute(values, axis, [(i, i ^ bit) for i in range(count)])  1.74 us
    pallas_call x2, Pallas kernels, in_products(): pl.pallas_call(functools.partial(in_kernel, pruned), out_shape=[jax.Shape...  1.69 us
    pallas_call x1, Pallas kernels, out_products(): pl.pallas_call(out_kernel, out_shape=jax.ShapeDtypeStruct((rows // count,...  1.16 us
    pallas_call x1, Pallas kernels, prune(): pl.pallas_call(functools.partial(prune_kernel, 0 if turned else 1), out_s...  1.05 us
  transfers between devices with their start and end apart: 7, of which 5 were waited for; matrix products, arithmetic and copies ran while one was open for 0% of the time, Pallas kernels for 6%

profile of v7, /device:TPU:0, one launch (start us, length us, event | category | flops | bytes accessed | tf_op | source)
XLA Modules:
  0.0 41.2 jit_solution(11801240124894203824)
XLA Ops:
  0.0 0.0 slice-start
  0.0 0.0 slice-start.2
  0.1 0.7 %copy-done.3 = bf16[1,4,3072]{2,1,0:T(4,128)(2,1)S(1)} copy-done((bf16[1,4,3072]{2,1,0:T(4,128)(2,1)S(1)}, bf16[1,4,3072]{2,1,0:T(4,128)(2,1)}, u32[]{:S(2)}) %copy-start.3) | copy-done | bytes 24600
  0.7 0.1 copy-done.2
  0.8 0.2 enter.1
  1.1 14.8 %all_to_all.10.got_ref = bf16[16,4,768]{2,1,0:T(4,128)(2,1)S(1)} all-to-all(bf16[16,4,768]{2,1,0:T(4,128)(2,1)S(1)} %get-tuple-element.22), channel_id=1, replica_groups=mesh['rep'=2,'seq'=4,'wt'=4] {'seq','wt'}, dimensions={0} | all-to-all | bytes 196608 | tf_op jit(solution)/shard_map/all_to_all | solution.py:383
  15.9 0.7 %in_products.2 = (f32[32,2304]{1,0:T(8,128)S(1)}, bf16[32,2304]{1,0:T(8,128)(2,1)S(1)}) custom-call(bf16[16,4,768]{2,1,0:T(4,128)(2,1)S(1)} %all_to_all.10.got_ref, bf16[3,768,768]{2,1,0:T(8,128)(2,1)S(1)} %bitcast.9), custom_call_target="tpu_custom_call" | custom-call | flops 226492416 | bytes 3538944 | tf_op jit(solution)/shard_map/in_products/pallas_call | solution.py:239
  16.6 0.1 collective-permute-start
  16.8 1.0 %in_products.3 = (f32[32,3072]{1,0:T(8,128)S(1)}, bf16[32,3072]{1,0:T(8,128)(2,1)S(1)}) custom-call(bf16[16,4,768]{2,1,0:T(4,128)(2,1)S(1)} %all_to_all.10.got_ref, f32[12,3072]{1,0:T(8,128)S(1)} %get-tuple-element.25.refs_0_, bf16[768,3072]{1,0:T(8,128)(2,1)S(1)} %bitcast.6), custom_call_target="tpu_custom_call" | custom-call | flops 301989888 | bytes 4718592 | tf_op jit(solution)/shard_map/in_products/pallas_call | solution.py:239
  17.7 0.4 collective-permute-done.got_ref
  18.1 0.1 share_kernel.1
  18.1 0.2 collective-permute-start.1
  18.4 0.0 collective-permute-start.3
  18.4 1.3 %collective-permute-done.1 = bf16[32,3072]{1,0:T(8,128)(2,1)S(1)} collective-permute-done((bf16[32,3072]{1,0:T(8,128)(2,1)S(1)}, bf16[32,3072]{1,0:T(8,128)(2,1)S(1)}, u32[]{:S(2)}, u32[]{:S(2)}) %collective-permute-start.1) | collective-permute-done | bytes 196640 | tf_op jit(solution)/shard_map/ppermute | solution.py:363
  19.7 0.8 %collective-permute-start.2 = (bf16[32,3072]{1,0:T(8,128)(2,1)S(1)}, bf16[32,3072]{1,0:T(8,128)(2,1)S(1)}, u32[]{:S(2)}, u32[]{:S(2)}) collective-permute-start(bf16[32,3072]{1,0:T(8,128)(2,1)S(1)} %get-tuple-element.39), channel_id=1, source_target_pairs={{0,2},{1,3},{2,0},{3,1},{4,6},{5,7},{6,4},{7,5},{8,10},{9,11},{10,... | collective-permute-start | bytes 589832 | tf_op jit(solution)/shard_map/ppermute | solution.py:363
  20.5 2.8 %collective-permute-done.3.other_ref = bf16[16,2304]{1,0:T(8,128)(2,1)S(1)} collective-permute-done((bf16[16,2304]{1,0:T(8,128)(2,1)S(1)}, bf16[16,2304]{1,0:T(8,128)(2,1)S(1)}, u32[]{:S(2)}, u32[]{:S(2)}) %collective-permute-start.3) | collective-permute-done | bytes 73760 | tf_op jit(solution)/shard_map/ppermute | solution.py:363
  23.3 0.4 attention.1
  23.7 0.1 collective-permute-start.4
  23.8 0.0 copy-start.6
  23.8 0.0 copy-start.1
  23.9 1.1 %prune.1.down_ref = bf16[3072,768]{1,0:T(8,128)(2,1)S(1)} custom-call(s32[12,48]{1,0:T(8,128)S(1)} %bitcast.14, bf16[3072,768]{1,0:T(8,128)(2,1)S(1)} %bitcast.8), custom_call_target="tpu_custom_call" | custom-call | tf_op jit(solution)/shard_map/prune/pallas_call | solution.py:192
  24.9 0.0 copy-start.5
  24.9 2.7 %collective-permute-done.4 = bf16[16,768]{1,0:T(8,128)(2,1)S(1)} collective-permute-done((bf16[16,768]{1,0:T(8,128)(2,1)S(1)}, bf16[16,768]{1,0:T(8,128)(2,1)S(1)}, u32[]{:S(2)}, u32[]{:S(2)}) %collective-permute-start.4) | collective-permute-done | bytes 24608 | tf_op jit(solution)/shard_map/ppermute | solution.py:363
  27.6 0.0 collective-permute-done.2.other_ref
  27.6 0.2 hidden.1.h_mine
  27.8 0.1 collective-permute-start.6
  27.9 0.5 %collective-permute-start.5 = (bf16[32,768]{1,0:T(8,128)(2,1)S(1)}, bf16[32,768]{1,0:T(8,128)(2,1)S(1)}, u32[]{:S(2)}, u32[]{:S(2)}) collective-permute-start(bf16[32,768]{1,0:T(8,128)(2,1)S(1)} %pad_maximum_fusion.a_mine), channel_id=1, source_target_pairs={{0,1},{1,0},{2,3},{3,2},{4,5},{5,4},{6,7},{7,6},{8,9},{9,8},{10,11... | collective-permute-start | bytes 147464 | tf_op jit(solution)/shard_map/ppermute | solution.py:363
  28.4 1.0 %collective-permute-done.5.a_theirs = bf16[32,768]{1,0:T(8,128)(2,1)S(1)} collective-permute-done((bf16[32,768]{1,0:T(8,128)(2,1)S(1)}, bf16[32,768]{1,0:T(8,128)(2,1)S(1)}, u32[]{:S(2)}, u32[]{:S(2)}) %collective-permute-start.5) | collective-permute-done | bytes 49184 | tf_op jit(solution)/shard_map/ppermute | solution.py:363
  29.4 0.0 collective-permute-done.6.h_theirs
  29.4 1.2 %out_products.1 = bf16[16,4,768]{2,1,0:T(4,128)(2,1)S(1)} custom-call(bf16[32,768]{1,0:T(8,128)(2,1)S(1)} %pad_maximum_fusion.a_mine, bf16[32,768]{1,0:T(8,128)(2,1)S(1)} %collective-permute-done.5.a_theirs, bf16[32,3072]{1,0:T(8,128)(2,1)S(1)} %hidden.1.h_mine, bf16[32,3072]{1,0:T(8,128)(2,1)S(1)} %collective-permute-done.6.h_theirs, ...), custom_call_target="tpu_custom_call" | custom-call | flops 377487360 | bytes 5898240 | tf_op jit(solution)/shard_map/out_products/pallas_call | solution.py:352
  30.6 10.0 %all_to_all.11.shares_ref = bf16[16,4,768]{2,1,0:T(4,128)(2,1)S(1)} all-to-all(bf16[16,4,768]{2,1,0:T(4,128)(2,1)S(1)} %out_products.1), channel_id=1, replica_groups=mesh['rep'=2,'seq'=4,'wt'=4] {'seq','wt'}, dimensions={0} | all-to-all | bytes 196608 | tf_op jit(solution)/shard_map/all_to_all | solution.py:402
  40.6 0.6 %leave_kernel.1 = bf16[1,4,3072]{2,1,0:T(4,128)(2,1)} custom-call(bf16[16,4,768]{2,1,0:T(4,128)(2,1)S(1)} %all_to_all.11.shares_ref, bf16[1,4,3072]{2,1,0:T(4,128)(2,1)S(1)} %copy-done.3, f32[3,1,3072]{2,1,0:T(1,128)S(1)} %bitcast.11, f32[1,3072]{1,0:T(1,128)S(1)} %bitcast.12), custom_call_target="tpu_custom_call" | custom-call | tf_op jit(solution)/shard_map/leave_kernel/pallas_call | solution.py:145
  (26 shorter events, 0.1 us)
Async XLA Ops:
  0.0 0.7 %copy-start.3 = (bf16[1,4,3072]{2,1,0:T(4,128)(2,1)S(1)}, bf16[1,4,3072]{2,1,0:T(4,128)(2,1)}, u32[]{:S(2)}) copy-start(bf16[1,4,3072]{2,1,0:T(4,128)(2,1)} %tokens_ref.3) | copy-start | bytes 73732
  0.0 0.7 %copy-start.9 = (s32[12,48]{1,0:T(8,128)S(1)}, s32[12,48]{1,0:T(8,128)}, u32[]{:S(2)}) copy-start(s32[12,48]{1,0:T(8,128)} %mask_ref.1) | copy-start | bytes 6916
  0.0 0.8 %copy-start.2 = (f32[1,3,3072]{2,0,1:T(1,128)S(1)}, f32[1,3,3072]{2,0,1:T(1,128)}, u32[]{:S(2)}) copy-start(f32[1,3,3072]{2,0,1:T(1,128)} %param.13) | copy-start | bytes 110596
  0.0 16.7 %slice-start = ((s8[4718592]{0:T(1024)(128)(4,1)}), s8[4194304]{0:T(1024)(128)(4,1)S(1)}, s32[]{:S(2)}) async-start(s8[4718592]{0:T(1024)(128)(4,1)} %bitcast.5), calls=%async_computation.2 | async-start | bytes 8388608
  0.0 23.8 %slice-start.2 = ((s8[4718592]{0:T(1024)(128)(4,1)}), s8[4194304]{0:T(1024)(128)(4,1)S(1)}, s32[]{:S(2)}) async-start(s8[4718592]{0:T(1024)(128)(4,1)} %bitcast.7), calls=%async_computation.4 | async-start | bytes 8388608
  0.8 15.1 %copy-start = (bf16[768,3,768]{2,0,1:T(8,128)(2,1)S(1)}, bf16[768,3,768]{2,0,1:T(8,128)(2,1)}, u32[]{:S(2)}) copy-start(bf16[768,3,768]{2,0,1:T(8,128)(2,1)} %param.14) | copy-start | bytes 10616836
  0.8 15.9 %slice-start.1 = ((s8[4718592]{0:T(1024)(128)(4,1)}), s8[524288]{0:T(1024)(128)(4,1)S(1)}, s32[]{:S(2)}) async-start(s8[4718592]{0:T(1024)(128)(4,1)} %bitcast.5), calls=%async_computation.3 | async-start | bytes 1048576
  0.8 23.0 %slice-start.3 = ((s8[4718592]{0:T(1024)(128)(4,1)}), s8[524288]{0:T(1024)(128)(4,1)S(1)}, s32[]{:S(2)}) async-start(s8[4718592]{0:T(1024)(128)(4,1)} %bitcast.7), calls=%async_computation.5 | async-start | bytes 1048576
  15.9 7.4 %copy-start.4 = (f32[3,768]{1,0:T(4,128)S(1)}, f32[3,768]{1,0:T(4,128)}, u32[]{:S(2)}) copy-start(f32[3,768]{1,0:T(4,128)} %bias_ref.1) | copy-start | bytes 27652
  15.9 7.4 %copy-start.8 = (f32[2,128]{1,0:T(2,128)S(1)}, f32[2,128]{1,0:T(2,128)}, u32[]{:S(2)}) copy-start(f32[2,128]{1,0:T(2,128)} %gains_ref.1) | copy-start | bytes 3076
  15.9 7.9 %copy-start.7 = (s32[48,12]{0,1:T(8,128)S(1)}, s32[48,12]{0,1:T(8,128)}, u32[]{:S(2)}) copy-start(s32[48,12]{0,1:T(8,128)} %param.22) | copy-start | bytes 6916
  16.6 1.4 %collective-permute-start = (bf16[32,2304]{1,0:T(8,128)(2,1)S(1)}, bf16[32,2304]{1,0:T(8,128)(2,1)S(1)}, u32[]{:S(2)}, u32[]{:S(2)}) collective-permute-start(bf16[32,2304]{1,0:T(8,128)(2,1)S(1)} %get-tuple-element.29), channel_id=1, source_target_pairs={{0,1},{1,0},{2,3},{3,2},{4,5},{5,4},{6,7},{7,6},{8,9},{9,8},{10,11... | collective-permute-start | bytes 442376 | tf_op jit(solution)/shard_map/ppermute | solution.py:363
  18.1 1.5 %collective-permute-start.1 = (bf16[32,3072]{1,0:T(8,128)(2,1)S(1)}, bf16[32,3072]{1,0:T(8,128)(2,1)S(1)}, u32[]{:S(2)}, u32[]{:S(2)}) collective-permute-start(bf16[32,3072]{1,0:T(8,128)(2,1)S(1)} %get-tuple-element.31), channel_id=1, source_target_pairs={{0,1},{1,0},{2,3},{3,2},{4,5},{5,4},{6,7},{7,6},{8,9},{9,8},{10,11... | collective-permute-start | bytes 589832 | tf_op jit(solution)/shard_map/ppermute | solution.py:363
  18.4 5.0 %collective-permute-start.3 = (bf16[16,2304]{1,0:T(8,128)(2,1)S(1)}, bf16[16,2304]{1,0:T(8,128)(2,1)S(1)}, u32[]{:S(2)}, u32[]{:S(2)}) collective-permute-start(bf16[16,2304]{1,0:T(8,128)(2,1)S(1)} %get-tuple-element.33), channel_id=1, source_target_pairs={{0,2},{1,3},{2,0},{3,1},{4,6},{5,7},{6,4},{7,5},{8,10},{9,11},{10,... | collective-permute-start | bytes 221192 | tf_op jit(solution)/shard_map/ppermute | solution.py:363
  19.7 7.9 %collective-permute-start.2 = (bf16[32,3072]{1,0:T(8,128)(2,1)S(1)}, bf16[32,3072]{1,0:T(8,128)(2,1)S(1)}, u32[]{:S(2)}, u32[]{:S(2)}) collective-permute-start(bf16[32,3072]{1,0:T(8,128)(2,1)S(1)} %get-tuple-element.39), channel_id=1, source_target_pairs={{0,2},{1,3},{2,0},{3,1},{4,6},{5,7},{6,4},{7,5},{8,10},{9,11},{10,... | collective-permute-start | bytes 589832 | tf_op jit(solution)/shard_map/ppermute | solution.py:363
  23.7 3.9 %collective-permute-start.4 = (bf16[16,768]{1,0:T(8,128)(2,1)S(1)}, bf16[16,768]{1,0:T(8,128)(2,1)S(1)}, u32[]{:S(2)}, u32[]{:S(2)}) collective-permute-start(bf16[16,768]{1,0:T(8,128)(2,1)S(1)} %attention.1), channel_id=1, source_target_pairs={{0,2},{1,3},{2,0},{3,1},{4,6},{5,7},{6,4},{7,5},{8,10},{9,11},{10,... | collective-permute-start | bytes 73736 | tf_op jit(solution)/shard_map/ppermute | solution.py:363
  23.8 3.8 %copy-start.6 = (f32[3072]{0:T(1024)S(1)}, f32[3072]{0:T(1024)}, u32[]{:S(2)}) copy-start(f32[3072]{0:T(1024)} %param.19) | copy-start | bytes 36868
  23.8 5.6 %copy-start.1 = (bf16[768,768]{1,0:T(8,128)(2,1)S(1)}, bf16[768,768]{1,0:T(8,128)(2,1)}, u32[]{:S(2)}) copy-start(bf16[768,768]{1,0:T(8,128)(2,1)} %proj_ref.1) | copy-start | bytes 3538948
  24.9 15.7 %copy-start.5 = (f32[3072]{0:T(1024)S(1)}, f32[3072]{0:T(1024)}, u32[]{:S(2)}) copy-start(f32[3072]{0:T(1024)} %param.23) | copy-start | bytes 36868
  27.8 1.6 %collective-permute-start.6 = (bf16[32,3072]{1,0:T(8,128)(2,1)S(1)}, bf16[32,3072]{1,0:T(8,128)(2,1)S(1)}, u32[]{:S(2)}, u32[]{:S(2)}) collective-permute-start(bf16[32,3072]{1,0:T(8,128)(2,1)S(1)} %hidden.1.h_mine), channel_id=1, source_target_pairs={{0,1},{1,0},{2,3},{3,2},{4,5},{5,4},{6,7},{7,6},{8,9},{9,8},{10,11... | collective-permute-start | bytes 589832 | tf_op jit(solution)/shard_map/ppermute | solution.py:363
  27.9 1.5 %collective-permute-start.5 = (bf16[32,768]{1,0:T(8,128)(2,1)S(1)}, bf16[32,768]{1,0:T(8,128)(2,1)S(1)}, u32[]{:S(2)}, u32[]{:S(2)}) collective-permute-start(bf16[32,768]{1,0:T(8,128)(2,1)S(1)} %pad_maximum_fusion.a_mine), channel_id=1, source_target_pairs={{0,1},{1,0},{2,3},{3,2},{4,5},{5,4},{6,7},{7,6},{8,9},{9,8},{10,11... | collective-permute-start | bytes 147464 | tf_op jit(solution)/shard_map/ppermute | solution.py:363

commit v8 on v7

--- a/solution.py
+++ b/solution.py
@@ -331,7 +331,7 @@
 
 def out_kernel(a_mine, a_theirs, h_mine, h_theirs, proj_ref, down_ref, out_ref):
     half = a_mine.shape[0] // 2
-    attended = jnp.concatenate([by_chip(ref[:half], ref[half:]) for ref in (a_mine, a_theirs)], axis=0)
+    attended = jnp.concatenate([by_chip(a_mine[:half], a_theirs[half:]), by_chip(a_theirs[:half], a_mine[half:])], axis=0)
     hidden = jnp.concatenate([h_mine[...], h_theirs[...]], axis=0)
     total = jnp.dot(attended, proj_ref[...], preferred_element_type=jnp.float32)
     total += jnp.dot(hidden, down_ref[...], preferred_element_type=jnp.float32)
@@ -392,7 +392,7 @@
     own = up_kept + swap(up_given, "wt", 1).astype(jnp.float32)
     pair = own, swap(own.astype(jnp.bfloat16), "wt", 2)
     down_pruned = prune(down_weight, down_mask, True, hint=0)
-    attended = jnp.concatenate([attended, swap(attended, "wt", 2)], axis=0)
+    attended = jnp.concatenate([attended, swap(attended, "wt", 3)], axis=0)
     attended, down_pruned = lax.optimization_barrier((attended, down_pruned))
     pair, attended = lax.optimization_barrier((pair, attended))
     hidden = activate(*pair, up_bias)

time: 41.4 us -> 41.2 us (level)
  no operation moved by 1% of the time
where the time goes in v8:
time: 41.2 us; the launch traced here: 41 us
  blocking collectives  24.8 us (60%)
  waiting for transfers between devices  7.93 us (19%)
  Pallas kernels  5.42 us (13%)
  starting transfers between devices  1.75 us (4%)
  local copies, waits for them, and re-layouts  0.8 us (2%)
    all_to_all x1, blocking collectives, fixed_shards(): got = lax.all_to_all(sent, both, split_axis=0, concat_axis=0, tiled=True)  14.8 us
    all_to_all x1, blocking collectives, fixed_shards(): lax.all_to_all(shares, both, split_axis=0, concat_axis=0, tiled=True)  9.99 us
    ppermute x7, waiting for transfers between devices, swap(): return lax.ppermute(values, axis, [(i, i ^ bit) for i in range(count)])  7.93 us
    ppermute x7, starting transfers between devices, swap(): return lax.ppermute(values, axis, [(i, i ^ bit) for i in range(count)])  1.75 us
    pallas_call x2, Pallas kernels, in_products(): pl.pallas_call(functools.partial(in_kernel, pruned), out_shape=[jax.Shape...  1.69 us
    pallas_call x1, Pallas kernels, out_products(): pl.pallas_call(out_kernel, out_shape=jax.ShapeDtypeStruct((rows // count,...  1.16 us
    pallas_call x1, Pallas kernels, prune(): pl.pallas_call(functools.partial(prune_kernel, 0 if turned else 1), out_s...  1.05 us
  transfers between devices with their start and end apart: 7, of which 5 were waited for; matrix products, arithmetic and copies ran while one was open for 0% of the time, Pallas kernels for 6%

profile of v8, /device:TPU:0, one launch (start us, length us, event | category | flops | bytes accessed | tf_op | source)
XLA Modules:
  0.0 41.0 jit_solution(2038347384011163662)
XLA Ops:
  0.0 0.0 slice-start
  0.0 0.0 slice-start.2
  0.1 0.7 %copy-done.3 = bf16[1,4,3072]{2,1,0:T(4,128)(2,1)S(1)} copy-done((bf16[1,4,3072]{2,1,0:T(4,128)(2,1)S(1)}, bf16[1,4,3072]{2,1,0:T(4,128)(2,1)}, u32[]{:S(2)}) %copy-start.3) | copy-done | bytes 24600
  0.7 0.1 copy-done.2
  0.8 0.2 enter.1
  1.1 14.8 %all_to_all.10.got_ref = bf16[16,4,768]{2,1,0:T(4,128)(2,1)S(1)} all-to-all(bf16[16,4,768]{2,1,0:T(4,128)(2,1)S(1)} %get-tuple-element.22), channel_id=1, replica_groups=mesh['rep'=2,'seq'=4,'wt'=4] {'seq','wt'}, dimensions={0} | all-to-all | bytes 196608 | tf_op jit(solution)/shard_map/all_to_all | solution.py:383
  15.9 0.7 %in_products.2 = (f32[32,2304]{1,0:T(8,128)S(1)}, bf16[32,2304]{1,0:T(8,128)(2,1)S(1)}) custom-call(bf16[16,4,768]{2,1,0:T(4,128)(2,1)S(1)} %all_to_all.10.got_ref, bf16[3,768,768]{2,1,0:T(8,128)(2,1)S(1)} %bitcast.9), custom_call_target="tpu_custom_call" | custom-call | flops 226492416 | bytes 3538944 | tf_op jit(solution)/shard_map/in_products/pallas_call | solution.py:239
  16.6 0.1 collective-permute-start
  16.8 1.0 %in_products.3 = (f32[32,3072]{1,0:T(8,128)S(1)}, bf16[32,3072]{1,0:T(8,128)(2,1)S(1)}) custom-call(bf16[16,4,768]{2,1,0:T(4,128)(2,1)S(1)} %all_to_all.10.got_ref, f32[12,3072]{1,0:T(8,128)S(1)} %get-tuple-element.25.refs_0_, bf16[768,3072]{1,0:T(8,128)(2,1)S(1)} %bitcast.6), custom_call_target="tpu_custom_call" | custom-call | flops 301989888 | bytes 4718592 | tf_op jit(solution)/shard_map/in_products/pallas_call | solution.py:239
  17.7 0.4 collective-permute-done.got_ref
  18.1 0.1 share_kernel.1
  18.1 0.2 collective-permute-start.1
  18.4 0.0 collective-permute-start.3
  18.4 1.3 %collective-permute-done.1 = bf16[32,3072]{1,0:T(8,128)(2,1)S(1)} collective-permute-done((bf16[32,3072]{1,0:T(8,128)(2,1)S(1)}, bf16[32,3072]{1,0:T(8,128)(2,1)S(1)}, u32[]{:S(2)}, u32[]{:S(2)}) %collective-permute-start.1) | collective-permute-done | bytes 196640 | tf_op jit(solution)/shard_map/ppermute | solution.py:363
  19.7 0.8 %collective-permute-start.2 = (bf16[32,3072]{1,0:T(8,128)(2,1)S(1)}, bf16[32,3072]{1,0:T(8,128)(2,1)S(1)}, u32[]{:S(2)}, u32[]{:S(2)}) collective-permute-start(bf16[32,3072]{1,0:T(8,128)(2,1)S(1)} %get-tuple-element.39), channel_id=1, source_target_pairs={{0,2},{1,3},{2,0},{3,1},{4,6},{5,7},{6,4},{7,5},{8,10},{9,11},{10,... | collective-permute-start | bytes 589832 | tf_op jit(solution)/shard_map/ppermute | solution.py:363
  20.5 2.8 %collective-permute-done.3.other_ref = bf16[16,2304]{1,0:T(8,128)(2,1)S(1)} collective-permute-done((bf16[16,2304]{1,0:T(8,128)(2,1)S(1)}, bf16[16,2304]{1,0:T(8,128)(2,1)S(1)}, u32[]{:S(2)}, u32[]{:S(2)}) %collective-permute-start.3) | collective-permute-done | bytes 73760 | tf_op jit(solution)/shard_map/ppermute | solution.py:363
  23.3 0.4 attention.1
  23.7 0.1 collective-permute-start.4
  23.8 0.0 copy-start.6
  23.8 0.0 copy-start.1
  23.9 1.1 %prune.1.down_ref = bf16[3072,768]{1,0:T(8,128)(2,1)S(1)} custom-call(s32[12,48]{1,0:T(8,128)S(1)} %bitcast.14, bf16[3072,768]{1,0:T(8,128)(2,1)S(1)} %bitcast.8), custom_call_target="tpu_custom_call" | custom-call | tf_op jit(solution)/shard_map/prune/pallas_call | solution.py:192
  24.9 0.0 copy-start.5
  24.9 2.4 %collective-permute-done.4 = bf16[16,768]{1,0:T(8,128)(2,1)S(1)} collective-permute-done((bf16[16,768]{1,0:T(8,128)(2,1)S(1)}, bf16[16,768]{1,0:T(8,128)(2,1)S(1)}, u32[]{:S(2)}, u32[]{:S(2)}) %collective-permute-start.4) | collective-permute-done | bytes 24608 | tf_op jit(solution)/shard_map/ppermute | solution.py:363
  27.4 0.0 collective-permute-done.2.other_ref
  27.4 0.2 hidden.1.h_mine
  27.6 0.2 collective-permute-start.6
  27.7 0.4 collective-permute-start.5
  28.1 1.0 %collective-permute-done.5.a_theirs = bf16[32,768]{1,0:T(8,128)(2,1)S(1)} collective-permute-done((bf16[32,768]{1,0:T(8,128)(2,1)S(1)}, bf16[32,768]{1,0:T(8,128)(2,1)S(1)}, u32[]{:S(2)}, u32[]{:S(2)}) %collective-permute-start.5) | collective-permute-done | bytes 49184 | tf_op jit(solution)/shard_map/ppermute | solution.py:363
  29.1 0.0 collective-permute-done.6.h_theirs
  29.1 1.2 %out_products.1 = bf16[16,4,768]{2,1,0:T(4,128)(2,1)S(1)} custom-call(bf16[32,768]{1,0:T(8,128)(2,1)S(1)} %pad_maximum_fusion.a_mine, bf16[32,768]{1,0:T(8,128)(2,1)S(1)} %collective-permute-done.5.a_theirs, bf16[32,3072]{1,0:T(8,128)(2,1)S(1)} %hidden.1.h_mine, bf16[32,3072]{1,0:T(8,128)(2,1)S(1)} %collective-permute-done.6.h_theirs, ...), custom_call_target="tpu_custom_call" | custom-call | flops 377487360 | bytes 5898240 | tf_op jit(solution)/shard_map/out_products/pallas_call | solution.py:352
  30.3 10.0 %all_to_all.11.shares_ref = bf16[16,4,768]{2,1,0:T(4,128)(2,1)S(1)} all-to-all(bf16[16,4,768]{2,1,0:T(4,128)(2,1)S(1)} %out_products.1), channel_id=1, replica_groups=mesh['rep'=2,'seq'=4,'wt'=4] {'seq','wt'}, dimensions={0} | all-to-all | bytes 196608 | tf_op jit(solution)/shard_map/all_to_all | solution.py:402
  40.3 0.6 %leave_kernel.1 = bf16[1,4,3072]{2,1,0:T(4,128)(2,1)} custom-call(bf16[16,4,768]{2,1,0:T(4,128)(2,1)S(1)} %all_to_all.11.shares_ref, bf16[1,4,3072]{2,1,0:T(4,128)(2,1)S(1)} %copy-done.3, f32[3,1,3072]{2,1,0:T(1,128)S(1)} %bitcast.11, f32[1,3072]{1,0:T(1,128)S(1)} %bitcast.12), custom_call_target="tpu_custom_call" | custom-call | tf_op jit(solution)/shard_map/leave_kernel/pallas_call | solution.py:145
  (26 shorter events, 0.1 us)
Async XLA Ops:
  0.0 0.7 %copy-start.3 = (bf16[1,4,3072]{2,1,0:T(4,128)(2,1)S(1)}, bf16[1,4,3072]{2,1,0:T(4,128)(2,1)}, u32[]{:S(2)}) copy-start(bf16[1,4,3072]{2,1,0:T(4,128)(2,1)} %tokens_ref.3) | copy-start | bytes 73732
  0.0 0.7 %copy-start.9 = (s32[12,48]{1,0:T(8,128)S(1)}, s32[12,48]{1,0:T(8,128)}, u32[]{:S(2)}) copy-start(s32[12,48]{1,0:T(8,128)} %mask_ref.1) | copy-start | bytes 6916
  0.0 0.8 %copy-start.2 = (f32[1,3,3072]{2,0,1:T(1,128)S(1)}, f32[1,3,3072]{2,0,1:T(1,128)}, u32[]{:S(2)}) copy-start(f32[1,3,3072]{2,0,1:T(1,128)} %param.13) | copy-start | bytes 110596
  0.0 16.7 %slice-start = ((s8[4718592]{0:T(1024)(128)(4,1)}), s8[4194304]{0:T(1024)(128)(4,1)S(1)}, s32[]{:S(2)}) async-start(s8[4718592]{0:T(1024)(128)(4,1)} %bitcast.5), calls=%async_computation.2 | async-start | bytes 8388608
  0.0 23.8 %slice-start.2 = ((s8[4718592]{0:T(1024)(128)(4,1)}), s8[4194304]{0:T(1024)(128)(4,1)S(1)}, s32[]{:S(2)}) async-start(s8[4718592]{0:T(1024)(128)(4,1)} %bitcast.7), calls=%async_computation.4 | async-start | bytes 8388608
  0.8 15.1 %copy-start = (bf16[768,3,768]{2,0,1:T(8,128)(2,1)S(1)}, bf16[768,3,768]{2,0,1:T(8,128)(2,1)}, u32[]{:S(2)}) copy-start(bf16[768,3,768]{2,0,1:T(8,128)(2,1)} %param.14) | copy-start | bytes 10616836
  0.8 15.9 %slice-start.1 = ((s8[4718592]{0:T(1024)(128)(4,1)}), s8[524288]{0:T(1024)(128)(4,1)S(1)}, s32[]{:S(2)}) async-start(s8[4718592]{0:T(1024)(128)(4,1)} %bitcast.5), calls=%async_computation.3 | async-start | bytes 1048576
  0.8 23.0 %slice-start.3 = ((s8[4718592]{0:T(1024)(128)(4,1)}), s8[524288]{0:T(1024)(128)(4,1)S(1)}, s32[]{:S(2)}) async-start(s8[4718592]{0:T(1024)(128)(4,1)} %bitcast.7), calls=%async_computation.5 | async-start | bytes 1048576
  15.9 7.4 %copy-start.4 = (f32[3,768]{1,0:T(4,128)S(1)}, f32[3,768]{1,0:T(4,128)}, u32[]{:S(2)}) copy-start(f32[3,768]{1,0:T(4,128)} %bias_ref.1) | copy-start | bytes 27652
  15.9 7.4 %copy-start.8 = (f32[2,128]{1,0:T(2,128)S(1)}, f32[2,128]{1,0:T(2,128)}, u32[]{:S(2)}) copy-start(f32[2,128]{1,0:T(2,128)} %gains_ref.1) | copy-start | bytes 3076
  15.9 7.9 %copy-start.7 = (s32[48,12]{0,1:T(8,128)S(1)}, s32[48,12]{0,1:T(8,128)}, u32[]{:S(2)}) copy-start(s32[48,12]{0,1:T(8,128)} %param.22) | copy-start | bytes 6916
  16.6 1.4 %collective-permute-start = (bf16[32,2304]{1,0:T(8,128)(2,1)S(1)}, bf16[32,2304]{1,0:T(8,128)(2,1)S(1)}, u32[]{:S(2)}, u32[]{:S(2)}) collective-permute-start(bf16[32,2304]{1,0:T(8,128)(2,1)S(1)} %get-tuple-element.29), channel_id=1, source_target_pairs={{0,1},{1,0},{2,3},{3,2},{4,5},{5,4},{6,7},{7,6},{8,9},{9,8},{10,11... | collective-permute-start | bytes 442376 | tf_op jit(solution)/shard_map/ppermute | solution.py:363
  18.1 1.5 %collective-permute-start.1 = (bf16[32,3072]{1,0:T(8,128)(2,1)S(1)}, bf16[32,3072]{1,0:T(8,128)(2,1)S(1)}, u32[]{:S(2)}, u32[]{:S(2)}) collective-permute-start(bf16[32,3072]{1,0:T(8,128)(2,1)S(1)} %get-tuple-element.31), channel_id=1, source_target_pairs={{0,1},{1,0},{2,3},{3,2},{4,5},{5,4},{6,7},{7,6},{8,9},{9,8},{10,11... | collective-permute-start | bytes 589832 | tf_op jit(solution)/shard_map/ppermute | solution.py:363
  18.4 5.0 %collective-permute-start.3 = (bf16[16,2304]{1,0:T(8,128)(2,1)S(1)}, bf16[16,2304]{1,0:T(8,128)(2,1)S(1)}, u32[]{:S(2)}, u32[]{:S(2)}) collective-permute-start(bf16[16,2304]{1,0:T(8,128)(2,1)S(1)} %get-tuple-element.33), channel_id=1, source_target_pairs={{0,2},{1,3},{2,0},{3,1},{4,6},{5,7},{6,4},{7,5},{8,10},{9,11},{10,... | collective-permute-start | bytes 221192 | tf_op jit(solution)/shard_map/ppermute | solution.py:363
  19.7 7.7 %collective-permute-start.2 = (bf16[32,3072]{1,0:T(8,128)(2,1)S(1)}, bf16[32,3072]{1,0:T(8,128)(2,1)S(1)}, u32[]{:S(2)}, u32[]{:S(2)}) collective-permute-start(bf16[32,3072]{1,0:T(8,128)(2,1)S(1)} %get-tuple-element.39), channel_id=1, source_target_pairs={{0,2},{1,3},{2,0},{3,1},{4,6},{5,7},{6,4},{7,5},{8,10},{9,11},{10,... | collective-permute-start | bytes 589832 | tf_op jit(solution)/shard_map/ppermute | solution.py:363
  23.7 3.6 %collective-permute-start.4 = (bf16[16,768]{1,0:T(8,128)(2,1)S(1)}, bf16[16,768]{1,0:T(8,128)(2,1)S(1)}, u32[]{:S(2)}, u32[]{:S(2)}) collective-permute-start(bf16[16,768]{1,0:T(8,128)(2,1)S(1)} %attention.1), channel_id=1, source_target_pairs={{0,3},{1,2},{2,1},{3,0},{4,7},{5,6},{6,5},{7,4},{8,11},{9,10},{10,... | collective-permute-start | bytes 73736 | tf_op jit(solution)/shard_map/ppermute | solution.py:363
  23.8 3.5 %copy-start.6 = (f32[3072]{0:T(1024)S(1)}, f32[3072]{0:T(1024)}, u32[]{:S(2)}) copy-start(f32[3072]{0:T(1024)} %param.19) | copy-start | bytes 36868
  23.8 5.3 %copy-start.1 = (bf16[768,768]{1,0:T(8,128)(2,1)S(1)}, bf16[768,768]{1,0:T(8,128)(2,1)}, u32[]{:S(2)}) copy-start(bf16[768,768]{1,0:T(8,128)(2,1)} %proj_ref.1) | copy-start | bytes 3538948
  24.9 15.4 %copy-start.5 = (f32[3072]{0:T(1024)S(1)}, f32[3072]{0:T(1024)}, u32[]{:S(2)}) copy-start(f32[3072]{0:T(1024)} %param.23) | copy-start | bytes 36868
  27.6 1.6 %collective-permute-start.6 = (bf16[32,3072]{1,0:T(8,128)(2,1)S(1)}, bf16[32,3072]{1,0:T(8,128)(2,1)S(1)}, u32[]{:S(2)}, u32[]{:S(2)}) collective-permute-start(bf16[32,3072]{1,0:T(8,128)(2,1)S(1)} %hidden.1.h_mine), channel_id=1, source_target_pairs={{0,1},{1,0},{2,3},{3,2},{4,5},{5,4},{6,7},{7,6},{8,9},{9,8},{10,11... | collective-permute-start | bytes 589832 | tf_op jit(solution)/shard_map/ppermute | solution.py:363
  27.7 1.4 %collective-permute-start.5 = (bf16[32,768]{1,0:T(8,128)(2,1)S(1)}, bf16[32,768]{1,0:T(8,128)(2,1)S(1)}, u32[]{:S(2)}, u32[]{:S(2)}) collective-permute-start(bf16[32,768]{1,0:T(8,128)(2,1)S(1)} %pad_maximum_fusion.a_mine), channel_id=1, source_target_pairs={{0,1},{1,0},{2,3},{3,2},{4,5},{5,4},{6,7},{7,6},{8,9},{9,8},{10,11... | collective-permute-start | bytes 147464 | tf_op jit(solution)/shard_map/ppermute | solution.py:363
